TPU v7x, 256 devices: a whole 4x4x8 slice. The times are simulated.
256 devices in a mesh: comp: 8 (over x, z_lo), row: 32 (over y, z_hi, core).
Axes of the slice: x: 4, y: 4, z: 8 (z_hi: 4, z_lo: 2; z = z_hi * 2 + z_lo), core: 2. Of those that a mesh axis runs over, the one named last changes fastest.
Arguments:
- baseline_uvw: float32 [3, 65536], P(None, 'row'), may hold values from -8000 to 8000
- sky_positions: float32 [2, 8192], P(None, 'comp'), may hold values from -0.03 to 0.03
- fluxes: float32 [8192], P('comp'), may hold values from 0.5 to 5
- clusters: int32 [8192], P('comp'), may hold values from 0 to 63
- stations: int32 [2, 65536], P(None, 'row'), may hold values from 0 to 511
- station_gains: float32 [512, 512], P('row'), may hold values from -4.2 to 4.2
- gain_step: float32 [512, 512], P('row'), may hold values from -1.8 to 1.8
- observed_vis: float32 [2, 4, 65536], P(None, None, 'row'), may hold values from -3072 to 3072
Outputs:
- new_fluxes: float32 [8192], P('comp')
Inputs may be any that keep to these rules, and one draw needn't show every extreme that they name: stations[0, r] and stations[1, r] name the two stations of row r.
All inputs are finite; a program needn't handle non-finite values.
Results may differ from a plain program's by a relative error of at most 0.011.
Values sent between devices are 32-bit elements; how exact they have to be, the bound alone decides.
No kernel may reach another device: no remote copies, remote signals or barrier semaphores. Data moves between devices by JAX's collectives and lax.ppermute only.
A program may use at most 128 MiB of HBM per device.

v0:
```python
import math

import jax
import jax.numpy as jnp
from jax import lax
from jax.sharding import PartitionSpec as P

C = 64
F = 4


TWO_PI = 2.0 * math.pi


def channel_scale(channel):
    return TWO_PI * (1.0 + 0.125 * channel)


def phase_tables(east_west, north_south, vertical, sky_east, sky_north, depth_term):
    base = (
        east_west[:, None] * sky_east[None, :]
        + north_south[:, None] * sky_north[None, :]
        + vertical[:, None] * depth_term[None, :]
    )
    cosines = []
    sines = []
    for channel in range(F):
        angle = base * channel_scale(channel)
        cosines.append(jnp.cos(angle).astype(jnp.bfloat16))
        sines.append(jnp.sin(angle).astype(jnp.bfloat16))
    return (jnp.concatenate(cosines, axis=0), jnp.concatenate(sines, axis=0))


def station_products(gain_table, first_station, second_station):
    row_count = first_station.shape[0]
    first_gain = jnp.take(gain_table, first_station, axis=0).reshape(row_count, 2, F, C)
    second_gain = jnp.take(gain_table, second_station, axis=0).reshape(row_count, 2, F, C)
    gain_re = first_gain[:, 0] * second_gain[:, 0] + first_gain[:, 1] * second_gain[:, 1]
    gain_im = first_gain[:, 1] * second_gain[:, 0] - first_gain[:, 0] * second_gain[:, 1]
    gain_re = jnp.transpose(gain_re, (1, 0, 2)).reshape(F * row_count, C)
    gain_im = jnp.transpose(gain_im, (1, 0, 2)).reshape(F * row_count, C)
    return (gain_re, gain_im)


def per_device(
    baseline_uvw, sky_positions, fluxes, clusters, stations, station_gains, gain_step, observed_vis
):
    owned = station_gains + gain_step
    gain_table = lax.all_gather(owned, "row", axis=0, tiled=True)
    cluster_ids = jnp.arange(C, dtype=jnp.int32)
    local_hot = clusters[:, None] == cluster_ids[None, :]
    flux_table = jnp.where(local_hot, fluxes[:, None], jnp.float32(0.0)).astype(jnp.bfloat16)
    sky_east = sky_positions[0]
    sky_north = sky_positions[1]
    depth_term = jnp.sqrt(1.0 - sky_east * sky_east - sky_north * sky_north) - 1.0
    row_count = baseline_uvw.shape[1]
    block_rows = min(512, row_count)
    block_count = row_count // block_rows
    dims = (((0,), (0,)), ((), ()))

    def visit(block_index, totals):
        scores, curvature = totals
        first_row = block_index * block_rows
        coords = lax.dynamic_slice_in_dim(baseline_uvw, first_row, block_rows, 1)
        pair = lax.dynamic_slice_in_dim(stations, first_row, block_rows, 1)
        cos_tab, sin_tab = phase_tables(
            coords[0], coords[1], coords[2], sky_east, sky_north, depth_term
        )
        gain_re, gain_im = station_products(gain_table, pair[0], pair[1])
        pred_re = jnp.dot(cos_tab, flux_table, preferred_element_type=jnp.float32)
        pred_im = -jnp.dot(sin_tab, flux_table, preferred_element_type=jnp.float32)
        model_re = jnp.sum(gain_re * pred_re - gain_im * pred_im, axis=1)
        model_im = jnp.sum(gain_re * pred_im + gain_im * pred_re, axis=1)
        model_part = jnp.stack([model_re, model_im])
        model = lax.psum(model_part, "comp")
        observed = lax.dynamic_slice_in_dim(observed_vis, first_row, block_rows, 2).reshape(
            2, F * block_rows
        )
        resid_re = (observed[0] - model[0])[:, None]
        resid_im = (observed[1] - model[1])[:, None]
        weight_re = (resid_re * gain_re + resid_im * gain_im).astype(jnp.bfloat16)
        weight_im = (resid_im * gain_re - resid_re * gain_im).astype(jnp.bfloat16)
        scores = scores + (
            lax.dot_general(cos_tab, weight_re, dims, preferred_element_type=jnp.float32)
            - lax.dot_general(sin_tab, weight_im, dims, preferred_element_type=jnp.float32)
        )
        curvature = curvature + jnp.sum(gain_re * gain_re + gain_im * gain_im, axis=0)
        return (scores, curvature)

    start_totals = (jnp.zeros((flux_table.shape[0], C), jnp.float32), jnp.zeros((C,), jnp.float32))
    scores, curvature = lax.fori_loop(0, block_count, visit, start_totals)
    numerator = jnp.sum(jnp.where(local_hot, scores, jnp.float32(0.0)), axis=1)
    numerator, curvature = lax.psum((numerator, curvature), "row")
    curvature_k = jnp.sum(jnp.where(local_hot, curvature[None, :], jnp.float32(0.0)), axis=1)
    return fluxes + numerator / curvature_k


def solution(mesh):
    return jax.shard_map(
        per_device,
        mesh=mesh,
        in_specs=(
            P(None, "row"),
            P(None, "comp"),
            P("comp"),
            P("comp"),
            P(None, "row"),
            P("row", None),
            P("row", None),
            P(None, None, "row"),
        ),
        out_specs=P("comp"),
        check_vma=False,
    )
```

profile of v0, /device:TPU:1, one launch (start us, length us, event | category | flops | bytes accessed | tf_op | source)
XLA Modules:
  0.0 548.9 jit_solution(8675093605659137495)
XLA Ops:
  9.5 56.8 %all-gather.2.cloned.1.call-done = f32[512,512]{1,0:T(8,128)} async-done(((f32[16,512]{1,0:T(8,128)}), f32[512,512]{1,0:T(8,128)}) %all-gather.2.cloned.1.call-update) | async-done | bytes 1048592 | tf_op jit(solution)/shard_map/all_gather | solution.py:49
  66.3 307.2 %while.16 = (s32[]{:T(128)}, f32[1024,64]{0,1:T(8,128)S(1)}, f32[64]{0:T(128)S(1)}, f32[3,2048]{1,0:T(4,128)}, f32[1,1024]{1,0:T(1,128)S(1)}, /*index=5*/f32[1,1...) while((s32[]{:T(128)}, f32[1024,64]{0,1:T(8,128)S(1)}, ...), condition=%wide.region_5.7_spmd.clone, body=%wide.region_0.6_spmd.clone.sunk | while | flops 1154305152 | bytes 86345320 | solution.py:91
  68.8 3.2 gather_fusion.1
  73.4 1.6 gather_fusion
  76.2 1.6 copy.27
  78.2 32.1 %sine_convert_fusion.5 = (bf16[512,1024]{1,0:T(8,128)(2,1)S(1)}, bf16[512,1024]{1,0:T(8,128)(2,1)S(1)}, bf16[512,1024]{1,0:T(8,128)(2,1)S(1)}, bf16[512,1024]{1,...) fusion(f32[1024]{0:T(1024)S(1)} %get-tuple-element.446, ...), kind=kLoop, calls=%fused_computation.9.clone.1 | loop fusion | flops 8912896 | bytes 8407040 | tf_op jit(solution)/shard_map/while/body/eval_jaxpr/convert_element_type | solution.py:30
  113.0 1.6 subtract_reduce_fusion.2
  114.6 26.0 %psum.29 = f32[2,2048]{1,0:T(2,128)S(1)} all-reduce(f32[2,2048]{1,0:T(2,128)S(1)} %pad_maximum_fusion.14), channel_id=1, replica_groups=mesh['comp'=8,'row'=32] {'comp'}, use_global_device_ids=true, to_apply=%region_3.4 | all-reduce | flops 4096 | bytes 32768 | tf_op jit(solution)/shard_map/while/body/eval_jaxpr/psum | solution.py:75
  140.6 3.1 fusion.38
  147.2 3.2 gather_fusion.1
  151.9 1.6 gather_fusion
  154.6 1.6 copy.27
  156.7 32.1 %sine_convert_fusion.5 = (bf16[512,1024]{1,0:T(8,128)(2,1)S(1)}, bf16[512,1024]{1,0:T(8,128)(2,1)S(1)}, bf16[512,1024]{1,0:T(8,128)(2,1)S(1)}, bf16[512,1024]{1,...) fusion(f32[1024]{0:T(1024)S(1)} %get-tuple-element.446, ...), kind=kLoop, calls=%fused_computation.9.clone.1 | loop fusion | flops 8912896 | bytes 8407040 | tf_op jit(solution)/shard_map/while/body/eval_jaxpr/convert_element_type | solution.py:30
  191.4 1.6 subtract_reduce_fusion.2
  193.0 23.8 %psum.29 = f32[2,2048]{1,0:T(2,128)S(1)} all-reduce(f32[2,2048]{1,0:T(2,128)S(1)} %pad_maximum_fusion.14), channel_id=1, replica_groups=mesh['comp'=8,'row'=32] {'comp'}, use_global_device_ids=true, to_apply=%region_3.4 | all-reduce | flops 4096 | bytes 32768 | tf_op jit(solution)/shard_map/while/body/eval_jaxpr/psum | solution.py:75
  216.9 3.1 fusion.38
  223.5 3.2 gather_fusion.1
  228.1 1.6 gather_fusion
  230.9 1.6 copy.27
  233.0 32.1 %sine_convert_fusion.5 = (bf16[512,1024]{1,0:T(8,128)(2,1)S(1)}, bf16[512,1024]{1,0:T(8,128)(2,1)S(1)}, bf16[512,1024]{1,0:T(8,128)(2,1)S(1)}, bf16[512,1024]{1,...) fusion(f32[1024]{0:T(1024)S(1)} %get-tuple-element.446, ...), kind=kLoop, calls=%fused_computation.9.clone.1 | loop fusion | flops 8912896 | bytes 8407040 | tf_op jit(solution)/shard_map/while/body/eval_jaxpr/convert_element_type | solution.py:30
  267.7 1.6 subtract_reduce_fusion.2
  269.3 23.8 %psum.29 = f32[2,2048]{1,0:T(2,128)S(1)} all-reduce(f32[2,2048]{1,0:T(2,128)S(1)} %pad_maximum_fusion.14), channel_id=1, replica_groups=mesh['comp'=8,'row'=32] {'comp'}, use_global_device_ids=true, to_apply=%region_3.4 | all-reduce | flops 4096 | bytes 32768 | tf_op jit(solution)/shard_map/while/body/eval_jaxpr/psum | solution.py:75
  293.2 3.1 fusion.38
  299.8 3.2 gather_fusion.1
  304.4 1.6 gather_fusion
  307.2 1.6 copy.27
  309.2 32.1 %sine_convert_fusion.5 = (bf16[512,1024]{1,0:T(8,128)(2,1)S(1)}, bf16[512,1024]{1,0:T(8,128)(2,1)S(1)}, bf16[512,1024]{1,0:T(8,128)(2,1)S(1)}, bf16[512,1024]{1,...) fusion(f32[1024]{0:T(1024)S(1)} %get-tuple-element.446, ...), kind=kLoop, calls=%fused_computation.9.clone.1 | loop fusion | flops 8912896 | bytes 8407040 | tf_op jit(solution)/shard_map/while/body/eval_jaxpr/convert_element_type | solution.py:30
  343.9 1.6 subtract_reduce_fusion.2
  345.5 23.8 %psum.29 = f32[2,2048]{1,0:T(2,128)S(1)} all-reduce(f32[2,2048]{1,0:T(2,128)S(1)} %pad_maximum_fusion.14), channel_id=1, replica_groups=mesh['comp'=8,'row'=32] {'comp'}, use_global_device_ids=true, to_apply=%region_3.4 | all-reduce | flops 4096 | bytes 32768 | tf_op jit(solution)/shard_map/while/body/eval_jaxpr/psum | solution.py:75
  369.4 3.1 fusion.38
  373.5 97.3 %psum.26 = f32[64]{0:T(128)S(1)} all-reduce(f32[64]{0:T(128)S(1)} %get-tuple-element.192), channel_id=1, replica_groups=mesh['comp'=8,'row'=32] {'row'}, use_global_device_ids=true, to_apply=%region_8.10 | all-reduce | flops 64 | bytes 512 | tf_op jit(solution)/shard_map/psum | solution.py:93
  471.6 69.9 %psum.25 = f32[1024]{0:T(1024)S(1)} all-reduce(f32[1024]{0:T(1024)S(1)} %get-tuple-element.239), channel_id=1, replica_groups=mesh['comp'=8,'row'=32] {'row'}, use_global_device_ids=true, to_apply=%region_7.9 | all-reduce | flops 1024 | bytes 8192 | tf_op jit(solution)/shard_map/psum | solution.py:93
  (203 shorter events, 39.7 us)
Async XLA Ops:
  6.5 59.7 %all-gather.2.cloned.1.call-start = ((), (), s32[]{:S(2)}) async-start(), calls=%async_computation | async-start | bytes 1081344 | tf_op jit(solution)/shard_map/all_gather | solution.py:49
  66.3 475.2 %copy-start.11 = (f32[1024]{0:T(1024)S(1)}, f32[1024]{0:T(1024)}, u32[]{:S(2)}) copy-start(f32[1024]{0:T(1024)} %param.14) | copy-start | bytes 12292
  78.1 34.7 %copy-start.7 = (f32[4,8,8,512]{3,2,0,1:T(8,128)}, f32[4,8,8,512]{3,2,0,1:T(8,128)S(1)}, u32[]{:S(2)}) copy-start(f32[4,8,8,512]{3,2,0,1:T(8,128)S(1)} %copy.29) | copy-start | bytes 1572868 | tf_op jit(solution)/shard_map/while
  78.2 34.7 %copy-start.9 = (f32[4,8,8,512]{3,2,0,1:T(8,128)}, f32[4,8,8,512]{3,2,0,1:T(8,128)S(1)}, u32[]{:S(2)}) copy-start(f32[4,8,8,512]{3,2,0,1:T(8,128)S(1)} %copy.30) | copy-start | bytes 1572868 | tf_op jit(solution)/shard_map/while
  78.2 33.2 %copy-start.12 = (s32[1024]{0:T(1024)S(1)}, s32[1024]{0:T(1024)}, u32[]{:S(2)}) copy-start(s32[1024]{0:T(1024)} %get-tuple-element.450) | copy-start | bytes 12292 | tf_op jit(solution)/shard_map/while
  110.4 2.5 copy-start.1
  110.4 2.5 copy-start.4
  110.4 2.5 copy-start.5
  110.4 2.5 copy-start.6
  140.6 3.1 copy-start.2
  140.6 3.1 copy-start.8
  140.6 3.1 copy-start.10
  156.6 34.7 %copy-start.7 = (f32[4,8,8,512]{3,2,0,1:T(8,128)}, f32[4,8,8,512]{3,2,0,1:T(8,128)S(1)}, u32[]{:S(2)}) copy-start(f32[4,8,8,512]{3,2,0,1:T(8,128)S(1)} %copy.29) | copy-start | bytes 1572868 | tf_op jit(solution)/shard_map/while
  156.6 34.7 %copy-start.9 = (f32[4,8,8,512]{3,2,0,1:T(8,128)}, f32[4,8,8,512]{3,2,0,1:T(8,128)S(1)}, u32[]{:S(2)}) copy-start(f32[4,8,8,512]{3,2,0,1:T(8,128)S(1)} %copy.30) | copy-start | bytes 1572868 | tf_op jit(solution)/shard_map/while
  156.7 33.2 %copy-start.12 = (s32[1024]{0:T(1024)S(1)}, s32[1024]{0:T(1024)}, u32[]{:S(2)}) copy-start(s32[1024]{0:T(1024)} %get-tuple-element.450) | copy-start | bytes 12292 | tf_op jit(solution)/shard_map/while
  188.8 2.5 copy-start.1
  188.9 2.5 copy-start.4
  216.9 3.1 copy-start.2
  216.9 3.1 copy-start.8
  216.9 3.1 copy-start.10
  232.9 34.7 %copy-start.7 = (f32[4,8,8,512]{3,2,0,1:T(8,128)}, f32[4,8,8,512]{3,2,0,1:T(8,128)S(1)}, u32[]{:S(2)}) copy-start(f32[4,8,8,512]{3,2,0,1:T(8,128)S(1)} %copy.29) | copy-start | bytes 1572868 | tf_op jit(solution)/shard_map/while
  232.9 34.7 %copy-start.9 = (f32[4,8,8,512]{3,2,0,1:T(8,128)}, f32[4,8,8,512]{3,2,0,1:T(8,128)S(1)}, u32[]{:S(2)}) copy-start(f32[4,8,8,512]{3,2,0,1:T(8,128)S(1)} %copy.30) | copy-start | bytes 1572868 | tf_op jit(solution)/shard_map/while
  232.9 33.2 %copy-start.12 = (s32[1024]{0:T(1024)S(1)}, s32[1024]{0:T(1024)}, u32[]{:S(2)}) copy-start(s32[1024]{0:T(1024)} %get-tuple-element.450) | copy-start | bytes 12292 | tf_op jit(solution)/shard_map/while
  293.2 3.1 copy-start.2
  293.2 3.1 copy-start.8
  293.2 3.1 copy-start.10
  309.1 34.7 %copy-start.7 = (f32[4,8,8,512]{3,2,0,1:T(8,128)}, f32[4,8,8,512]{3,2,0,1:T(8,128)S(1)}, u32[]{:S(2)}) copy-start(f32[4,8,8,512]{3,2,0,1:T(8,128)S(1)} %copy.29) | copy-start | bytes 1572868 | tf_op jit(solution)/shard_map/while
  309.2 34.7 %copy-start.9 = (f32[4,8,8,512]{3,2,0,1:T(8,128)}, f32[4,8,8,512]{3,2,0,1:T(8,128)S(1)}, u32[]{:S(2)}) copy-start(f32[4,8,8,512]{3,2,0,1:T(8,128)S(1)} %copy.30) | copy-start | bytes 1572868 | tf_op jit(solution)/shard_map/while
  309.2 33.2 %copy-start.12 = (s32[1024]{0:T(1024)S(1)}, s32[1024]{0:T(1024)}, u32[]{:S(2)}) copy-start(s32[1024]{0:T(1024)} %get-tuple-element.450) | copy-start | bytes 12292 | tf_op jit(solution)/shard_map/while
  369.4 3.1 copy-start.2
  369.4 3.1 copy-start.8
  369.4 3.1 copy-start.10
  (18 other events, 34.0 us)
Sparse Core Ops, SparseCore 0:
  9.9 56.2 all-gather.1
where the time goes:
time: 550 us; the launch traced here: 549 us
  blocking collectives  265 us (48%)
  other arithmetic  140 us (25%)
  waiting for transfers between devices  56.8 us (10%)
  local copies, waits for them, and re-layouts  44.7 us (8%)
  matrix products  28.2 us (5%)
  between operations  13.4 us (2%)
    psum x2, blocking collectives, per_device(): numerator, curvature = lax.psum((numerator, curvature), 'row')  167 us
    convert_element_type x4, other arithmetic, phase_tables(): sines.append(jnp.sin(angle).astype(jnp.bfloat16))  129 us
    psum x4, blocking collectives, visit(): model = lax.psum(model_part, 'comp')  97.5 us
    all_gather x1, waiting for transfers between devices, per_device(): gain_table = lax.all_gather(owned, 'row', axis=0, tiled=True)  56.8 us
    gather x4, local copies, waits for them, and re-layouts, station_products(): jnp.take(gain_table, first_station, axis=0).reshape(row_count, 2, F, C)  13 us
    dot_general x4, matrix products, visit(): lax.dot_general(cos_tab, weight_re, dims, preferred_element_type=jnp.floa...  12.4 us
  transfers between devices with their start and end apart: 1, of which 1 were waited for; matrix products, arithmetic and copies ran while one was open for 0% of the time, Pallas kernels for 0%

commit v1 on v0

v1 whole, which is shorter than its diff:
```python
import functools
import math

import jax
import jax.numpy as jnp
import numpy as np
from jax import lax
from jax.experimental import pallas as pl
from jax.experimental.pallas import tpu as pltpu
from jax.sharding import PartitionSpec as P

C = 64
F = 4
BLOCK = 256
WIDE = 2 * F * BLOCK
CHUNK = 256
TILE = 16
GROUPS = (3, 5)
MIB = 1 << 20
F32 = jnp.float32
BF16 = jnp.bfloat16


def unit_circle_fit():
    y = 0.5 * np.cos(np.pi * (np.arange(400) + 0.5) / 400)
    even = np.polynomial.polynomial.polyfit(y * y, np.cos(0.5 * np.pi * y), 3)
    odd = np.polynomial.polynomial.polyfit(y * y, np.sin(0.5 * np.pi * y) / y, 3)
    return [float(np.float32(v)) for v in even], [float(np.float32(v)) for v in odd]


EVEN, ODD = unit_circle_fit()
ROUND = 12582912.0


def split3(x):
    high = x.astype(BF16).astype(F32)
    rest = x - high
    mid = rest.astype(BF16).astype(F32)
    return high, mid, rest - mid


def left_terms(x):
    h, m, l = split3(x)
    return [h, h, m, h, l, m, m, l]


def right_terms(x):
    h, m, l = split3(x)
    return [h, m, h, l, h, m, l, m]


def stack_terms(terms):
    pad = jnp.zeros((8, terms[0].shape[1]), F32)
    return jnp.concatenate(terms + [pad], axis=0)


def phases(eighth):
    y = eighth - ((eighth + ROUND) - ROUND)
    y2 = y * y
    c = EVEN[0] + y2 * (EVEN[1] + y2 * (EVEN[2] + y2 * EVEN[3]))
    s = y * (ODD[0] + y2 * (ODD[1] + y2 * (ODD[2] + y2 * ODD[3])))

    def double(c, s):
        c2 = c + c
        return c2 * c - 1.0, c2 * s

    c, s = double(c, s)
    c1, s1 = double(c, s)
    c, s = double(c1, s1)
    c, s = double(c, s)
    c8, s8 = double(c, s)
    c9, s9 = c8 * c1 - s8 * s1, s8 * c1 + c8 * s1
    t = c1 + c1
    c10, s10 = t * c9 - c8, t * s9 - s8
    c11, s11 = t * c10 - c9, t * s10 - s9
    return (c8, c9, c10, c11, s8, s9, s10, s11)


def table_kernel(sky_ref, flux_ref, clus_ref, uvw_ref, *rest):
    table_ref, pred_ref, left, hot = rest[-4:]
    comps = sky_ref.shape[1]

    @pl.when(pl.program_id(0) == 0)
    def _():
        east, north = sky_ref[0:1, :], sky_ref[1:2, :]
        depth = jnp.sqrt(1.0 - east * east - north * north) - 1.0
        place = jnp.concatenate([east, north, depth], axis=0)
        left[...] = jnp.transpose(stack_terms(left_terms(place))).astype(BF16)
        ids = lax.broadcasted_iota(jnp.int32, (C, comps), 0)
        hot[...] = jnp.where(ids == clus_ref[...], flux_ref[...], 0.0).astype(BF16)

    right = stack_terms(right_terms(uvw_ref[...] * 0.125)).astype(BF16)

    def matmul(chunk):
        at = pl.ds(chunk * CHUNK, CHUNK)
        part = jnp.dot(hot[:, at], table_ref[at, :], preferred_element_type=F32)
        if chunk == 0:
            pred_ref[...] = part
        else:
            pred_ref[...] += part

    for chunk in range(comps // CHUNK):
        base = jnp.dot(
            left[pl.ds(chunk * CHUNK, CHUNK), :], right, preferred_element_type=F32
        )
        for tile in range(CHUNK // TILE):
            values = phases(base[tile * TILE : (tile + 1) * TILE, :])
            for j, value in enumerate(values):
                table_ref[
                    pl.ds(chunk * CHUNK + tile * TILE, TILE), pl.ds(j * BLOCK, BLOCK)
                ] = value.astype(BF16)
        if chunk:
            matmul(chunk - 1)
    matmul(comps // CHUNK - 1)


def make_tables(first, count, sky, fluxes, clusters, uvw, after):
    comps = sky.shape[1]
    whole = lambda i: (0, 0)
    return pl.pallas_call(
        table_kernel,
        grid=(count,),
        in_specs=[
            pl.BlockSpec((2, comps), whole),
            pl.BlockSpec((1, comps), whole),
            pl.BlockSpec((1, comps), whole),
            pl.BlockSpec((3, BLOCK), lambda i: (0, i + first)),
        ]
        + [pl.BlockSpec(memory_space=pl.ANY)] * len(after),
        out_specs=[
            pl.BlockSpec((comps, WIDE), lambda i: (0, i)),
            pl.BlockSpec((C, WIDE), lambda i: (0, i)),
        ],
        out_shape=[
            jax.ShapeDtypeStruct((comps, count * WIDE), BF16),
            jax.ShapeDtypeStruct((C, count * WIDE), F32),
        ],
        scratch_shapes=[pltpu.VMEM((comps, 32), BF16), pltpu.VMEM((C, comps), BF16)],
        compiler_params=pltpu.CompilerParams(vmem_limit_bytes=20 * MIB),
        name="tables",
    )(sky, fluxes, clusters, uvw, *after)


def model_kernel(me_ref, *rest):
    pieces, (pair_ref, pred_ref, gain_ref, model_ref, curv_ref, table) = rest[:4], rest[4:]
    owned = pieces[0].shape[0] // 8

    @pl.when(pl.program_id(0) == 0)
    def _():
        for n, piece in enumerate(pieces):
            flat = jnp.transpose(piece[...])
            high = flat.astype(BF16)
            at = pl.ds(n * flat.shape[1], flat.shape[1])
            table[pl.ds(0, flat.shape[0]), at] = high
            table[pl.ds(flat.shape[0], flat.shape[0]), at] = (
                flat - high.astype(F32)
            ).astype(BF16)
        curv_ref[...] = jnp.zeros_like(curv_ref)

    me = me_ref[0]
    my_y, my_z, my_core = me >> 3, (me >> 1) & 3, me & 1
    stations = table.shape[1]
    columns = table.shape[0] // 2
    ids = lax.broadcasted_iota(jnp.int32, (stations, BLOCK), 0)

    def gather(station):
        owner, own = station // owned, station % owned
        y, z, core = owner >> 3, (owner >> 1) & 3, owner & 1
        slot = ((((my_z - z) & 3) * 4 + ((my_y - y) & 3)) * 2 + (core ^ my_core)) * owned + own
        hot = jnp.where(ids == slot, 1.0, 0.0).astype(BF16)
        both = jnp.dot(table[...], hot, preferred_element_type=F32)
        return both[:columns] + both[columns:]

    first = gather(pair_ref[0:1, :])
    second = gather(pair_ref[1:2, :])
    rows = []
    curv = jnp.zeros((C, BLOCK), F32)
    for f in range(F):
        re, im = pl.ds(f * BLOCK, BLOCK), pl.ds((F + f) * BLOCK, BLOCK)
        p_re, p_im = first[f * C : (f + 1) * C], first[(F + f) * C : (F + f + 1) * C]
        q_re, q_im = second[f * C : (f + 1) * C], second[(F + f) * C : (F + f + 1) * C]
        g_re = p_re * q_re + p_im * q_im
        g_im = p_im * q_re - p_re * q_im
        gain_ref[:, re] = g_re
        gain_ref[:, im] = g_im
        cos_sum, sin_sum = pred_ref[:, re], pred_ref[:, im]
        rows.append(
            (
                jnp.sum(g_re * cos_sum + g_im * sin_sum, axis=0, keepdims=True),
                jnp.sum(g_im * cos_sum - g_re * sin_sum, axis=0, keepdims=True),
            )
        )
        curv = curv + (g_re * g_re + g_im * g_im)
    model = jnp.concatenate([r[0] for r in rows] + [r[1] for r in rows], axis=0)
    for n in range(model_ref.shape[0]):
        model_ref[n] = model
    curv_ref[...] += curv[:, :128] + curv[:, 128:]


def make_model(first, count, me, pieces, stations, pred, peers):
    whole = lambda i: (0, 0)
    rows, columns = pieces[0].shape
    return pl.pallas_call(
        model_kernel,
        grid=(count,),
        in_specs=[pl.BlockSpec(memory_space=pltpu.SMEM)]
        + [pl.BlockSpec((rows, columns), whole)] * 4
        + [
            pl.BlockSpec((2, BLOCK), lambda i: (0, i + first)),
            pl.BlockSpec((C, WIDE), lambda i: (0, i)),
        ],
        out_specs=[
            pl.BlockSpec((C, WIDE), lambda i: (0, i)),
            pl.BlockSpec((peers, 2 * F, BLOCK), lambda i: (0, 0, i)),
            pl.BlockSpec((C, 128), whole),
        ],
        out_shape=[
            jax.ShapeDtypeStruct((C, count * WIDE), F32),
            jax.ShapeDtypeStruct((peers, 2 * F, count * BLOCK), F32),
            jax.ShapeDtypeStruct((C, 128), F32),
        ],
        scratch_shapes=[pltpu.VMEM((2 * columns, 4 * rows), BF16)],
        compiler_params=pltpu.CompilerParams(vmem_limit_bytes=20 * MIB),
        name="model",
    )(me, *pieces, stations, pred)


def score_kernel(parts_ref, obs_ref, gain_ref, table_ref, clus_ref, *rest):
    *before, out_ref, total, weight = rest
    step = pl.program_id(0)
    curvs, earlier = before[: len(GROUPS)], before[len(GROUPS) :]

    @pl.when(step == 0)
    def _():
        total[...] = earlier[0][...] if earlier else jnp.zeros_like(total)

    model = jnp.sum(parts_ref[...], axis=0)
    for f in range(F):
        re, im = pl.ds(f * BLOCK, BLOCK), pl.ds((F + f) * BLOCK, BLOCK)
        r_re = obs_ref[0, f : f + 1, :] - model[f : f + 1, :]
        r_im = obs_ref[1, f : f + 1, :] - model[F + f : F + f + 1, :]
        g_re, g_im = gain_ref[:, re], gain_ref[:, im]
        weight[:, re] = (r_re * g_re + r_im * g_im).astype(BF16)
        weight[:, im] = (r_re * g_im - r_im * g_re).astype(BF16)
    total[...] += lax.dot_general(
        table_ref[...], weight[...], (((1,), (1,)), ((), ())), preferred_element_type=F32
    )

    @pl.when(step == pl.num_programs(0) - 1)
    def _():
        if not curvs:
            out_ref[...] = total[...]
            return
        scores = jnp.transpose(total[...])
        hot = lax.broadcasted_iota(jnp.int32, scores.shape, 0) == clus_ref[...]
        curv = jnp.sum(sum(c[...] for c in curvs), axis=1, keepdims=True)
        out_ref[0:1, :] = jnp.sum(jnp.where(hot, scores, 0.0), axis=0, keepdims=True)
        out_ref[1:2, :] = jnp.sum(jnp.where(hot, curv, 0.0), axis=0, keepdims=True)


def make_scores(first, count, parts, observed, gain, table, clusters, curvs, earlier):
    whole = lambda i: (0, 0)
    comps = table.shape[0]
    peers = parts.shape[0]
    shape = (2, comps) if curvs else (comps, C)
    return pl.pallas_call(
        score_kernel,
        grid=(count,),
        in_specs=[
            pl.BlockSpec((peers, 2 * F, BLOCK), lambda i: (0, 0, i)),
            pl.BlockSpec((2, F, BLOCK), lambda i: (0, 0, i + first)),
            pl.BlockSpec((C, WIDE), lambda i: (0, i)),
            pl.BlockSpec((comps, WIDE), lambda i: (0, i)),
            pl.BlockSpec((1, comps), whole),
        ]
        + [pl.BlockSpec((C, 128), whole)] * len(curvs)
        + [pl.BlockSpec((comps, C), whole)] * len(earlier),
        out_specs=pl.BlockSpec(shape, whole),
        out_shape=jax.ShapeDtypeStruct(shape, F32),
        scratch_shapes=[pltpu.VMEM((comps, C), F32), pltpu.VMEM((C, WIDE), BF16)],
        compiler_params=pltpu.CompilerParams(vmem_limit_bytes=20 * MIB),
        name="scores",
    )(parts, observed, gain, table, clusters, *curvs, *earlier)


def other_core():
    return [(i, i ^ 1) for i in range(32)]


def turn_y(k):
    return [(i, (i + 8 * k) % 32) for i in range(32)]


def turn_z(k):
    return [(i, i // 8 * 8 + ((i // 2 % 4 + k) % 4) * 2 + i % 2) for i in range(32)]


def plane_groups():
    return [[2 * i + core for i in range(16)] for core in range(2)]


def permute(x, pairs):
    return lax.ppermute(x, "row", pairs)


def per_device(
    baseline_uvw, sky_positions, fluxes, clusters, stations, station_gains, gain_step, observed_vis
):
    flux_row, cluster_row = fluxes[None, :], clusters[None, :]
    peers = lax.axis_size("comp")
    me = lax.axis_index("row").astype(jnp.int32)[None]
    firsts = [sum(GROUPS[:n]) for n in range(len(GROUPS))]

    owned = station_gains + gain_step
    chip = jnp.concatenate([owned, permute(owned, other_core())], axis=0)
    line = jnp.concatenate([chip] + [permute(chip, turn_y(k)) for k in (1, 2, 3)], axis=0)
    pieces = [line] + [permute(line, turn_z(k)) for k in (1, 2, 3)]

    after = ([chip], [line])
    tables, preds = zip(
        *(
            make_tables(
                firsts[n], GROUPS[n], sky_positions, flux_row, cluster_row, baseline_uvw, after[n]
            )
            for n in range(len(GROUPS))
        )
    )
    gains, models, curvs = zip(
        *(
            make_model(firsts[n], GROUPS[n], me, pieces, stations, preds[n], peers)
            for n in range(len(GROUPS))
        )
    )
    sent = [lax.all_to_all(m, "comp", 0, 0, tiled=True) for m in models]
    scores = ()
    for n in range(len(GROUPS)):
        last = n == len(GROUPS) - 1
        scores = (
            make_scores(
                firsts[n],
                GROUPS[n],
                sent[n],
                observed_vis,
                gains[n],
                tables[n],
                cluster_row,
                curvs if last else (),
                scores,
            ),
        )
    sums = scores[0]
    sums = sums + permute(sums, other_core())
    sums = lax.all_to_all(
        jnp.broadcast_to(sums[None], (16,) + sums.shape),
        "row",
        0,
        0,
        axis_index_groups=plane_groups(),
        tiled=True,
    ).sum(0)
    return fluxes + sums[0] / sums[1]


def solution(mesh):
    return jax.shard_map(
        per_device,
        mesh=mesh,
        in_specs=(
            P(None, "row"),
            P(None, "comp"),
            P("comp"),
            P("comp"),
            P(None, "row"),
            P("row", None),
            P("row", None),
            P(None, None, "row"),
        ),
        out_specs=P("comp"),
        check_vma=False,
    )
```

time: 550 us -> 138 us (0.25)
  blocking collectives: 265 us -> 16.9 us
  other arithmetic: 140 us -> 1.5 us
  waiting for transfers between devices: 56.8 us -> 6.79 us
  Pallas kernels: 0 us -> 45.6 us
  starting transfers between devices: 0.01 us -> 31.9 us
  matrix products: 28.2 us -> 0 us
  between operations: 13.4 us -> 0.23 us
  local copies, waits for them, and re-layouts: 44.7 us -> 33.7 us
    psum x6 -> x0, blocking collectives: 265 us -> none  [the longest x2 167 us: per_device(): numerator, curvature = lax.psum((numerator, curvature), 'row')]
    convert_element_type x4 -> x0, other arithmetic: 129 us -> none  [phase_tables(): sines.append(jnp.sin(angle).astype(jnp.bfloat16))]
    all_gather x1 -> x0, waiting for transfers between devices: 56.8 us -> none  [per_device(): gain_table = lax.all_gather(owned, 'row', axis=0, tiled=True)]
    pallas_call x0 -> x6, Pallas kernels: none -> 45.6 us  [the longest x2 23.6 us: make_tables(): pl.pallas_call(table_kernel, grid=(count,), in_specs=[pl.BlockSpec((2, co...]
    unnamed x2 -> x51, local copies, waits for them, and re-layouts: 0.01 us -> 33.6 us
    dot_general x16 -> x0, matrix products: 28.2 us -> none  [the longest x4 12.4 us: visit(): lax.dot_general(cos_tab, weight_re, dims, preferred_element_type=jnp.floa...]
    gather x8 -> x0, local copies, waits for them, and re-layouts: 19.4 us -> none  [the longest x4 13 us: station_products(): jnp.take(gain_table, first_station, axis=0).reshape(row_count, 2, F, C)]
    all_to_all x0 -> x1, blocking collectives: none -> 16.9 us  [per_device(): lax.all_to_all(jnp.broadcast_to(sums[None], (16,) + sums.shape), 'row', 0...]
  transfers between devices with their start and end apart: 1 -> 10, of which waited for: 1 -> 3; matrix products, arithmetic and copies ran while one was open for 0% -> 0% of each run, Pallas kernels for 0% -> 25%
where the time goes in v1:
time: 138 us; the launch traced here: 137 us
  Pallas kernels  45.6 us (33%)
  local copies, waits for them, and re-layouts  33.7 us (24%)
  starting transfers between devices  31.9 us (23%)
  blocking collectives  16.9 us (12%)
  waiting for transfers between devices  6.79 us (5%)
  other arithmetic  1.5 us (1%)
    unnamed x51, local copies, waits for them, and re-layouts  33.6 us
    pallas_call x2, Pallas kernels, make_tables(): pl.pallas_call(table_kernel, grid=(count,), in_specs=[pl.BlockSpec((2, co...  23.6 us
    all_to_all x1, blocking collectives, per_device(): lax.all_to_all(jnp.broadcast_to(sums[None], (16,) + sums.shape), 'row', 0...  16.9 us
    ppermute x8, starting transfers between devices, permute(): return lax.ppermute(x, 'row', pairs)  16.8 us
    all_to_all x2, starting transfers between devices, per_device(): sent = [lax.all_to_all(m, 'comp', 0, 0, tiled=True) for m in models]  15.1 us
    pallas_call x2, Pallas kernels, make_scores(): pl.pallas_call(score_kernel, grid=(count,), in_specs=[pl.BlockSpec((peers...  13.3 us
    pallas_call x2, Pallas kernels, make_model(): pl.pallas_call(model_kernel, grid=(count,), in_specs=[pl.BlockSpec(memory...  8.66 us
    ppermute x8, waiting for transfers between devices, permute(): return lax.ppermute(x, 'row', pairs)  6.78 us
  transfers between devices with their start and end apart: 10, of which 3 were waited for; matrix products, arithmetic and copies ran while one was open for 0% of the time, Pallas kernels for 25%

profile of v1, /device:TPU:1, one launch (start us, length us, event | category | flops | bytes accessed | tf_op | source)
XLA Modules:
  0.0 136.5 jit_solution(7146276117492414073)
XLA Ops:
  0.0 0.8 constant_dynamic-update-slice_fusion.4
  0.9 3.2 %collective-permute-start = (f32[16,512]{1,0:T(8,128)S(1)}, f32[16,512]{1,0:T(8,128)S(1)}, u32[]{:S(2)}, u32[]{:S(2)}) collective-permute-start(f32[16,512]{1,0:T(8,128)S(1)} %get-tuple-element.26), channel_id=1, source_target_pairs={{0,1},{1,0},{2,3},{3,2},{4,5},{5,4},{6,7},{7,6},{8,9},{9,8},{10,11... | collective-permute-start | bytes 98312 | tf_op jit(solution)/shard_map/ppermute | solution.py:303
  4.1 0.9 collective-permute-done
  5.0 1.0 collective-permute-start.3
  7.0 5.1 %collective-permute-done.1 = f32[32,512]{1,0:T(8,128)S(1)} collective-permute-done((f32[32,512]{1,0:T(8,128)S(1)}, f32[32,512]{1,0:T(8,128)S(1)}, u32[]{:S(2)}, u32[]{:S(2)}) %collective-permute-start.1) | collective-permute-done | bytes 65568 | tf_op jit(solution)/shard_map/ppermute | solution.py:303
  12.1 6.4 %collective-permute-start.6 = (f32[128,512]{1,0:T(8,128)S(1)}, f32[128,512]{1,0:T(8,128)S(1)}, u32[]{:S(2)}, u32[]{:S(2)}) collective-permute-start(f32[128,512]{1,0:T(8,128)S(1)} %constant_dynamic-update-slice_fusion.rest_0_), channel_id=1, source_target_pairs={{0,6},{1,7},{2,0},{3,1},{4,2},{5,3},{6,4},{7,5},{8,14},{9,15},{10,... | collective-permute-start | bytes 786440 | tf_op jit(solution)/shard_map/ppermute | solution.py:303
  18.5 1.0 collective-permute-start.5
  19.5 2.3 %collective-permute-start.4 = (f32[128,512]{1,0:T(8,128)S(1)}, f32[128,512]{1,0:T(8,128)S(1)}, u32[]{:S(2)}, u32[]{:S(2)}) collective-permute-start(f32[128,512]{1,0:T(8,128)S(1)} %constant_dynamic-update-slice_fusion.rest_0_), channel_id=1, source_target_pairs={{0,2},{1,3},{2,4},{3,5},{4,6},{5,7},{6,0},{7,1},{8,10},{9,11},{10,... | collective-permute-start | bytes 786440 | tf_op jit(solution)/shard_map/ppermute | solution.py:303
  21.8 0.8 copy-done.10
  23.9 0.7 copy-done.22
  24.6 8.9 %tables.3 = (bf16[1024,6144]{1,0:T(8,128)(2,1)S(1)}, f32[64,6144]{1,0:T(8,128)S(1)}) custom-call(f32[2,1024]{1,0:T(2,128)S(1)} %copy-done.22, f32[1,1024]{1,0:T(1,128)S(1)} %bitcast.8, s32[1,1024]{1,0:T(1,128)S(1)} %bitcast.4, f32[3,2048]{1,0:T(4,128)S(1)} %copy-done.10, f32[32,512]{1,0:T(8,128)S(1)} %pad_maximum_fusion.rest_0_), custom_call_target="tpu_custom_call" | custom-call | tf_op jit(solution)/shard_map/tables/pallas_call | solution.py:120
  33.5 4.5 %copy-done.2 = bf16[1024,6144]{1,0:T(8,128)(2,1)} copy-done((bf16[1024,6144]{1,0:T(8,128)(2,1)}, bf16[1024,6144]{1,0:T(8,128)(2,1)S(1)}, u32[]{:S(2)}) %copy-start.2) | copy-done | bytes 12582936
  38.0 0.7 copy-done.12
  38.7 3.7 %model.3 = (f32[64,6144]{1,0:T(8,128)S(1)}, f32[8,8,768]{2,1,0:T(8,128)}, f32[64,128]{1,0:T(8,128)S(1)}) custom-call(s32[1]{0:T(128)} %bitcast.me_ref, f32[128,512]{1,0:T(8,128)S(1)} %constant_dynamic-update-slice_fusion.rest_0_, f32[128,512]{1,0:T(8,128)S(1)} %collective-permute-done.4.rest_1_, f32[128,512]{1,0:T(8,128)S(1)} %collective-permute-done.5.rest_2_, ...), custom_call_target="tpu_custom_call" | custom-call | tf_op jit(solution)/shard_map/model/pallas_call | solution.py:203
  42.5 1.2 copy-done.4
  44.3 9.9 %all-to-all-start.1 = ((f32[8,8,768]{2,1,0:T(8,128)}), f32[8,8,768]{2,1,0:T(8,128)}, u32[]{:S(2)}, u32[]{:S(2)}) async-start(f32[8,8,768]{2,1,0:T(8,128)} %get-tuple-element.22), calls=%async_computation.1 | async-start | bytes 393216 | tf_op jit(solution)/shard_map/all_to_all | solution.py:334
  54.2 14.7 %tables.2 = (bf16[1024,10240]{1,0:T(8,128)(2,1)S(1)}, f32[64,10240]{1,0:T(8,128)S(1)}) custom-call(f32[2,1024]{1,0:T(2,128)S(1)} %copy-done.23, f32[1,1024]{1,0:T(1,128)S(1)} %bitcast.9, s32[1,1024]{1,0:T(1,128)S(1)} %bitcast.5, f32[3,2048]{1,0:T(4,128)S(1)} %copy-done.11, f32[128,512]{1,0:T(8,128)S(1)} %constant_dynamic-update-slice_fusion.rest_0_), custom_call_target="tpu_custom_call" | custom-call | tf_op jit(solution)/shard_map/tables/pallas_call | solution.py:120
  68.9 7.0 %copy-done = bf16[1024,10240]{1,0:T(8,128)(2,1)} copy-done((bf16[1024,10240]{1,0:T(8,128)(2,1)}, bf16[1024,10240]{1,0:T(8,128)(2,1)S(1)}, u32[]{:S(2)}) %copy-start) | copy-done | bytes 20971544
  75.9 0.9 copy-done.7
  76.9 4.9 %model.2 = (f32[64,10240]{1,0:T(8,128)S(1)}, f32[8,8,1280]{2,1,0:T(8,128)S(1)}, f32[64,128]{1,0:T(8,128)S(1)}) custom-call(s32[1]{0:T(128)} %bitcast.me_ref, f32[128,512]{1,0:T(8,128)S(1)} %constant_dynamic-update-slice_fusion.rest_0_, f32[128,512]{1,0:T(8,128)S(1)} %copy-done.7, f32[128,512]{1,0:T(8,128)S(1)} %collective-permute-done.5.rest_2_, ...), custom_call_target="tpu_custom_call" | custom-call | tf_op jit(solution)/shard_map/model/pallas_call | solution.py:203
  81.9 0.8 copy-done.8
  83.2 5.1 %all-to-all-start = ((f32[8,8,1280]{2,1,0:T(8,128)}), f32[8,8,1280]{2,1,0:T(8,128)S(1)}, u32[]{:S(2)}, u32[]{:S(2)}) async-start(f32[8,8,1280]{2,1,0:T(8,128)} %copy-done.8), calls=%async_computation | async-start | bytes 655360 | tf_op jit(solution)/shard_map/all_to_all | solution.py:334
  88.4 4.6 %copy-done.3 = bf16[1024,6144]{1,0:T(8,128)(2,1)S(1)} copy-done((bf16[1024,6144]{1,0:T(8,128)(2,1)S(1)}, bf16[1024,6144]{1,0:T(8,128)(2,1)}, u32[]{:S(2)}) %copy-start.3) | copy-done | bytes 12582936
  92.9 1.4 %copy-done.5 = f32[64,6144]{1,0:T(8,128)S(1)} copy-done((f32[64,6144]{1,0:T(8,128)S(1)}, f32[64,6144]{1,0:T(8,128)}, u32[]{:S(2)}) %copy-start.5) | copy-done | bytes 1572888
  94.3 5.1 %scores.2.rest_2_ = f32[1024,64]{1,0:T(8,128)S(1)} custom-call(f32[8,8,768]{2,1,0:T(8,128)} %all-to-all-done.1.parts_ref, f32[2,4,2048]{2,1,0:T(4,128)S(1)} %copy-done.9, f32[64,6144]{1,0:T(8,128)S(1)} %copy-done.5, bf16[1024,6144]{1,0:T(8,128)(2,1)S(1)} %copy-done.3, s32[1,1024]{1,0:T(1,128)S(1)} %bitcast.6), custom_call_target="tpu_custom_call" | custom-call | tf_op jit(solution)/shard_map/scores/pallas_call | solution.py:266
  99.4 7.0 %copy-done.1 = bf16[1024,10240]{1,0:T(8,128)(2,1)S(1)} copy-done((bf16[1024,10240]{1,0:T(8,128)(2,1)S(1)}, bf16[1024,10240]{1,0:T(8,128)(2,1)}, u32[]{:S(2)}) %copy-start.1) | copy-done | bytes 20971544
  106.4 0.8 copy-done.19
  107.1 0.8 copy-done.21
  107.9 8.3 %scores.3 = f32[2,1024]{1,0:T(2,128)S(1)} custom-call(f32[8,8,1280]{2,1,0:T(8,128)S(1)} %all-to-all-done.parts_ref, f32[2,4,2048]{2,1,0:T(4,128)S(1)} %copy-done.9, f32[64,10240]{1,0:T(8,128)S(1)} %get-tuple-element.17.gain_ref, bf16[1024,10240]{1,0:T(8,128)(2,1)S(1)} %copy-done.1, s32[1,1024]{1,0:T(1,128)S(1)} %bitcast.7, f32[64,128]{1,0:T(8,128)S(1)} %copy-done.19, ...), custom_call_target="tpu_custom_call" | custom-call | tf_op jit(solution)/shard_map/scores/pallas_call | solution.py:266
  116.2 1.9 %collective-permute-start.7 = (f32[2,1024]{1,0:T(2,128)S(1)}, f32[2,1024]{1,0:T(2,128)S(1)}, u32[]{:S(2)}, u32[]{:S(2)}) collective-permute-start(f32[2,1024]{1,0:T(2,128)S(1)} %scores.3), channel_id=1, source_target_pairs={{0,1},{1,0},{2,3},{3,2},{4,5},{5,4},{6,7},{7,6},{8,9},{9,8},{10,11... | collective-permute-start | bytes 24584 | tf_op jit(solution)/shard_map/ppermute | solution.py:303
  118.1 0.8 collective-permute-done.7
  118.9 16.9 %all_to_all.15 = f32[16,2,1024]{2,1,0:T(2,128)S(1)} all-to-all(f32[16,2,1024]{2,1,0:T(2,128)S(1)} %broadcast_in_dim.18), channel_id=1, replica_groups={{0,2,4,6,8,10,12,14,16,18,20,22,24,26,28,30},{1,3,5,7,9,11,13,15,17,19,..., dimensions={0} | all-to-all | bytes 262144 | tf_op jit(solution)/shard_map/all_to_all | solution.py:353
  (54 shorter events, 4.4 us)
Async XLA Ops:
  0.0 54.2 %copy-start.17 = (f32[1024]{0:T(1024)S(1)}, f32[1024]{0:T(1024)}, u32[]{:S(2)}) copy-start(f32[1024]{0:T(1024)} %param.10) | copy-start | bytes 12292
  0.0 54.2 %copy-start.23 = (f32[2,1024]{1,0:T(2,128)S(1)}, f32[2,1024]{1,0:T(2,128)}, u32[]{:S(2)}) copy-start(f32[2,1024]{1,0:T(2,128)} %sky_ref.3) | copy-start | bytes 24580
  0.0 54.2 %copy-start.11 = (f32[3,2048]{1,0:T(4,128)S(1)}, f32[3,2048]{1,0:T(4,128)}, u32[]{:S(2)}) copy-start(f32[3,2048]{1,0:T(4,128)} %uvw_ref.3) | copy-start | bytes 73732
  0.0 54.2 %copy-start.15 = (s32[1024]{0:T(1024)S(1)}, s32[1024]{0:T(1024)}, u32[]{:S(2)}) copy-start(s32[1024]{0:T(1024)} %param.11) | copy-start | bytes 12292
  0.0 75.9 %copy-start.13 = (s32[2,2048]{1,0:T(2,128)S(1)}, s32[2,2048]{1,0:T(2,128)}, u32[]{:S(2)}) copy-start(s32[2,2048]{1,0:T(2,128)} %rest_4_.3) | copy-start | bytes 49156
  0.9 4.1 %collective-permute-start = (f32[16,512]{1,0:T(8,128)S(1)}, f32[16,512]{1,0:T(8,128)S(1)}, u32[]{:S(2)}, u32[]{:S(2)}) collective-permute-start(f32[16,512]{1,0:T(8,128)S(1)} %get-tuple-element.26), channel_id=1, source_target_pairs={{0,1},{1,0},{2,3},{3,2},{4,5},{5,4},{6,7},{7,6},{8,9},{9,8},{10,11... | collective-permute-start | bytes 98312 | tf_op jit(solution)/shard_map/ppermute | solution.py:303
  5.0 7.2 %collective-permute-start.3 = (f32[32,512]{1,0:T(8,128)S(1)}, f32[32,512]{1,0:T(8,128)S(1)}, u32[]{:S(2)}, u32[]{:S(2)}) collective-permute-start(f32[32,512]{1,0:T(8,128)S(1)} %pad_maximum_fusion.rest_0_), channel_id=1, source_target_pairs={{0,24},{1,25},{2,26},{3,27},{4,28},{5,29},{6,30},{7,31},{8,0},{9,1... | collective-permute-start | bytes 196616 | tf_op jit(solution)/shard_map/ppermute | solution.py:303
  6.0 6.1 %collective-permute-start.2 = (f32[32,512]{1,0:T(8,128)S(1)}, f32[32,512]{1,0:T(8,128)S(1)}, u32[]{:S(2)}, u32[]{:S(2)}) collective-permute-start(f32[32,512]{1,0:T(8,128)S(1)} %pad_maximum_fusion.rest_0_), channel_id=1, source_target_pairs={{0,16},{1,17},{2,18},{3,19},{4,20},{5,21},{6,22},{7,23},{8,24},{9,... | collective-permute-start | bytes 196616 | tf_op jit(solution)/shard_map/ppermute | solution.py:303
  6.3 5.8 %collective-permute-start.1 = (f32[32,512]{1,0:T(8,128)S(1)}, f32[32,512]{1,0:T(8,128)S(1)}, u32[]{:S(2)}, u32[]{:S(2)}) collective-permute-start(f32[32,512]{1,0:T(8,128)S(1)} %pad_maximum_fusion.rest_0_), channel_id=1, source_target_pairs={{0,8},{1,9},{2,10},{3,11},{4,12},{5,13},{6,14},{7,15},{8,16},{9,17... | collective-permute-start | bytes 196616 | tf_op jit(solution)/shard_map/ppermute | solution.py:303
  12.1 25.8 %collective-permute-start.6 = (f32[128,512]{1,0:T(8,128)S(1)}, f32[128,512]{1,0:T(8,128)S(1)}, u32[]{:S(2)}, u32[]{:S(2)}) collective-permute-start(f32[128,512]{1,0:T(8,128)S(1)} %constant_dynamic-update-slice_fusion.rest_0_), channel_id=1, source_target_pairs={{0,6},{1,7},{2,0},{3,1},{4,2},{5,3},{6,4},{7,5},{8,14},{9,15},{10,... | collective-permute-start | bytes 786440 | tf_op jit(solution)/shard_map/ppermute | solution.py:303
  18.5 19.4 %collective-permute-start.5 = (f32[128,512]{1,0:T(8,128)S(1)}, f32[128,512]{1,0:T(8,128)S(1)}, u32[]{:S(2)}, u32[]{:S(2)}) collective-permute-start(f32[128,512]{1,0:T(8,128)S(1)} %constant_dynamic-update-slice_fusion.rest_0_), channel_id=1, source_target_pairs={{0,4},{1,5},{2,6},{3,7},{4,0},{5,1},{6,2},{7,3},{8,12},{9,13},{10,... | collective-permute-start | bytes 786440 | tf_op jit(solution)/shard_map/ppermute | solution.py:303
  19.5 18.5 %collective-permute-start.4 = (f32[128,512]{1,0:T(8,128)S(1)}, f32[128,512]{1,0:T(8,128)S(1)}, u32[]{:S(2)}, u32[]{:S(2)}) collective-permute-start(f32[128,512]{1,0:T(8,128)S(1)} %constant_dynamic-update-slice_fusion.rest_0_), channel_id=1, source_target_pairs={{0,2},{1,3},{2,4},{3,5},{4,6},{5,7},{6,0},{7,1},{8,10},{9,11},{10,... | collective-permute-start | bytes 786440 | tf_op jit(solution)/shard_map/ppermute | solution.py:303
  21.8 0.8 copy-start.10
  22.5 0.7 copy-start.14
  23.2 0.7 copy-start.16
  23.9 0.7 copy-start.22
  33.5 4.5 %copy-start.2 = (bf16[1024,6144]{1,0:T(8,128)(2,1)}, bf16[1024,6144]{1,0:T(8,128)(2,1)S(1)}, u32[]{:S(2)}) copy-start(bf16[1024,6144]{1,0:T(8,128)(2,1)S(1)} %get-tuple-element.24.table_ref) | copy-start | bytes 37748740
  38.0 30.9 %copy-start.6 = (f32[128,512]{1,0:T(8,128)}, f32[128,512]{1,0:T(8,128)S(1)}, u32[]{:S(2)}) copy-start(f32[128,512]{1,0:T(8,128)S(1)} %collective-permute-done.4.rest_1_) | copy-start | bytes 786436
  38.0 0.7 copy-start.12
  42.5 1.2 copy-start.4
  44.3 44.1 %copy-start.9 = (f32[2,4,2048]{2,1,0:T(4,128)S(1)}, f32[2,4,2048]{2,1,0:T(4,128)}, u32[]{:S(2)}) copy-start(f32[2,4,2048]{2,1,0:T(4,128)} %obs_ref.3) | copy-start | bytes 196612
  44.3 39.0 %all-to-all-start.1 = ((f32[8,8,768]{2,1,0:T(8,128)}), f32[8,8,768]{2,1,0:T(8,128)}, u32[]{:S(2)}, u32[]{:S(2)}) async-start(f32[8,8,768]{2,1,0:T(8,128)} %get-tuple-element.22), calls=%async_computation.1 | async-start | bytes 393216 | tf_op jit(solution)/shard_map/all_to_all | solution.py:334
  68.9 7.0 %copy-start = (bf16[1024,10240]{1,0:T(8,128)(2,1)}, bf16[1024,10240]{1,0:T(8,128)(2,1)S(1)}, u32[]{:S(2)}) copy-start(bf16[1024,10240]{1,0:T(8,128)(2,1)S(1)} %get-tuple-element.18.table_ref) | copy-start | bytes 62914564
  75.9 1.0 copy-start.7
  81.8 0.8 copy-start.8
  83.2 16.2 %all-to-all-start = ((f32[8,8,1280]{2,1,0:T(8,128)}), f32[8,8,1280]{2,1,0:T(8,128)S(1)}, u32[]{:S(2)}, u32[]{:S(2)}) async-start(f32[8,8,1280]{2,1,0:T(8,128)} %copy-done.8), calls=%async_computation | async-start | bytes 655360 | tf_op jit(solution)/shard_map/all_to_all | solution.py:334
  88.4 4.6 %copy-start.3 = (bf16[1024,6144]{1,0:T(8,128)(2,1)S(1)}, bf16[1024,6144]{1,0:T(8,128)(2,1)}, u32[]{:S(2)}) copy-start(bf16[1024,6144]{1,0:T(8,128)(2,1)} %copy-done.2) | copy-start | bytes 37748740
  92.9 1.4 %copy-start.5 = (f32[64,6144]{1,0:T(8,128)S(1)}, f32[64,6144]{1,0:T(8,128)}, u32[]{:S(2)}) copy-start(f32[64,6144]{1,0:T(8,128)} %copy-done.4) | copy-start | bytes 4718596
  99.4 7.0 %copy-start.1 = (bf16[1024,10240]{1,0:T(8,128)(2,1)S(1)}, bf16[1024,10240]{1,0:T(8,128)(2,1)}, u32[]{:S(2)}) copy-start(bf16[1024,10240]{1,0:T(8,128)(2,1)} %copy-done) | copy-start | bytes 62914564
  106.4 0.8 copy-start.19
  107.1 0.8 copy-start.21
  116.2 2.7 %collective-permute-start.7 = (f32[2,1024]{1,0:T(2,128)S(1)}, f32[2,1024]{1,0:T(2,128)S(1)}, u32[]{:S(2)}, u32[]{:S(2)}) collective-permute-start(f32[2,1024]{1,0:T(2,128)S(1)} %scores.3), channel_id=1, source_target_pairs={{0,1},{1,0},{2,3},{3,2},{4,5},{5,4},{6,7},{7,6},{8,9},{9,8},{10,11... | collective-permute-start | bytes 24584 | tf_op jit(solution)/shard_map/ppermute | solution.py:303
  (2 other events, 1.2 us)

commit v2 on v0

v2 whole, which is shorter than its diff:
```python
import functools
import math

import jax
import jax.numpy as jnp
import numpy as np
from jax import lax
from jax.experimental import pallas as pl
from jax.experimental.pallas import tpu as pltpu
from jax.sharding import PartitionSpec as P

C = 64
F = 4
BLOCK = 256
WIDE = 2 * F * BLOCK
CHUNK = 256
TILE = 16
GROUPS = (4, 4)
SCOPED = 10 << 20
F32 = jnp.float32
BF16 = jnp.bfloat16


def sine_fit():
    y = 0.5 * np.cos(np.pi * (np.arange(400) + 0.5) / 400)
    fit = np.polynomial.polynomial.polyfit(y * y, 2.0 * np.sin(0.5 * np.pi * y) / y, 2)
    return [float(np.float32(v)) for v in fit]


ODD = sine_fit()
SCALES = (0.5, 0.25, 0.25, 0.25)
ROUND = 12582912.0


def split3(x):
    high = x.astype(BF16).astype(F32)
    rest = x - high
    mid = rest.astype(BF16).astype(F32)
    return high, mid, rest - mid


def left_terms(x):
    h, m, l = split3(x)
    return [h, h, m, h, l, m, m, l]


def right_terms(x):
    h, m, l = split3(x)
    return [h, m, h, l, h, m, l, m]


def stack_terms(terms):
    pad = jnp.zeros((8, terms[0].shape[1]), F32)
    return jnp.concatenate(terms + [pad], axis=0)


def phases(eighth):
    y = eighth - (jnp.round(eighth))
    y2 = y * y
    s = y * (ODD[0] + y2 * (ODD[1] + y2 * ODD[2]))
    cc = 4.0 - s * s
    s = s * (cc * lax.rsqrt(cc))
    c = cc - 2.0

    def double(c, s):
        return c * c - 2.0, s * c

    c1, s1 = double(c, s)
    c, s = double(c1, s1)
    c, s = double(c, s)
    c8, s8 = double(c, s)
    c9, s9 = c8 * c1 - s8 * s1, s8 * c1 + c8 * s1
    c10, s10 = c1 * c9 - (c8 + c8), c1 * s9 - (s8 + s8)
    c11, s11 = c1 * c10 - c9, c1 * s10 - s9
    return (c8, c9, c10, c11, s8, s9, s10, s11)


def table_kernel(first, count, sky_ref, flux_ref, clus_ref, uvw_ref, *rest):
    *table_refs, pred_ref, left, hot, late = rest[-(sky_ref.shape[1] // CHUNK + 4) :]
    comps = sky_ref.shape[1]
    chunks, tiles, pieces = comps // CHUNK, CHUNK // TILE, WIDE // CHUNK

    east, north = sky_ref[0:1, :], sky_ref[1:2, :]
    depth = jnp.sqrt(1.0 - east * east - north * north) - 1.0
    place = jnp.concatenate([east, north, depth], axis=0)
    left[...] = jnp.transpose(stack_terms(left_terms(place))).astype(BF16)
    ids = lax.broadcasted_iota(jnp.int32, (C, comps), 0)
    hot[...] = jnp.where(ids == clus_ref[...], flux_ref[...], 0.0).astype(BF16)
    late[...] = jnp.zeros_like(late)
    last = chunks - 1

    def matmul(i, chunk, n):
        at, to = pl.ds(chunk * CHUNK, CHUNK), pl.ds(n * CHUNK, CHUNK)
        source = late[:, to] if chunk == last else table_refs[chunk][i, :, to]
        part = jnp.dot(hot[:, at], source, preferred_element_type=F32)
        if chunk == 0:
            pred_ref[i, :, to] = part
        else:
            pred_ref[i, :, to] += part

    def block(i, carry):
        before = jnp.maximum(i - 1, 0)
        uvw = uvw_ref[:, pl.ds(pl.multiple_of((i + first) * BLOCK, BLOCK), BLOCK)]
        right = stack_terms(right_terms(uvw * 0.125)).astype(BF16)
        for chunk in range(chunks):
            base = jnp.dot(
                left[pl.ds(chunk * CHUNK, CHUNK), :], right, preferred_element_type=F32
            )
            for tile in range(tiles):
                values = phases(base[tile * TILE : (tile + 1) * TILE, :])
                for j, value in enumerate(values):
                    value = value.astype(BF16)
                    to = pl.ds(j * BLOCK, BLOCK)
                    table_refs[chunk][i, pl.ds(tile * TILE, TILE), to] = value
                    if chunk == last:
                        late[pl.ds(tile * TILE, TILE), to] = value
                if tile % (tiles // pieces) == 0:
                    n = tile // (tiles // pieces)
                    if chunk:
                        matmul(i, chunk - 1, n)
                    else:
                        matmul(before, last, n)
        return carry

    pred_ref[0] = jnp.zeros(pred_ref.shape[1:], F32)
    lax.fori_loop(0, count, block, 0)
    for n in range(pieces):
        matmul(count - 1, last, n)


def in_vmem(x):
    return pltpu.with_memory_space_constraint(x, pltpu.VMEM)


def make_tables(first, count, sky, fluxes, clusters, uvw, after, held):
    comps = sky.shape[1]
    vmem = pl.BlockSpec(memory_space=pltpu.VMEM)
    chunks = comps // CHUNK
    return pl.pallas_call(
        functools.partial(table_kernel, first, count),
        in_specs=[vmem] * (4 + len(held)) + [pl.BlockSpec(memory_space=pl.ANY)] * len(after),
        out_specs=[vmem] * (chunks + 1),
        out_shape=[pltpu.VMEM((count, CHUNK, WIDE), BF16)] * chunks
        + [pltpu.VMEM((count, C, WIDE), F32)],
        scratch_shapes=[
            pltpu.VMEM((comps, 32), BF16),
            pltpu.VMEM((C, comps), BF16),
            pltpu.VMEM((CHUNK, WIDE), BF16),
        ],
        compiler_params=pltpu.CompilerParams(vmem_limit_bytes=SCOPED),
        name="tables",
    )(sky, fluxes, clusters, uvw, *map(in_vmem, held), *after)


def model_kernel(me_ref, *rest):
    pieces, pair_ref, preds = rest[:4], rest[4], rest[5 : 5 + len(GROUPS)]
    gain_ref, model_ref, curv_ref, table, found = rest[-5:]
    owned = pieces[0].shape[0] // 8
    for n, piece in enumerate(pieces):
        flat = jnp.transpose(piece[...])
        high = flat.astype(BF16)
        at = pl.ds(n * flat.shape[1], flat.shape[1])
        table[pl.ds(0, flat.shape[0]), at] = high
        table[pl.ds(flat.shape[0], flat.shape[0]), at] = (flat - high.astype(F32)).astype(BF16)

    me = me_ref[0]
    my_y, my_z, my_core = me >> 3, (me >> 1) & 3, me & 1
    stations = table.shape[1]
    columns = table.shape[0] // 2
    ids = lax.broadcasted_iota(jnp.int32, (stations, BLOCK), 0)
    pair = pair_ref[...]
    owner, own = pair // owned, pair % owned
    y, z, core = owner >> 3, (owner >> 1) & 3, owner & 1
    slot = ((((my_z - z) & 3) * 4 + ((my_y - y) & 3)) * 2 + (core ^ my_core)) * owned + own

    def gather(i):
        for side in range(2):
            hot = ids == slot[side : side + 1, i * BLOCK : (i + 1) * BLOCK]
            hot = jnp.where(hot, 1.0, 0.0).astype(BF16)
            both = jnp.dot(table[...], hot, preferred_element_type=F32)
            found[i % 2, side] = both[:columns] + both[columns:]

    curv = jnp.zeros((C, BLOCK), F32)
    count = gain_ref.shape[0]
    gather(0)
    blocks = [(pred, i) for pred in preds for i in range(pred.shape[0])]
    for i, (pred_ref, own_i) in enumerate(blocks):
        if i + 1 < count:
            gather(i + 1)
        rows = []
        for f in range(F):
            re, im = pl.ds(f * BLOCK, BLOCK), pl.ds((F + f) * BLOCK, BLOCK)
            at_re, at_im = pl.ds(f * C, C), pl.ds((F + f) * C, C)
            p_re, p_im = found[i % 2, 0, at_re], found[i % 2, 0, at_im]
            q_re, q_im = found[i % 2, 1, at_re], found[i % 2, 1, at_im]
            g_re = p_re * q_re + p_im * q_im
            g_im = p_im * q_re - p_re * q_im
            gain_ref[i, :, re] = g_re
            gain_ref[i, :, im] = g_im
            cos_sum, sin_sum = pred_ref[own_i, :, re], pred_ref[own_i, :, im]
            rows.append(
                (
                    SCALES[f] * jnp.sum(g_re * cos_sum + g_im * sin_sum, axis=0, keepdims=True),
                    SCALES[f] * jnp.sum(g_im * cos_sum - g_re * sin_sum, axis=0, keepdims=True),
                )
            )
            curv = curv + (g_re * g_re + g_im * g_im)
        model = jnp.concatenate([r[0] for r in rows] + [r[1] for r in rows], axis=0)
        for n in range(model_ref.shape[0]):
            model_ref[n, :, pl.ds(i * BLOCK, BLOCK)] = model
    curv_ref[...] = curv[:, :128] + curv[:, 128:]


def make_model(me, pieces, stations, preds, held, peers):
    rows, columns = pieces[0].shape
    count = sum(pred.shape[0] for pred in preds)
    vmem = pl.BlockSpec(memory_space=pltpu.VMEM)
    return pl.pallas_call(
        model_kernel,
        in_specs=[pl.BlockSpec(memory_space=pltpu.SMEM)] + [vmem] * (5 + len(preds) + len(held)),
        out_specs=[vmem] * 3,
        out_shape=[
            pltpu.VMEM((count, C, WIDE), F32),
            jax.ShapeDtypeStruct((peers, 2 * F, count * BLOCK), F32),
            jax.ShapeDtypeStruct((C, 128), F32),
        ],
        scratch_shapes=[
            pltpu.VMEM((2 * columns, 4 * rows), BF16),
            pltpu.VMEM((2, 2, columns, BLOCK), F32),
        ],
        compiler_params=pltpu.CompilerParams(vmem_limit_bytes=SCOPED),
        name="model",
    )(me, *pieces, stations, *map(in_vmem, preds), *map(in_vmem, held))


def score_kernel(parts_ref, obs_ref, gain_ref, clus_ref, curv_ref, *rest):
    *tables, out_ref, weight = rest
    chunks = len(tables) // len(GROUPS)
    blocks = [
        (tables[n * chunks : (n + 1) * chunks], i) for n in range(len(GROUPS)) for i in range(GROUPS[n])
    ]

    def weigh(i):
        at = pl.ds(i * BLOCK, BLOCK)
        model = jnp.sum(parts_ref[:, :, at], axis=0)
        for f in range(F):
            re, im = pl.ds(f * BLOCK, BLOCK), pl.ds((F + f) * BLOCK, BLOCK)
            r_re = SCALES[f] * (obs_ref[0, f : f + 1, at] - model[f : f + 1, :])
            r_im = SCALES[f] * (obs_ref[1, f : f + 1, at] - model[F + f : F + f + 1, :])
            g_re, g_im = gain_ref[i, :, re], gain_ref[i, :, im]
            weight[i % 2, :, re] = (r_re * g_re + r_im * g_im).astype(BF16)
            weight[i % 2, :, im] = (r_re * g_im - r_im * g_re).astype(BF16)

    weigh(0)
    scores = [jnp.zeros((C, CHUNK), F32)] * chunks
    for i, (group, own_i) in enumerate(blocks):
        for n in range(chunks):
            scores[n] = scores[n] + lax.dot_general(
                weight[i % 2], group[n][own_i], (((1,), (1,)), ((), ())), preferred_element_type=F32
            )
        if i + 1 < len(blocks):
            weigh(i + 1)
    scores = jnp.concatenate(scores, axis=1)
    hot = lax.broadcasted_iota(jnp.int32, scores.shape, 0) == clus_ref[...]
    curv = jnp.sum(curv_ref[...], axis=1, keepdims=True)
    out_ref[0:1, :] = jnp.sum(jnp.where(hot, scores, 0.0), axis=0, keepdims=True)
    out_ref[1:2, :] = jnp.sum(jnp.where(hot, curv, 0.0), axis=0, keepdims=True)


def make_scores(parts, observed, gain, clusters, curv, tables):
    comps = clusters.shape[1]
    vmem = pl.BlockSpec(memory_space=pltpu.VMEM)
    return pl.pallas_call(
        score_kernel,
        in_specs=[vmem] * (5 + len(tables)),
        out_specs=vmem,
        out_shape=jax.ShapeDtypeStruct((2, comps), F32),
        scratch_shapes=[pltpu.VMEM((2, C, WIDE), BF16)],
        compiler_params=pltpu.CompilerParams(vmem_limit_bytes=SCOPED),
        name="scores",
    )(parts, observed, in_vmem(gain), clusters, curv, *map(in_vmem, tables))


def other_core():
    return [(i, i ^ 1) for i in range(32)]


def turn_y(k):
    return [(i, (i + 8 * k) % 32) for i in range(32)]


def turn_z(k):
    return [(i, i // 8 * 8 + ((i // 2 % 4 + k) % 4) * 2 + i % 2) for i in range(32)]


def plane_groups():
    return [[2 * i + core for i in range(16)] for core in range(2)]


def permute(x, pairs):
    return lax.ppermute(x, "row", pairs)


def per_device(
    baseline_uvw, sky_positions, fluxes, clusters, stations, station_gains, gain_step, observed_vis
):
    flux_row, cluster_row = fluxes[None, :], clusters[None, :]
    peers = lax.axis_size("comp")
    me = lax.axis_index("row").astype(jnp.int32)[None]
    firsts = [sum(GROUPS[:n]) for n in range(len(GROUPS))]

    owned = station_gains + gain_step
    chip = jnp.concatenate([owned, permute(owned, other_core())], axis=0)
    line = jnp.concatenate([chip] + [permute(chip, turn_y(k)) for k in (1, 2, 3)], axis=0)
    pieces = [line] + [permute(line, turn_z(k)) for k in (1, 2, 3)]

    after = ([chip], [line])
    tables, preds = [], []
    for n, count in enumerate(GROUPS):
        *parts, pred = make_tables(
            firsts[n],
            count,
            sky_positions,
            flux_row,
            cluster_row,
            baseline_uvw,
            after[n],
            tables + preds,
        )
        tables += parts
        preds.append(pred)
    gain, model, curv = make_model(me, pieces, stations, preds, tables, peers)
    parts = lax.all_to_all(model, "comp", 0, 0, tiled=True)
    sums = make_scores(parts, observed_vis, gain, cluster_row, curv, tables)
    sums = sums + permute(sums, other_core())
    sums = lax.all_to_all(
        jnp.broadcast_to(sums[None], (16,) + sums.shape),
        "row",
        0,
        0,
        axis_index_groups=plane_groups(),
        tiled=True,
    ).sum(0)
    return fluxes + sums[0] / sums[1]


def solution(mesh):
    return jax.shard_map(
        per_device,
        mesh=mesh,
        in_specs=(
            P(None, "row"),
            P(None, "comp"),
            P("comp"),
            P("comp"),
            P(None, "row"),
            P("row", None),
            P("row", None),
            P(None, None, "row"),
        ),
        out_specs=P("comp"),
        check_vma=False,
    )
```

time: 550 us -> 94.3 us (0.17)
  blocking collectives: 265 us -> 29 us
  other arithmetic: 140 us -> 1.46 us
  waiting for transfers between devices: 56.8 us -> 6.78 us
  local copies, waits for them, and re-layouts: 44.7 us -> 2.91 us
  Pallas kernels: 0 us -> 35.5 us
  matrix products: 28.2 us -> 0 us
  starting transfers between devices: 0.01 us -> 18 us
  between operations: 13.4 us -> 0.14 us
    psum x6 -> x0, blocking collectives: 265 us -> none  [the longest x2 167 us: per_device(): numerator, curvature = lax.psum((numerator, curvature), 'row')]
    convert_element_type x4 -> x0, other arithmetic: 129 us -> none  [phase_tables(): sines.append(jnp.sin(angle).astype(jnp.bfloat16))]
    all_gather x1 -> x0, waiting for transfers between devices: 56.8 us -> none  [per_device(): gain_table = lax.all_gather(owned, 'row', axis=0, tiled=True)]
    pallas_call x0 -> x4, Pallas kernels: none -> 35.5 us  [the longest x2 19.2 us: make_tables(): pl.pallas_call(functools.partial(table_kernel, first, count), in_specs=[v...]
    all_to_all x0 -> x2, blocking collectives: none -> 29 us  [the longest x1 16.7 us: per_device(): lax.all_to_all(jnp.broadcast_to(sums[None], (16,) + sums.shape), 'row', 0...]
    dot_general x16 -> x0, matrix products: 28.2 us -> none  [the longest x4 12.4 us: visit(): lax.dot_general(cos_tab, weight_re, dims, preferred_element_type=jnp.floa...]
    gather x8 -> x0, local copies, waits for them, and re-layouts: 19.4 us -> none  [the longest x4 13 us: station_products(): jnp.take(gain_table, first_station, axis=0).reshape(row_count, 2, F, C)]
    ppermute x0 -> x8, starting transfers between devices: none -> 18 us  [permute(): return lax.ppermute(x, 'row', pairs)]
  transfers between devices with their start and end apart: 1 -> 8, of which waited for: 1 -> 3; matrix products, arithmetic and copies ran while one was open for 0% -> 0% of each run, Pallas kernels for 0% -> 20%
where the time goes in v2:
time: 94.3 us; the launch traced here: 93.9 us
  Pallas kernels  35.5 us (38%)
  blocking collectives  29 us (31%)
  starting transfers between devices  18 us (19%)
  waiting for transfers between devices  6.78 us (7%)
  local copies, waits for them, and re-layouts  2.91 us (3%)
  other arithmetic  1.46 us (2%)
    pallas_call x2, Pallas kernels, make_tables(): pl.pallas_call(functools.partial(table_kernel, first, count), in_specs=[v...  19.2 us
    ppermute x8, starting transfers between devices, permute(): return lax.ppermute(x, 'row', pairs)  18 us
    all_to_all x1, blocking collectives, per_device(): lax.all_to_all(jnp.broadcast_to(sums[None], (16,) + sums.shape), 'row', 0...  16.7 us
    all_to_all x1, blocking collectives, per_device(): parts = lax.all_to_all(model, 'comp', 0, 0, tiled=True)  12.3 us
    pallas_call x1, Pallas kernels, make_scores(): pl.pallas_call(score_kernel, in_specs=[vmem] * (5 + len(tables)), out_spe...  10.3 us
    ppermute x8, waiting for transfers between devices, permute(): return lax.ppermute(x, 'row', pairs)  6.78 us
    pallas_call x1, Pallas kernels, make_model(): pl.pallas_call(model_kernel, in_specs=[pl.BlockSpec(memory_space=pltpu.SM...  5.99 us
    unnamed x19, local copies, waits for them, and re-layouts  2.87 us
  transfers between devices with their start and end apart: 8, of which 3 were waited for; matrix products, arithmetic and copies ran while one was open for 0% of the time, Pallas kernels for 20%

profile of v2, /device:TPU:1, one launch (start us, length us, event | category | flops | bytes accessed | tf_op | source)
XLA Modules:
  0.0 93.9 jit_solution(12748586074892831802)
XLA Ops:
  0.0 0.8 constant_dynamic-update-slice_fusion.4
  0.8 3.2 %collective-permute-start = (f32[16,512]{1,0:T(8,128)S(1)}, f32[16,512]{1,0:T(8,128)S(1)}, u32[]{:S(2)}, u32[]{:S(2)}) collective-permute-start(f32[16,512]{1,0:T(8,128)S(1)} %get-tuple-element.32), channel_id=1, source_target_pairs={{0,1},{1,0},{2,3},{3,2},{4,5},{5,4},{6,7},{7,6},{8,9},{9,8},{10,11... | collective-permute-start | bytes 98312 | tf_op jit(solution)/shard_map/ppermute | solution.py:301
  4.0 0.9 collective-permute-done
  4.9 1.0 %collective-permute-start.3 = (f32[32,512]{1,0:T(8,128)S(1)}, f32[32,512]{1,0:T(8,128)S(1)}, u32[]{:S(2)}, u32[]{:S(2)}) collective-permute-start(f32[32,512]{1,0:T(8,128)S(1)} %pad_maximum_fusion.rest_0_), channel_id=1, source_target_pairs={{0,24},{1,25},{2,26},{3,27},{4,28},{5,29},{6,30},{7,31},{8,0},{9,1... | collective-permute-start | bytes 196616 | tf_op jit(solution)/shard_map/ppermute | solution.py:301
  5.9 0.3 collective-permute-start.2
  6.2 0.7 collective-permute-start.1
  6.9 5.1 %collective-permute-done.1 = f32[32,512]{1,0:T(8,128)S(1)} collective-permute-done((f32[32,512]{1,0:T(8,128)S(1)}, f32[32,512]{1,0:T(8,128)S(1)}, u32[]{:S(2)}, u32[]{:S(2)}) %collective-permute-start.1) | collective-permute-done | bytes 65568 | tf_op jit(solution)/shard_map/ppermute | solution.py:301
  12.0 0.0 collective-permute-done.2
  12.0 0.0 collective-permute-done.3
  12.1 6.4 %collective-permute-start.6 = (f32[128,512]{1,0:T(8,128)S(1)}, f32[128,512]{1,0:T(8,128)}, u32[]{:S(2)}, u32[]{:S(2)}) collective-permute-start(f32[128,512]{1,0:T(8,128)S(1)} %constant_dynamic-update-slice_fusion.rest_5_.rest_0_), channel_id=1, source_target_pairs={{0,6},{1,7},{2,0},{3,1},{4,2},{5,3},{6,4},{7,5},{8,14},{9,15},{10,... | collective-permute-start | bytes 786440 | tf_op jit(solution)/shard_map/ppermute | solution.py:301
  18.5 1.0 %collective-permute-start.5 = (f32[128,512]{1,0:T(8,128)S(1)}, f32[128,512]{1,0:T(8,128)}, u32[]{:S(2)}, u32[]{:S(2)}) collective-permute-start(f32[128,512]{1,0:T(8,128)S(1)} %constant_dynamic-update-slice_fusion.rest_5_.rest_0_), channel_id=1, source_target_pairs={{0,4},{1,5},{2,6},{3,7},{4,0},{5,1},{6,2},{7,3},{8,12},{9,13},{10,... | collective-permute-start | bytes 786440 | tf_op jit(solution)/shard_map/ppermute | solution.py:301
  19.4 2.3 %collective-permute-start.4 = (f32[128,512]{1,0:T(8,128)S(1)}, f32[128,512]{1,0:T(8,128)}, u32[]{:S(2)}, u32[]{:S(2)}) collective-permute-start(f32[128,512]{1,0:T(8,128)S(1)} %constant_dynamic-update-slice_fusion.rest_5_.rest_0_), channel_id=1, source_target_pairs={{0,2},{1,3},{2,4},{3,5},{4,6},{5,7},{6,0},{7,1},{8,10},{9,11},{10,... | collective-permute-start | bytes 786440 | tf_op jit(solution)/shard_map/ppermute | solution.py:301
  21.7 0.8 copy-done
  22.5 0.7 copy-done.2
  23.2 0.7 copy-done.4
  23.8 0.7 copy-done.6
  24.5 9.7 %tables.2 = (bf16[4,256,2048]{2,1,0:T(8,128)(2,1)S(1)}, bf16[4,256,2048]{2,1,0:T(8,128)(2,1)S(1)}, bf16[4,256,2048]{2,1,0:T(8,128)(2,1)S(1)}, bf16[4,256,2048]{2,1,0:T(8,128)(2,1)S(1)}, f32[4,64,2048]{2,1,0:T(8,128)S(1)}) custom-call(f32[2,1024]{1,0:T(2,128)S(1)} %copy-done.6, f32[1,1024]{1,0:T(1,128)S(1)} %bitcast.7, s32[1,1024]{1,0:T(1,128)S(1)} %bitcast.4, ...), custom_call_target="tpu_custom_call" | custom-call | tf_op jit(solution)/shard_map/tables/pallas_call | solution.py:139
  34.2 0.0 copy-start.7
  34.2 9.6 %tables.3 = (bf16[4,256,2048]{2,1,0:T(8,128)(2,1)S(1)}, bf16[4,256,2048]{2,1,0:T(8,128)(2,1)S(1)}, bf16[4,256,2048]{2,1,0:T(8,128)(2,1)S(1)}, bf16[4,256,2048]{2,1,0:T(8,128)(2,1)S(1)}, f32[4,64,2048]{2,1,0:T(8,128)S(1)}) custom-call(f32[2,1024]{1,0:T(2,128)S(1)} %copy-done.6, f32[1,1024]{1,0:T(1,128)S(1)} %bitcast.8, s32[1,1024]{1,0:T(1,128)S(1)} %bitcast.5, ...), custom_call_target="tpu_custom_call" | custom-call | tf_op jit(solution)/shard_map/tables/pallas_call | solution.py:139
  43.8 0.0 collective-permute-done.6.rest_3_
  43.8 0.0 collective-permute-done.5.rest_2_
  43.8 0.0 collective-permute-done.4.rest_1_
  43.8 0.0 copy-start.1
  43.9 0.0 copy-start.3
  43.9 6.0 %model.1 = (f32[8,64,2048]{2,1,0:T(8,128)S(1)}, f32[8,8,2048]{2,1,0:T(8,128)S(1)}, f32[64,128]{1,0:T(8,128)S(1)}) custom-call(s32[1]{0:T(128)} %bitcast.me_ref, f32[128,512]{1,0:T(8,128)S(1)} %constant_dynamic-update-slice_fusion.rest_5_.rest_0_, f32[128,512]{1,0:T(8,128)} %collective-permute-done.4.rest_1_, f32[128,512]{1,0:T(8,128)} %collective-permute-done.5.rest_2_, ...), custom_call_target="tpu_custom_call" | custom-call | tf_op jit(solution)/shard_map/model/pallas_call | solution.py:218
  49.9 12.3 %all_to_all.10.parts_ref = f32[8,8,2048]{2,1,0:T(8,128)S(1)} all-to-all(f32[8,8,2048]{2,1,0:T(8,128)S(1)} %get-tuple-element.28), channel_id=1, replica_groups=mesh['comp'=8,'row'=32] {'comp'}, dimensions={0} | all-to-all | bytes 1048576 | tf_op jit(solution)/shard_map/all_to_all | solution.py:333
  62.1 10.3 %scores.1 = f32[2,1024]{1,0:T(2,128)S(1)} custom-call(f32[8,8,2048]{2,1,0:T(8,128)S(1)} %all_to_all.10.parts_ref, f32[2,4,2048]{2,1,0:T(4,128)S(1)} %copy-done.1, f32[8,64,2048]{2,1,0:T(8,128)S(1)} %get-tuple-element.29.gain_ref, s32[1,1024]{1,0:T(1,128)S(1)} %bitcast.6, f32[64,128]{1,0:T(8,128)S(1)} %get-tuple-element.30.curv_ref, ...), custom_call_target="tpu_custom_call" | custom-call | tf_op jit(solution)/shard_map/scores/pallas_call | solution.py:273
  72.4 3.1 %collective-permute-start.7 = (f32[2,1024]{1,0:T(2,128)S(1)}, f32[2,1024]{1,0:T(2,128)S(1)}, u32[]{:S(2)}, u32[]{:S(2)}) collective-permute-start(f32[2,1024]{1,0:T(2,128)S(1)} %scores.1), channel_id=1, source_target_pairs={{0,1},{1,0},{2,3},{3,2},{4,5},{5,4},{6,7},{7,6},{8,9},{9,8},{10,11... | collective-permute-start | bytes 24584 | tf_op jit(solution)/shard_map/ppermute | solution.py:301
  75.6 0.8 collective-permute-done.7
  76.5 16.7 %all_to_all.11 = f32[16,2,1024]{2,1,0:T(2,128)S(1)} all-to-all(f32[16,2,1024]{2,1,0:T(2,128)S(1)} %broadcast_in_dim.18), channel_id=1, replica_groups={{0,2,4,6,8,10,12,14,16,18,20,22,24,26,28,30},{1,3,5,7,9,11,13,15,17,19,..., dimensions={0} | all-to-all | bytes 262144 | tf_op jit(solution)/shard_map/all_to_all | solution.py:336
  93.2 0.1 reduce_sum.9
  93.3 0.6 add.11
  (17 shorter events, 0.1 us)
Async XLA Ops:
  0.8 4.1 %collective-permute-start = (f32[16,512]{1,0:T(8,128)S(1)}, f32[16,512]{1,0:T(8,128)S(1)}, u32[]{:S(2)}, u32[]{:S(2)}) collective-permute-start(f32[16,512]{1,0:T(8,128)S(1)} %get-tuple-element.32), channel_id=1, source_target_pairs={{0,1},{1,0},{2,3},{3,2},{4,5},{5,4},{6,7},{7,6},{8,9},{9,8},{10,11... | collective-permute-start | bytes 98312 | tf_op jit(solution)/shard_map/ppermute | solution.py:301
  4.9 7.2 %collective-permute-start.3 = (f32[32,512]{1,0:T(8,128)S(1)}, f32[32,512]{1,0:T(8,128)S(1)}, u32[]{:S(2)}, u32[]{:S(2)}) collective-permute-start(f32[32,512]{1,0:T(8,128)S(1)} %pad_maximum_fusion.rest_0_), channel_id=1, source_target_pairs={{0,24},{1,25},{2,26},{3,27},{4,28},{5,29},{6,30},{7,31},{8,0},{9,1... | collective-permute-start | bytes 196616 | tf_op jit(solution)/shard_map/ppermute | solution.py:301
  5.9 6.1 %collective-permute-start.2 = (f32[32,512]{1,0:T(8,128)S(1)}, f32[32,512]{1,0:T(8,128)S(1)}, u32[]{:S(2)}, u32[]{:S(2)}) collective-permute-start(f32[32,512]{1,0:T(8,128)S(1)} %pad_maximum_fusion.rest_0_), channel_id=1, source_target_pairs={{0,16},{1,17},{2,18},{3,19},{4,20},{5,21},{6,22},{7,23},{8,24},{9,... | collective-permute-start | bytes 196616 | tf_op jit(solution)/shard_map/ppermute | solution.py:301
  6.2 5.8 %collective-permute-start.1 = (f32[32,512]{1,0:T(8,128)S(1)}, f32[32,512]{1,0:T(8,128)S(1)}, u32[]{:S(2)}, u32[]{:S(2)}) collective-permute-start(f32[32,512]{1,0:T(8,128)S(1)} %pad_maximum_fusion.rest_0_), channel_id=1, source_target_pairs={{0,8},{1,9},{2,10},{3,11},{4,12},{5,13},{6,14},{7,15},{8,16},{9,17... | collective-permute-start | bytes 196616 | tf_op jit(solution)/shard_map/ppermute | solution.py:301
  12.1 31.7 %collective-permute-start.6 = (f32[128,512]{1,0:T(8,128)S(1)}, f32[128,512]{1,0:T(8,128)}, u32[]{:S(2)}, u32[]{:S(2)}) collective-permute-start(f32[128,512]{1,0:T(8,128)S(1)} %constant_dynamic-update-slice_fusion.rest_5_.rest_0_), channel_id=1, source_target_pairs={{0,6},{1,7},{2,0},{3,1},{4,2},{5,3},{6,4},{7,5},{8,14},{9,15},{10,... | collective-permute-start | bytes 786440 | tf_op jit(solution)/shard_map/ppermute | solution.py:301
  18.5 25.4 %collective-permute-start.5 = (f32[128,512]{1,0:T(8,128)S(1)}, f32[128,512]{1,0:T(8,128)}, u32[]{:S(2)}, u32[]{:S(2)}) collective-permute-start(f32[128,512]{1,0:T(8,128)S(1)} %constant_dynamic-update-slice_fusion.rest_5_.rest_0_), channel_id=1, source_target_pairs={{0,4},{1,5},{2,6},{3,7},{4,0},{5,1},{6,2},{7,3},{8,12},{9,13},{10,... | collective-permute-start | bytes 786440 | tf_op jit(solution)/shard_map/ppermute | solution.py:301
  19.4 24.4 %collective-permute-start.4 = (f32[128,512]{1,0:T(8,128)S(1)}, f32[128,512]{1,0:T(8,128)}, u32[]{:S(2)}, u32[]{:S(2)}) collective-permute-start(f32[128,512]{1,0:T(8,128)S(1)} %constant_dynamic-update-slice_fusion.rest_5_.rest_0_), channel_id=1, source_target_pairs={{0,2},{1,3},{2,4},{3,5},{4,6},{5,7},{6,0},{7,1},{8,10},{9,11},{10,... | collective-permute-start | bytes 786440 | tf_op jit(solution)/shard_map/ppermute | solution.py:301
  21.7 0.8 copy-start
  22.5 0.7 copy-start.2
  23.2 0.7 copy-start.4
  23.8 0.7 copy-start.6
  34.2 9.6 %copy-start.7 = (s32[2,2048]{1,0:T(2,128)S(1)}, s32[2,2048]{1,0:T(2,128)}, u32[]{:S(2)}) copy-start(s32[2,2048]{1,0:T(2,128)} %rest_4_.1) | copy-start | bytes 49156
  43.8 18.3 %copy-start.1 = (f32[2,4,2048]{2,1,0:T(4,128)S(1)}, f32[2,4,2048]{2,1,0:T(4,128)}, u32[]{:S(2)}) copy-start(f32[2,4,2048]{2,1,0:T(4,128)} %obs_ref.1) | copy-start | bytes 196612
  43.9 18.3 %copy-start.3 = (s32[1024]{0:T(1024)S(1)}, s32[1024]{0:T(1024)}, u32[]{:S(2)}) copy-start(s32[1024]{0:T(1024)} %param.11) | copy-start | bytes 12292
  62.1 31.1 %copy-start.5 = (f32[1024]{0:T(1024)S(1)}, f32[1024]{0:T(1024)}, u32[]{:S(2)}) copy-start(f32[1024]{0:T(1024)} %param.10) | copy-start | bytes 12292
  72.4 4.0 %collective-permute-start.7 = (f32[2,1024]{1,0:T(2,128)S(1)}, f32[2,1024]{1,0:T(2,128)S(1)}, u32[]{:S(2)}, u32[]{:S(2)}) collective-permute-start(f32[2,1024]{1,0:T(2,128)S(1)} %scores.1), channel_id=1, source_target_pairs={{0,1},{1,0},{2,3},{3,2},{4,5},{5,4},{6,7},{7,6},{8,9},{9,8},{10,11... | collective-permute-start | bytes 24584 | tf_op jit(solution)/shard_map/ppermute | solution.py:301

commit v3 on v2

--- a/solution.py
+++ b/solution.py
@@ -75,45 +75,56 @@
     return (c8, c9, c10, c11, s8, s9, s10, s11)
 
 
-def table_kernel(first, count, sky_ref, flux_ref, clus_ref, uvw_ref, *rest):
-    *table_refs, pred_ref, left, hot, late = rest[-(sky_ref.shape[1] // CHUNK + 4) :]
+def table_kernel(first, count, me_ref, sky_ref, flux_ref, clus_ref, uvw_ref, pass_ref, *rest):
+    *table_refs, pred_ref, passed, place_ref, baseline, base, hot, late = rest[
+        -(sky_ref.shape[1] // CHUNK + 7) :
+    ]
+    passed[...] = pass_ref[0 : passed.shape[0], :]
     comps = sky_ref.shape[1]
-    chunks, tiles, pieces = comps // CHUNK, CHUNK // TILE, WIDE // CHUNK
+    chunks, tiles, pieces = comps // CHUNK, BLOCK // TILE, WIDE // BLOCK
 
     east, north = sky_ref[0:1, :], sky_ref[1:2, :]
     depth = jnp.sqrt(1.0 - east * east - north * north) - 1.0
     place = jnp.concatenate([east, north, depth], axis=0)
-    left[...] = jnp.transpose(stack_terms(left_terms(place))).astype(BF16)
+    place_ref[...] = stack_terms(left_terms(place)).astype(BF16)
     ids = lax.broadcasted_iota(jnp.int32, (C, comps), 0)
     hot[...] = jnp.where(ids == clus_ref[...], flux_ref[...], 0.0).astype(BF16)
     late[...] = jnp.zeros_like(late)
     last = chunks - 1
+    dims = (((1,), (1,)), ((), ()))
 
     def matmul(i, chunk, n):
-        at, to = pl.ds(chunk * CHUNK, CHUNK), pl.ds(n * CHUNK, CHUNK)
-        source = late[:, to] if chunk == last else table_refs[chunk][i, :, to]
-        part = jnp.dot(hot[:, at], source, preferred_element_type=F32)
+        at, to = pl.ds(chunk * CHUNK, CHUNK), pl.ds(n * BLOCK, BLOCK)
+        source = late[to, :] if chunk == last else table_refs[chunk][i, to, :]
+        part = lax.dot_general(hot[:, at], source, dims, preferred_element_type=F32)
         if chunk == 0:
             pred_ref[i, :, to] = part
         else:
             pred_ref[i, :, to] += part
 
+    def turn(i):
+        uvw = uvw_ref[:, pl.ds(pl.multiple_of((i + first) * BLOCK, BLOCK), BLOCK)]
+        baseline[...] = jnp.transpose(stack_terms(right_terms(uvw * 0.125))).astype(BF16)
+
+    def project(chunk):
+        base[chunk % 2] = jnp.dot(
+            baseline[...], place_ref[:, pl.ds(chunk * CHUNK, CHUNK)], preferred_element_type=F32
+        )
+
     def block(i, carry):
         before = jnp.maximum(i - 1, 0)
-        uvw = uvw_ref[:, pl.ds(pl.multiple_of((i + first) * BLOCK, BLOCK), BLOCK)]
-        right = stack_terms(right_terms(uvw * 0.125)).astype(BF16)
         for chunk in range(chunks):
-            base = jnp.dot(
-                left[pl.ds(chunk * CHUNK, CHUNK), :], right, preferred_element_type=F32
-            )
+            if chunk == last:
+                turn(jnp.minimum(i + 1, count - 1))
+            project((chunk + 1) % chunks)
             for tile in range(tiles):
-                values = phases(base[tile * TILE : (tile + 1) * TILE, :])
+                values = phases(base[chunk % 2, pl.ds(tile * TILE, TILE), :])
                 for j, value in enumerate(values):
                     value = value.astype(BF16)
-                    to = pl.ds(j * BLOCK, BLOCK)
-                    table_refs[chunk][i, pl.ds(tile * TILE, TILE), to] = value
+                    to = pl.ds(j * BLOCK + tile * TILE, TILE)
+                    table_refs[chunk][i, to, :] = value
                     if chunk == last:
-                        late[pl.ds(tile * TILE, TILE), to] = value
+                        late[to, :] = value
                 if tile % (tiles // pieces) == 0:
                     n = tile // (tiles // pieces)
                     if chunk:
@@ -123,6 +134,8 @@
         return carry
 
     pred_ref[0] = jnp.zeros(pred_ref.shape[1:], F32)
+    turn(0)
+    project(0)
     lax.fori_loop(0, count, block, 0)
     for n in range(pieces):
         matmul(count - 1, last, n)
@@ -132,24 +145,34 @@
     return pltpu.with_memory_space_constraint(x, pltpu.VMEM)
 
 
-def make_tables(first, count, sky, fluxes, clusters, uvw, after, held):
+def make_tables(first, count, me, sky, fluxes, clusters, uvw, after, passed, held):
     comps = sky.shape[1]
     vmem = pl.BlockSpec(memory_space=pltpu.VMEM)
     chunks = comps // CHUNK
     return pl.pallas_call(
         functools.partial(table_kernel, first, count),
-        in_specs=[vmem] * (4 + len(held)) + [pl.BlockSpec(memory_space=pl.ANY)] * len(after),
-        out_specs=[vmem] * (chunks + 1),
-        out_shape=[pltpu.VMEM((count, CHUNK, WIDE), BF16)] * chunks
-        + [pltpu.VMEM((count, C, WIDE), F32)],
+        in_specs=[pl.BlockSpec(memory_space=pltpu.SMEM)] + [vmem] * (5 + len(held)),
+        out_specs=[vmem] * (chunks + 2),
+        out_shape=[pltpu.VMEM((count, WIDE, CHUNK), BF16)] * chunks
+        + [
+            pltpu.VMEM((count, C, WIDE), F32),
+            jax.ShapeDtypeStruct((passed, after.shape[1]), F32),
+        ],
         scratch_shapes=[
-            pltpu.VMEM((comps, 32), BF16),
+            pltpu.VMEM((32, comps), BF16),
+            pltpu.VMEM((BLOCK, 32), BF16),
+            pltpu.VMEM((2, BLOCK, CHUNK), F32),
             pltpu.VMEM((C, comps), BF16),
-            pltpu.VMEM((CHUNK, WIDE), BF16),
+            pltpu.VMEM((WIDE, CHUNK), BF16),
         ],
         compiler_params=pltpu.CompilerParams(vmem_limit_bytes=SCOPED),
+        cost_estimate=pl.CostEstimate(
+            flops=2 * C * comps * count * WIDE,
+            bytes_accessed=2 * comps * count * WIDE,
+            transcendentals=4 * comps * count * WIDE,
+        ),
         name="tables",
-    )(sky, fluxes, clusters, uvw, *map(in_vmem, held), *after)
+    )(me, sky, fluxes, clusters, uvw, after, *map(in_vmem, held))
 
 
 def model_kernel(me_ref, *rest):
@@ -255,8 +278,8 @@
     scores = [jnp.zeros((C, CHUNK), F32)] * chunks
     for i, (group, own_i) in enumerate(blocks):
         for n in range(chunks):
-            scores[n] = scores[n] + lax.dot_general(
-                weight[i % 2], group[n][own_i], (((1,), (1,)), ((), ())), preferred_element_type=F32
+            scores[n] = scores[n] + jnp.dot(
+                weight[i % 2], group[n][own_i], preferred_element_type=F32
             )
         if i + 1 < len(blocks):
             weigh(i + 1)
@@ -311,24 +334,28 @@
 
     owned = station_gains + gain_step
     chip = jnp.concatenate([owned, permute(owned, other_core())], axis=0)
-    line = jnp.concatenate([chip] + [permute(chip, turn_y(k)) for k in (1, 2, 3)], axis=0)
-    pieces = [line] + [permute(line, turn_z(k)) for k in (1, 2, 3)]
-
-    after = ([chip], [line])
+    others = [permute(chip, turn_y(k)) for k in (1, 2, 3)]
     tables, preds = [], []
+    after, passed = chip, chip.shape[0]
     for n, count in enumerate(GROUPS):
-        *parts, pred = make_tables(
+        *parts, pred, after = make_tables(
             firsts[n],
             count,
+            me,
             sky_positions,
             flux_row,
             cluster_row,
             baseline_uvw,
-            after[n],
+            after,
+            passed,
             tables + preds,
         )
         tables += parts
         preds.append(pred)
+        if n == 0:
+            after = jnp.concatenate([after] + others, axis=0)
+            pieces = [after] + [permute(after, turn_z(k)) for k in (1, 2, 3)]
+            passed = 8
     gain, model, curv = make_model(me, pieces, stations, preds, tables, peers)
     parts = lax.all_to_all(model, "comp", 0, 0, tiled=True)
     sums = make_scores(parts, observed_vis, gain, cluster_row, curv, tables)

time: 94.3 us -> 99.1 us (1.051)
  blocking collectives: 29 us -> 37.6 us
  Pallas kernels: 35.5 us -> 33.3 us
  starting transfers between devices: 18 us -> 17 us
    all_to_all x1, blocking collectives: 12.3 us -> 18.6 us  [per_device(): parts = lax.all_to_all(model, 'comp', 0, 0, tiled=True)]
    pallas_call x1, Pallas kernels: 10.3 us -> 5.9 us  [make_scores(): pl.pallas_call(score_kernel, in_specs=[vmem] * (5 + len(tables)), out_spe...]
    pallas_call x2, Pallas kernels: 19.2 us -> 22.3 us  [make_tables(): pl.pallas_call(functools.partial(table_kernel, first, count), in_specs=[p...]
    all_to_all x1, blocking collectives: 16.7 us -> 19 us  [per_device(): lax.all_to_all(jnp.broadcast_to(sums[None], (16,) + sums.shape), 'row', 0...]
    ppermute x8, starting transfers between devices: 18 us -> 17 us  [permute(): return lax.ppermute(x, 'row', pairs)]
    unnamed x19 -> x23, local copies, waits for them, and re-layouts: 2.87 us -> 2.87 us
  transfers between devices with their start and end apart: 8 -> 8, of which waited for: 3 -> 4; matrix products, arithmetic and copies ran while one was open for 0% -> 0% of each run, Pallas kernels for 20% -> 23%
where the time goes in v3:
time: 99.1 us; the launch traced here: 98.7 us
  blocking collectives  37.6 us (38%)
  Pallas kernels  33.3 us (34%)
  starting transfers between devices  17 us (17%)
  waiting for transfers between devices  6.38 us (6%)
  local copies, waits for them, and re-layouts  2.91 us (3%)
  other arithmetic  1.46 us (1%)
    pallas_call x2, Pallas kernels, make_tables(): pl.pallas_call(functools.partial(table_kernel, first, count), in_specs=[p...  22.3 us
    all_to_all x1, blocking collectives, per_device(): lax.all_to_all(jnp.broadcast_to(sums[None], (16,) + sums.shape), 'row', 0...  19 us
    all_to_all x1, blocking collectives, per_device(): parts = lax.all_to_all(model, 'comp', 0, 0, tiled=True)  18.6 us
    ppermute x8, starting transfers between devices, permute(): return lax.ppermute(x, 'row', pairs)  17 us
    ppermute x8, waiting for transfers between devices, permute(): return lax.ppermute(x, 'row', pairs)  6.38 us
    pallas_call x1, Pallas kernels, make_scores(): pl.pallas_call(score_kernel, in_specs=[vmem] * (5 + len(tables)), out_spe...  5.9 us
    pallas_call x1, Pallas kernels, make_model(): pl.pallas_call(model_kernel, in_specs=[pl.BlockSpec(memory_space=pltpu.SM...  5.02 us
    unnamed x23, local copies, waits for them, and re-layouts  2.87 us
  transfers between devices with their start and end apart: 8, of which 4 were waited for; matrix products, arithmetic and copies ran while one was open for 0% of the time, Pallas kernels for 23%

profile of v3, /device:TPU:1, one launch (start us, length us, event | category | flops | bytes accessed | tf_op | source)
XLA Modules:
  0.0 98.7 jit_solution(1086384787033483927)
XLA Ops:
  0.0 0.8 add.9
  0.8 3.2 %collective-permute-start = (f32[16,512]{1,0:T(8,128)S(1)}, f32[16,512]{1,0:T(8,128)S(1)}, u32[]{:S(2)}, u32[]{:S(2)}) collective-permute-start(f32[16,512]{1,0:T(8,128)S(1)} %add.9), channel_id=1, source_target_pairs={{0,1},{1,0},{2,3},{3,2},{4,5},{5,4},{6,7},{7,6},{8,9},{9,8},{10,11... | collective-permute-start | bytes 98312 | tf_op jit(solution)/shard_map/ppermute | solution.py:324
  4.0 0.9 collective-permute-done
  4.9 1.0 %collective-permute-start.3 = (f32[32,512]{1,0:T(8,128)S(1)}, f32[32,512]{1,0:T(8,128)S(1)}, u32[]{:S(2)}, u32[]{:S(2)}) collective-permute-start(f32[32,512]{1,0:T(8,128)S(1)} %pad_maximum_fusion.pass_ref), channel_id=1, source_target_pairs={{0,24},{1,25},{2,26},{3,27},{4,28},{5,29},{6,30},{7,31},{8,0},{9,1... | collective-permute-start | bytes 196616 | tf_op jit(solution)/shard_map/ppermute | solution.py:324
  5.9 0.3 collective-permute-start.2
  6.2 0.7 collective-permute-start.1
  6.9 0.7 copy-done.2
  7.6 0.7 copy-done.4
  8.3 0.8 copy-done.6
  9.1 0.7 copy-done.8
  9.8 11.1 %tables.2 = (bf16[4,2048,256]{2,1,0:T(8,128)(2,1)S(1)}, bf16[4,2048,256]{2,1,0:T(8,128)(2,1)S(1)}, bf16[4,2048,256]{2,1,0:T(8,128)(2,1)S(1)}, bf16[4,2048,256]{2...) custom-call(s32[1]{0:T(128)} %bitcast.me_ref, f32[2,1024]{1,0:T(2,128)S(1)} %copy-done.8, ...), custom_call_target="tpu_custom_call" | custom-call | flops 1073741824 | bytes 16777216 | tf_op jit(solution)/shard_map/tables/pallas_call | solution.py:152
  20.8 0.0 collective-permute-done.1
  20.9 0.0 collective-permute-done.2
  20.9 0.0 collective-permute-done.3
  20.9 6.1 %collective-permute-start.6 = (f32[128,512]{1,0:T(8,128)S(1)}, f32[128,512]{1,0:T(8,128)S(1)}, u32[]{:S(2)}, u32[]{:S(2)}) collective-permute-start(f32[128,512]{1,0:T(8,128)S(1)} %constant_dynamic-update-slice_fusion.pass_ref.rest_0_), channel_id=1, source_target_pairs={{0,6},{1,7},{2,0},{3,1},{4,2},{5,3},{6,4},{7,5},{8,14},{9,15},{10,... | collective-permute-start | bytes 786440 | tf_op jit(solution)/shard_map/ppermute | solution.py:324
  27.0 1.0 %collective-permute-start.5 = (f32[128,512]{1,0:T(8,128)S(1)}, f32[128,512]{1,0:T(8,128)S(1)}, u32[]{:S(2)}, u32[]{:S(2)}) collective-permute-start(f32[128,512]{1,0:T(8,128)S(1)} %constant_dynamic-update-slice_fusion.pass_ref.rest_0_), channel_id=1, source_target_pairs={{0,4},{1,5},{2,6},{3,7},{4,0},{5,1},{6,2},{7,3},{8,12},{9,13},{10,... | collective-permute-start | bytes 786440 | tf_op jit(solution)/shard_map/ppermute | solution.py:324
  28.0 2.3 %collective-permute-start.4 = (f32[128,512]{1,0:T(8,128)S(1)}, f32[128,512]{1,0:T(8,128)S(1)}, u32[]{:S(2)}, u32[]{:S(2)}) collective-permute-start(f32[128,512]{1,0:T(8,128)S(1)} %constant_dynamic-update-slice_fusion.pass_ref.rest_0_), channel_id=1, source_target_pairs={{0,2},{1,3},{2,4},{3,5},{4,6},{5,7},{6,0},{7,1},{8,10},{9,11},{10,... | collective-permute-start | bytes 786440 | tf_op jit(solution)/shard_map/ppermute | solution.py:324
  30.3 0.0 copy-done.3
  30.3 0.0 copy-done.7
  30.3 0.0 copy-start.1
  30.3 11.3 %tables.3 = (bf16[4,2048,256]{2,1,0:T(8,128)(2,1)S(1)}, bf16[4,2048,256]{2,1,0:T(8,128)(2,1)S(1)}, bf16[4,2048,256]{2,1,0:T(8,128)(2,1)S(1)}, bf16[4,2048,256]{2...) custom-call(s32[1]{0:T(128)} %bitcast.me_ref, f32[2,1024]{1,0:T(2,128)S(1)} %copy-done.9, ...), custom_call_target="tpu_custom_call" | custom-call | flops 1073741824 | bytes 16777216 | tf_op jit(solution)/shard_map/tables/pallas_call | solution.py:152
  41.6 0.0 collective-permute-done.6.rest_3_
  41.6 1.7 %collective-permute-done.5.rest_2_ = f32[128,512]{1,0:T(8,128)S(1)} collective-permute-done((f32[128,512]{1,0:T(8,128)S(1)}, f32[128,512]{1,0:T(8,128)S(1)}, u32[]{:S(2)}, u32[]{:S(2)}) %collective-permute-start.5) | collective-permute-done | bytes 262176 | tf_op jit(solution)/shard_map/ppermute | solution.py:324
  43.2 3.0 %collective-permute-done.4.rest_1_ = f32[128,512]{1,0:T(8,128)S(1)} collective-permute-done((f32[128,512]{1,0:T(8,128)S(1)}, f32[128,512]{1,0:T(8,128)S(1)}, u32[]{:S(2)}, u32[]{:S(2)}) %collective-permute-start.4) | collective-permute-done | bytes 262176 | tf_op jit(solution)/shard_map/ppermute | solution.py:324
  46.3 5.0 %model.1 = (f32[8,64,2048]{2,1,0:T(8,128)S(1)}, f32[8,8,2048]{2,1,0:T(8,128)S(1)}, f32[64,128]{1,0:T(8,128)S(1)}) custom-call(s32[1]{0:T(128)} %bitcast.me_ref, f32[128,512]{1,0:T(8,128)S(1)} %constant_dynamic-update-slice_fusion.pass_ref.rest_0_, f32[128,512]{1,0:T(8,128)S(1)} %collective-permute-done.4.rest_1_, ...), custom_call_target="tpu_custom_call" | custom-call | tf_op jit(solution)/shard_map/model/pallas_call | solution.py:241
  51.3 18.6 %all_to_all.10.parts_ref = f32[8,8,2048]{2,1,0:T(8,128)S(1)} all-to-all(f32[8,8,2048]{2,1,0:T(8,128)S(1)} %get-tuple-element.30), channel_id=1, replica_groups=mesh['comp'=8,'row'=32] {'comp'}, dimensions={0} | all-to-all | bytes 1048576 | tf_op jit(solution)/shard_map/all_to_all | solution.py:360
  69.9 5.9 %scores.1 = f32[2,1024]{1,0:T(2,128)S(1)} custom-call(f32[8,8,2048]{2,1,0:T(8,128)S(1)} %all_to_all.10.parts_ref, f32[2,4,2048]{2,1,0:T(4,128)S(1)} %copy-done, f32[8,64,2048]{2,1,0:T(8,128)S(1)} %get-tuple-element.31.gain_ref, s32[1,1024]{1,0:T(1,128)S(1)} %bitcast.6, f32[64,128]{1,0:T(8,128)S(1)} %get-tuple-element.32.curv_ref, ...), custom_call_target="tpu_custom_call" | custom-call | tf_op jit(solution)/shard_map/scores/pallas_call | solution.py:296
  75.8 2.3 %collective-permute-start.7 = (f32[2,1024]{1,0:T(2,128)S(1)}, f32[2,1024]{1,0:T(2,128)S(1)}, u32[]{:S(2)}, u32[]{:S(2)}) collective-permute-start(f32[2,1024]{1,0:T(2,128)S(1)} %scores.1), channel_id=1, source_target_pairs={{0,1},{1,0},{2,3},{3,2},{4,5},{5,4},{6,7},{7,6},{8,9},{9,8},{10,11... | collective-permute-start | bytes 24584 | tf_op jit(solution)/shard_map/ppermute | solution.py:324
  78.2 0.8 collective-permute-done.7
  79.0 19.0 %all_to_all.11 = f32[16,2,1024]{2,1,0:T(2,128)S(1)} all-to-all(f32[16,2,1024]{2,1,0:T(2,128)S(1)} %broadcast_in_dim.18), channel_id=1, replica_groups={{0,2,4,6,8,10,12,14,16,18,20,22,24,26,28,30},{1,3,5,7,9,11,13,15,17,19,..., dimensions={0} | all-to-all | bytes 262144 | tf_op jit(solution)/shard_map/all_to_all | solution.py:363
  98.0 0.1 reduce_sum.9
  98.1 0.6 add.11
  (21 shorter events, 0.1 us)
Async XLA Ops:
  0.8 4.1 %collective-permute-start = (f32[16,512]{1,0:T(8,128)S(1)}, f32[16,512]{1,0:T(8,128)S(1)}, u32[]{:S(2)}, u32[]{:S(2)}) collective-permute-start(f32[16,512]{1,0:T(8,128)S(1)} %add.9), channel_id=1, source_target_pairs={{0,1},{1,0},{2,3},{3,2},{4,5},{5,4},{6,7},{7,6},{8,9},{9,8},{10,11... | collective-permute-start | bytes 98312 | tf_op jit(solution)/shard_map/ppermute | solution.py:324
  4.9 16.0 %collective-permute-start.3 = (f32[32,512]{1,0:T(8,128)S(1)}, f32[32,512]{1,0:T(8,128)S(1)}, u32[]{:S(2)}, u32[]{:S(2)}) collective-permute-start(f32[32,512]{1,0:T(8,128)S(1)} %pad_maximum_fusion.pass_ref), channel_id=1, source_target_pairs={{0,24},{1,25},{2,26},{3,27},{4,28},{5,29},{6,30},{7,31},{8,0},{9,1... | collective-permute-start | bytes 196616 | tf_op jit(solution)/shard_map/ppermute | solution.py:324
  5.9 15.0 %collective-permute-start.2 = (f32[32,512]{1,0:T(8,128)S(1)}, f32[32,512]{1,0:T(8,128)S(1)}, u32[]{:S(2)}, u32[]{:S(2)}) collective-permute-start(f32[32,512]{1,0:T(8,128)S(1)} %pad_maximum_fusion.pass_ref), channel_id=1, source_target_pairs={{0,16},{1,17},{2,18},{3,19},{4,20},{5,21},{6,22},{7,23},{8,24},{9,... | collective-permute-start | bytes 196616 | tf_op jit(solution)/shard_map/ppermute | solution.py:324
  6.2 14.6 %collective-permute-start.1 = (f32[32,512]{1,0:T(8,128)S(1)}, f32[32,512]{1,0:T(8,128)S(1)}, u32[]{:S(2)}, u32[]{:S(2)}) collective-permute-start(f32[32,512]{1,0:T(8,128)S(1)} %pad_maximum_fusion.pass_ref), channel_id=1, source_target_pairs={{0,8},{1,9},{2,10},{3,11},{4,12},{5,13},{6,14},{7,15},{8,16},{9,17... | collective-permute-start | bytes 196616 | tf_op jit(solution)/shard_map/ppermute | solution.py:324
  6.9 0.7 copy-start.2
  7.6 0.7 copy-start.4
  8.3 0.8 copy-start.6
  9.1 0.7 copy-start.8
  9.8 20.5 %copy-start.3 = (s32[1024]{0:T(1024)S(1)}, s32[1024]{0:T(1024)}, u32[]{:S(2)}) copy-start(s32[1024]{0:T(1024)} %param.11) | copy-start | bytes 12292
  9.8 20.5 %copy-start.5 = (f32[1024]{0:T(1024)S(1)}, f32[1024]{0:T(1024)}, u32[]{:S(2)}) copy-start(f32[1024]{0:T(1024)} %param.10) | copy-start | bytes 12292
  9.8 20.5 %copy-start.7 = (f32[3,2048]{1,0:T(4,128)S(1)}, f32[3,2048]{1,0:T(4,128)}, u32[]{:S(2)}) copy-start(f32[3,2048]{1,0:T(4,128)} %uvw_ref.3) | copy-start | bytes 73732
  9.8 20.5 %copy-start.9 = (f32[2,1024]{1,0:T(2,128)S(1)}, f32[2,1024]{1,0:T(2,128)}, u32[]{:S(2)}) copy-start(f32[2,1024]{1,0:T(2,128)} %sky_ref.3) | copy-start | bytes 24580
  20.9 20.6 %collective-permute-start.6 = (f32[128,512]{1,0:T(8,128)S(1)}, f32[128,512]{1,0:T(8,128)S(1)}, u32[]{:S(2)}, u32[]{:S(2)}) collective-permute-start(f32[128,512]{1,0:T(8,128)S(1)} %constant_dynamic-update-slice_fusion.pass_ref.rest_0_), channel_id=1, source_target_pairs={{0,6},{1,7},{2,0},{3,1},{4,2},{5,3},{6,4},{7,5},{8,14},{9,15},{10,... | collective-permute-start | bytes 786440 | tf_op jit(solution)/shard_map/ppermute | solution.py:324
  27.0 16.2 %collective-permute-start.5 = (f32[128,512]{1,0:T(8,128)S(1)}, f32[128,512]{1,0:T(8,128)S(1)}, u32[]{:S(2)}, u32[]{:S(2)}) collective-permute-start(f32[128,512]{1,0:T(8,128)S(1)} %constant_dynamic-update-slice_fusion.pass_ref.rest_0_), channel_id=1, source_target_pairs={{0,4},{1,5},{2,6},{3,7},{4,0},{5,1},{6,2},{7,3},{8,12},{9,13},{10,... | collective-permute-start | bytes 786440 | tf_op jit(solution)/shard_map/ppermute | solution.py:324
  28.0 18.2 %collective-permute-start.4 = (f32[128,512]{1,0:T(8,128)S(1)}, f32[128,512]{1,0:T(8,128)S(1)}, u32[]{:S(2)}, u32[]{:S(2)}) collective-permute-start(f32[128,512]{1,0:T(8,128)S(1)} %constant_dynamic-update-slice_fusion.pass_ref.rest_0_), channel_id=1, source_target_pairs={{0,2},{1,3},{2,4},{3,5},{4,6},{5,7},{6,0},{7,1},{8,10},{9,11},{10,... | collective-permute-start | bytes 786440 | tf_op jit(solution)/shard_map/ppermute | solution.py:324
  30.3 16.0 %copy-start.1 = (s32[2,2048]{1,0:T(2,128)S(1)}, s32[2,2048]{1,0:T(2,128)}, u32[]{:S(2)}) copy-start(s32[2,2048]{1,0:T(2,128)} %rest_4_.1) | copy-start | bytes 49156
  46.3 23.7 %copy-start = (f32[2,4,2048]{2,1,0:T(4,128)S(1)}, f32[2,4,2048]{2,1,0:T(4,128)}, u32[]{:S(2)}) copy-start(f32[2,4,2048]{2,1,0:T(4,128)} %obs_ref.1) | copy-start | bytes 196612
  75.8 3.2 %collective-permute-start.7 = (f32[2,1024]{1,0:T(2,128)S(1)}, f32[2,1024]{1,0:T(2,128)S(1)}, u32[]{:S(2)}, u32[]{:S(2)}) collective-permute-start(f32[2,1024]{1,0:T(2,128)S(1)} %scores.1), channel_id=1, source_target_pairs={{0,1},{1,0},{2,3},{3,2},{4,5},{5,4},{6,7},{7,6},{8,9},{9,8},{10,11... | collective-permute-start | bytes 24584 | tf_op jit(solution)/shard_map/ppermute | solution.py:324

commit v4 on v3

--- a/solution.py
+++ b/solution.py
@@ -76,10 +76,8 @@
 
 
 def table_kernel(first, count, me_ref, sky_ref, flux_ref, clus_ref, uvw_ref, pass_ref, *rest):
-    *table_refs, pred_ref, passed, place_ref, baseline, base, hot, late = rest[
-        -(sky_ref.shape[1] // CHUNK + 7) :
-    ]
-    passed[...] = pass_ref[0 : passed.shape[0], :]
+    *table_refs, pred_ref, passed, place_ref, hot = rest[-(sky_ref.shape[1] // CHUNK + 4) :]
+    passed[...] = pass_ref[...]
     comps = sky_ref.shape[1]
     chunks, tiles, pieces = comps // CHUNK, BLOCK // TILE, WIDE // BLOCK
 
@@ -89,63 +87,45 @@
     place_ref[...] = stack_terms(left_terms(place)).astype(BF16)
     ids = lax.broadcasted_iota(jnp.int32, (C, comps), 0)
     hot[...] = jnp.where(ids == clus_ref[...], flux_ref[...], 0.0).astype(BF16)
-    late[...] = jnp.zeros_like(late)
-    last = chunks - 1
     dims = (((1,), (1,)), ((), ()))
 
-    def matmul(i, chunk, n):
-        at, to = pl.ds(chunk * CHUNK, CHUNK), pl.ds(n * BLOCK, BLOCK)
-        source = late[to, :] if chunk == last else table_refs[chunk][i, to, :]
-        part = lax.dot_general(hot[:, at], source, dims, preferred_element_type=F32)
-        if chunk == 0:
-            pred_ref[i, :, to] = part
-        else:
-            pred_ref[i, :, to] += part
-
-    def turn(i):
-        uvw = uvw_ref[:, pl.ds(pl.multiple_of((i + first) * BLOCK, BLOCK), BLOCK)]
-        baseline[...] = jnp.transpose(stack_terms(right_terms(uvw * 0.125))).astype(BF16)
-
-    def project(chunk):
-        base[chunk % 2] = jnp.dot(
-            baseline[...], place_ref[:, pl.ds(chunk * CHUNK, CHUNK)], preferred_element_type=F32
-        )
-
-    def block(i, carry):
-        before = jnp.maximum(i - 1, 0)
+    def matmul(i, n):
+        to = pl.ds(n * BLOCK, BLOCK)
+        part = jnp.zeros((C, BLOCK), F32)
         for chunk in range(chunks):
-            if chunk == last:
-                turn(jnp.minimum(i + 1, count - 1))
-            project((chunk + 1) % chunks)
+            part = part + lax.dot_general(
+                hot[:, pl.ds(chunk * CHUNK, CHUNK)],
+                table_refs[chunk][i, to, :],
+                dims,
+                preferred_element_type=F32,
+            )
+        pred_ref[i, :, to] = part
+
+    for i in range(count):
+        uvw = uvw_ref[:, pl.ds((i + first) * BLOCK, BLOCK)]
+        baseline = jnp.transpose(stack_terms(right_terms(uvw * 0.125))).astype(BF16)
+        for chunk in range(chunks):
+            base = jnp.dot(
+                baseline, place_ref[:, pl.ds(chunk * CHUNK, CHUNK)], preferred_element_type=F32
+            )
             for tile in range(tiles):
-                values = phases(base[chunk % 2, pl.ds(tile * TILE, TILE), :])
+                values = phases(base[tile * TILE : (tile + 1) * TILE, :])
                 for j, value in enumerate(values):
-                    value = value.astype(BF16)
                     to = pl.ds(j * BLOCK + tile * TILE, TILE)
-                    table_refs[chunk][i, to, :] = value
-                    if chunk == last:
-                        late[to, :] = value
-                if tile % (tiles // pieces) == 0:
-                    n = tile // (tiles // pieces)
-                    if chunk:
-                        matmul(i, chunk - 1, n)
-                    else:
-                        matmul(before, last, n)
-        return carry
-
-    pred_ref[0] = jnp.zeros(pred_ref.shape[1:], F32)
-    turn(0)
-    project(0)
-    lax.fori_loop(0, count, block, 0)
+                    table_refs[chunk][i, to, :] = value.astype(BF16)
+                done = chunk * tiles + tile
+                each = chunks * tiles // pieces
+                if i and done % each == each - 1:
+                    matmul(i - 1, done // each)
     for n in range(pieces):
-        matmul(count - 1, last, n)
+        matmul(count - 1, n)
 
 
 def in_vmem(x):
     return pltpu.with_memory_space_constraint(x, pltpu.VMEM)
 
 
-def make_tables(first, count, me, sky, fluxes, clusters, uvw, after, passed, held):
+def make_tables(first, count, me, sky, fluxes, clusters, uvw, after, held):
     comps = sky.shape[1]
     vmem = pl.BlockSpec(memory_space=pltpu.VMEM)
     chunks = comps // CHUNK
@@ -156,14 +136,11 @@
         out_shape=[pltpu.VMEM((count, WIDE, CHUNK), BF16)] * chunks
         + [
             pltpu.VMEM((count, C, WIDE), F32),
-            jax.ShapeDtypeStruct((passed, after.shape[1]), F32),
+            jax.ShapeDtypeStruct(after.shape, F32),
         ],
         scratch_shapes=[
             pltpu.VMEM((32, comps), BF16),
-            pltpu.VMEM((BLOCK, 32), BF16),
-            pltpu.VMEM((2, BLOCK, CHUNK), F32),
             pltpu.VMEM((C, comps), BF16),
-            pltpu.VMEM((WIDE, CHUNK), BF16),
         ],
         compiler_params=pltpu.CompilerParams(vmem_limit_bytes=SCOPED),
         cost_estimate=pl.CostEstimate(
@@ -176,9 +153,9 @@
 
 
 def model_kernel(me_ref, *rest):
-    pieces, pair_ref, preds = rest[:4], rest[4], rest[5 : 5 + len(GROUPS)]
+    pieces, pair_ref, preds = rest[:2], rest[2], rest[3 : 3 + len(GROUPS)]
     gain_ref, model_ref, curv_ref, table, found = rest[-5:]
-    owned = pieces[0].shape[0] // 8
+    owned = pieces[0].shape[0] // 16
     for n, piece in enumerate(pieces):
         flat = jnp.transpose(piece[...])
         high = flat.astype(BF16)
@@ -194,7 +171,7 @@
     pair = pair_ref[...]
     owner, own = pair // owned, pair % owned
     y, z, core = owner >> 3, (owner >> 1) & 3, owner & 1
-    slot = ((((my_z - z) & 3) * 4 + ((my_y - y) & 3)) * 2 + (core ^ my_core)) * owned + own
+    slot = (((core ^ my_core) * 4 + ((my_y - y) & 3)) * 4 + ((my_z - z) & 3)) * owned + own
 
     def gather(i):
         for side in range(2):
@@ -240,7 +217,7 @@
     vmem = pl.BlockSpec(memory_space=pltpu.VMEM)
     return pl.pallas_call(
         model_kernel,
-        in_specs=[pl.BlockSpec(memory_space=pltpu.SMEM)] + [vmem] * (5 + len(preds) + len(held)),
+        in_specs=[pl.BlockSpec(memory_space=pltpu.SMEM)] + [vmem] * (3 + len(preds) + len(held)),
         out_specs=[vmem] * 3,
         out_shape=[
             pltpu.VMEM((count, C, WIDE), F32),
@@ -248,7 +225,7 @@
             jax.ShapeDtypeStruct((C, 128), F32),
         ],
         scratch_shapes=[
-            pltpu.VMEM((2 * columns, 4 * rows), BF16),
+            pltpu.VMEM((2 * columns, 2 * rows), BF16),
             pltpu.VMEM((2, 2, columns, BLOCK), F32),
         ],
         compiler_params=pltpu.CompilerParams(vmem_limit_bytes=SCOPED),
@@ -333,10 +310,9 @@
     firsts = [sum(GROUPS[:n]) for n in range(len(GROUPS))]
 
     owned = station_gains + gain_step
-    chip = jnp.concatenate([owned, permute(owned, other_core())], axis=0)
-    others = [permute(chip, turn_y(k)) for k in (1, 2, 3)]
+    others = [permute(owned, turn_z(k)) for k in (1, 2, 3)]
     tables, preds = [], []
-    after, passed = chip, chip.shape[0]
+    after = owned
     for n, count in enumerate(GROUPS):
         *parts, pred, after = make_tables(
             firsts[n],
@@ -347,15 +323,15 @@
             cluster_row,
             baseline_uvw,
             after,
-            passed,
             tables + preds,
         )
         tables += parts
         preds.append(pred)
         if n == 0:
             after = jnp.concatenate([after] + others, axis=0)
-            pieces = [after] + [permute(after, turn_z(k)) for k in (1, 2, 3)]
-            passed = 8
+            others = [permute(after, turn_y(k)) for k in (1, 2, 3)]
+    plane = jnp.concatenate([after] + others, axis=0)
+    pieces = [plane, permute(plane, other_core())]
     gain, model, curv = make_model(me, pieces, stations, preds, tables, peers)
     parts = lax.all_to_all(model, "comp", 0, 0, tiled=True)
     sums = make_scores(parts, observed_vis, gain, cluster_row, curv, tables)

time: 99.1 us -> 84.5 us (0.85)
  blocking collectives: 37.6 us -> 29.2 us
  waiting for transfers between devices: 6.38 us -> 2.38 us
  Pallas kernels: 33.3 us -> 29.4 us
  starting transfers between devices: 17 us -> 18.5 us
    all_to_all x1, blocking collectives: 18.6 us -> 13.5 us  [per_device(): parts = lax.all_to_all(model, 'comp', 0, 0, tiled=True)]
    ppermute x8, waiting for transfers between devices: 6.38 us -> 2.38 us  [permute(): return lax.ppermute(x, 'row', pairs)]
    pallas_call x2, Pallas kernels: 22.3 us -> 18.5 us  [make_tables(): pl.pallas_call(functools.partial(table_kernel, first, count), in_specs=[p...]
    all_to_all x1, blocking collectives: 19 us -> 15.7 us  [per_device(): lax.all_to_all(jnp.broadcast_to(sums[None], (16,) + sums.shape), 'row', 0...]
    ppermute x8, starting transfers between devices: 17 us -> 18.5 us  [permute(): return lax.ppermute(x, 'row', pairs)]
    unnamed x23 -> x26, local copies, waits for them, and re-layouts: 2.87 us -> 2.9 us
  transfers between devices with their start and end apart: 8 -> 8, of which waited for: 4 -> 2; matrix products, arithmetic and copies ran while one was open for 0% -> 0% of each run, Pallas kernels for 23% -> 22%
where the time goes in v4:
time: 84.5 us; the launch traced here: 84.1 us
  Pallas kernels  29.4 us (35%)
  blocking collectives  29.2 us (35%)
  starting transfers between devices  18.5 us (22%)
  local copies, waits for them, and re-layouts  2.96 us (4%)
  waiting for transfers between devices  2.38 us (3%)
  other arithmetic  1.45 us (2%)
    ppermute x8, starting transfers between devices, permute(): return lax.ppermute(x, 'row', pairs)  18.5 us
    pallas_call x2, Pallas kernels, make_tables(): pl.pallas_call(functools.partial(table_kernel, first, count), in_specs=[p...  18.5 us
    all_to_all x1, blocking collectives, per_device(): lax.all_to_all(jnp.broadcast_to(sums[None], (16,) + sums.shape), 'row', 0...  15.7 us
    all_to_all x1, blocking collectives, per_device(): parts = lax.all_to_all(model, 'comp', 0, 0, tiled=True)  13.5 us
    pallas_call x1, Pallas kernels, make_scores(): pl.pallas_call(score_kernel, in_specs=[vmem] * (5 + len(tables)), out_spe...  5.91 us
    pallas_call x1, Pallas kernels, make_model(): pl.pallas_call(model_kernel, in_specs=[pl.BlockSpec(memory_space=pltpu.SM...  4.99 us
    unnamed x26, local copies, waits for them, and re-layouts  2.9 us
    ppermute x8, waiting for transfers between devices, permute(): return lax.ppermute(x, 'row', pairs)  2.38 us
  transfers between devices with their start and end apart: 8, of which 2 were waited for; matrix products, arithmetic and copies ran while one was open for 0% of the time, Pallas kernels for 22%

profile of v4, /device:TPU:1, one launch (start us, length us, event | category | flops | bytes accessed | tf_op | source)
XLA Modules:
  0.0 84.1 jit_solution(296166425678506643)
XLA Ops:
  0.0 0.8 add.9.pass_ref
  0.8 6.8 %collective-permute-start.2 = (f32[16,512]{1,0:T(8,128)S(1)}, f32[16,512]{1,0:T(8,128)S(1)}, u32[]{:S(2)}, u32[]{:S(2)}) collective-permute-start(f32[16,512]{1,0:T(8,128)S(1)} %add.9.pass_ref), channel_id=1, source_target_pairs={{0,6},{1,7},{2,0},{3,1},{4,2},{5,3},{6,4},{7,5},{8,14},{9,15},{10,... | collective-permute-start | bytes 98312 | tf_op jit(solution)/shard_map/ppermute | solution.py:301
  7.6 1.0 %collective-permute-start.1 = (f32[16,512]{1,0:T(8,128)S(1)}, f32[16,512]{1,0:T(8,128)S(1)}, u32[]{:S(2)}, u32[]{:S(2)}) collective-permute-start(f32[16,512]{1,0:T(8,128)S(1)} %add.9.pass_ref), channel_id=1, source_target_pairs={{0,4},{1,5},{2,6},{3,7},{4,0},{5,1},{6,2},{7,3},{8,12},{9,13},{10,... | collective-permute-start | bytes 98312 | tf_op jit(solution)/shard_map/ppermute | solution.py:301
  8.6 2.3 %collective-permute-start = (f32[16,512]{1,0:T(8,128)S(1)}, f32[16,512]{1,0:T(8,128)S(1)}, u32[]{:S(2)}, u32[]{:S(2)}) collective-permute-start(f32[16,512]{1,0:T(8,128)S(1)} %add.9.pass_ref), channel_id=1, source_target_pairs={{0,2},{1,3},{2,4},{3,5},{4,6},{5,7},{6,0},{7,1},{8,10},{9,11},{10,... | collective-permute-start | bytes 98312 | tf_op jit(solution)/shard_map/ppermute | solution.py:301
  10.9 0.7 copy-done.2
  11.6 0.7 copy-done.4
  12.3 0.8 copy-done.6
  13.0 0.7 copy-done.8
  13.7 9.3 %tables.2 = (bf16[4,2048,256]{2,1,0:T(8,128)(2,1)S(1)}, bf16[4,2048,256]{2,1,0:T(8,128)(2,1)S(1)}, bf16[4,2048,256]{2,1,0:T(8,128)(2,1)S(1)}, bf16[4,2048,256]{2...) custom-call(s32[1]{0:T(128)} %bitcast.me_ref, f32[2,1024]{1,0:T(2,128)S(1)} %copy-done.8, ...), custom_call_target="tpu_custom_call" | custom-call | flops 1073741824 | bytes 16777216 | tf_op jit(solution)/shard_map/tables/pallas_call | solution.py:132
  23.0 0.0 collective-permute-done
  23.0 0.0 collective-permute-done.1
  23.0 0.0 collective-permute-done.2
  23.1 2.8 %collective-permute-start.5 = (f32[64,512]{1,0:T(8,128)S(1)}, f32[64,512]{1,0:T(8,128)S(1)}, u32[]{:S(2)}, u32[]{:S(2)}) collective-permute-start(f32[64,512]{1,0:T(8,128)S(1)} %constant_dynamic-update-slice_fusion.pass_ref), channel_id=1, source_target_pairs={{0,24},{1,25},{2,26},{3,27},{4,28},{5,29},{6,30},{7,31},{8,0},{9,1... | collective-permute-start | bytes 393224 | tf_op jit(solution)/shard_map/ppermute | solution.py:301
  25.9 0.3 collective-permute-start.4
  26.2 0.7 collective-permute-start.3
  26.9 0.0 copy-done.5
  26.9 0.0 copy-done.9
  26.9 0.0 copy-start.1
  27.0 9.3 %tables.3 = (bf16[4,2048,256]{2,1,0:T(8,128)(2,1)S(1)}, bf16[4,2048,256]{2,1,0:T(8,128)(2,1)S(1)}, bf16[4,2048,256]{2,1,0:T(8,128)(2,1)S(1)}, bf16[4,2048,256]{2...) custom-call(s32[1]{0:T(128)} %bitcast.me_ref, f32[2,1024]{1,0:T(2,128)S(1)} %copy-done.9, ...), custom_call_target="tpu_custom_call" | custom-call | flops 1073741824 | bytes 16777216 | tf_op jit(solution)/shard_map/tables/pallas_call | solution.py:132
  36.2 0.0 collective-permute-done.3
  36.3 0.0 collective-permute-done.4
  36.3 0.0 collective-permute-done.5
  36.3 2.7 %collective-permute-start.6 = (f32[256,512]{1,0:T(8,128)S(1)}, f32[256,512]{1,0:T(8,128)S(1)}, u32[]{:S(2)}, u32[]{:S(2)}) collective-permute-start(f32[256,512]{1,0:T(8,128)S(1)} %constant_dynamic-update-slice_fusion.4.rest_0_), channel_id=1, source_target_pairs={{0,1},{1,0},{2,3},{3,2},{4,5},{5,4},{6,7},{7,6},{8,9},{9,8},{10,11... | collective-permute-start | bytes 1572872 | tf_op jit(solution)/shard_map/ppermute | solution.py:301
  39.0 1.5 %collective-permute-done.6.rest_1_ = f32[256,512]{1,0:T(8,128)S(1)} collective-permute-done((f32[256,512]{1,0:T(8,128)S(1)}, f32[256,512]{1,0:T(8,128)S(1)}, u32[]{:S(2)}, u32[]{:S(2)}) %collective-permute-start.6) | collective-permute-done | bytes 524320 | tf_op jit(solution)/shard_map/ppermute | solution.py:301
  40.5 5.0 %model.1 = (f32[8,64,2048]{2,1,0:T(8,128)S(1)}, f32[8,8,2048]{2,1,0:T(8,128)S(1)}, f32[64,128]{1,0:T(8,128)S(1)}) custom-call(s32[1]{0:T(128)} %bitcast.me_ref, f32[256,512]{1,0:T(8,128)S(1)} %constant_dynamic-update-slice_fusion.4.rest_0_, f32[256,512]{1,0:T(8,128)S(1)} %collective-permute-done.6.rest_1_, s32[2,2048]{1,0:T(2,128)S(1)} %copy-done.1, ...), custom_call_target="tpu_custom_call" | custom-call | tf_op jit(solution)/shard_map/model/pallas_call | solution.py:218
  45.5 13.5 %all_to_all.10.parts_ref = f32[8,8,2048]{2,1,0:T(8,128)S(1)} all-to-all(f32[8,8,2048]{2,1,0:T(8,128)S(1)} %get-tuple-element.32), channel_id=1, replica_groups=mesh['comp'=8,'row'=32] {'comp'}, dimensions={0} | all-to-all | bytes 1048576 | tf_op jit(solution)/shard_map/all_to_all | solution.py:336
  59.0 5.9 %scores.1 = f32[2,1024]{1,0:T(2,128)S(1)} custom-call(f32[8,8,2048]{2,1,0:T(8,128)S(1)} %all_to_all.10.parts_ref, f32[2,4,2048]{2,1,0:T(4,128)S(1)} %copy-done, f32[8,64,2048]{2,1,0:T(8,128)S(1)} %get-tuple-element.33.gain_ref, s32[1,1024]{1,0:T(1,128)S(1)} %bitcast.6, f32[64,128]{1,0:T(8,128)S(1)} %get-tuple-element.34.curv_ref, ...), custom_call_target="tpu_custom_call" | custom-call | tf_op jit(solution)/shard_map/scores/pallas_call | solution.py:273
  64.9 1.9 %collective-permute-start.7 = (f32[2,1024]{1,0:T(2,128)S(1)}, f32[2,1024]{1,0:T(2,128)S(1)}, u32[]{:S(2)}, u32[]{:S(2)}) collective-permute-start(f32[2,1024]{1,0:T(2,128)S(1)} %scores.1), channel_id=1, source_target_pairs={{0,1},{1,0},{2,3},{3,2},{4,5},{5,4},{6,7},{7,6},{8,9},{9,8},{10,11... | collective-permute-start | bytes 24584 | tf_op jit(solution)/shard_map/ppermute | solution.py:301
  66.8 0.8 collective-permute-done.7
  67.7 15.7 %all_to_all.11 = f32[16,2,1024]{2,1,0:T(2,128)S(1)} all-to-all(f32[16,2,1024]{2,1,0:T(2,128)S(1)} %broadcast_in_dim.18), channel_id=1, replica_groups={{0,2,4,6,8,10,12,14,16,18,20,22,24,26,28,30},{1,3,5,7,9,11,13,15,17,19,..., dimensions={0} | all-to-all | bytes 262144 | tf_op jit(solution)/shard_map/all_to_all | solution.py:339
  83.4 0.1 reduce_sum.9
  83.5 0.6 add.11
  (24 shorter events, 0.1 us)
Async XLA Ops:
  0.8 22.3 %collective-permute-start.2 = (f32[16,512]{1,0:T(8,128)S(1)}, f32[16,512]{1,0:T(8,128)S(1)}, u32[]{:S(2)}, u32[]{:S(2)}) collective-permute-start(f32[16,512]{1,0:T(8,128)S(1)} %add.9.pass_ref), channel_id=1, source_target_pairs={{0,6},{1,7},{2,0},{3,1},{4,2},{5,3},{6,4},{7,5},{8,14},{9,15},{10,... | collective-permute-start | bytes 98312 | tf_op jit(solution)/shard_map/ppermute | solution.py:301
  7.6 15.4 %collective-permute-start.1 = (f32[16,512]{1,0:T(8,128)S(1)}, f32[16,512]{1,0:T(8,128)S(1)}, u32[]{:S(2)}, u32[]{:S(2)}) collective-permute-start(f32[16,512]{1,0:T(8,128)S(1)} %add.9.pass_ref), channel_id=1, source_target_pairs={{0,4},{1,5},{2,6},{3,7},{4,0},{5,1},{6,2},{7,3},{8,12},{9,13},{10,... | collective-permute-start | bytes 98312 | tf_op jit(solution)/shard_map/ppermute | solution.py:301
  8.6 14.4 %collective-permute-start = (f32[16,512]{1,0:T(8,128)S(1)}, f32[16,512]{1,0:T(8,128)S(1)}, u32[]{:S(2)}, u32[]{:S(2)}) collective-permute-start(f32[16,512]{1,0:T(8,128)S(1)} %add.9.pass_ref), channel_id=1, source_target_pairs={{0,2},{1,3},{2,4},{3,5},{4,6},{5,7},{6,0},{7,1},{8,10},{9,11},{10,... | collective-permute-start | bytes 98312 | tf_op jit(solution)/shard_map/ppermute | solution.py:301
  10.9 0.7 copy-start.2
  11.6 0.7 copy-start.4
  12.3 0.8 copy-start.6
  13.0 0.7 copy-start.8
  13.7 13.2 %copy-start.3 = (s32[1024]{0:T(1024)S(1)}, s32[1024]{0:T(1024)}, u32[]{:S(2)}) copy-start(s32[1024]{0:T(1024)} %param.11) | copy-start | bytes 12292
  13.7 13.2 %copy-start.5 = (f32[1024]{0:T(1024)S(1)}, f32[1024]{0:T(1024)}, u32[]{:S(2)}) copy-start(f32[1024]{0:T(1024)} %param.10) | copy-start | bytes 12292
  13.7 13.2 %copy-start.7 = (f32[3,2048]{1,0:T(4,128)S(1)}, f32[3,2048]{1,0:T(4,128)}, u32[]{:S(2)}) copy-start(f32[3,2048]{1,0:T(4,128)} %uvw_ref.3) | copy-start | bytes 73732
  13.7 13.2 %copy-start.9 = (f32[2,1024]{1,0:T(2,128)S(1)}, f32[2,1024]{1,0:T(2,128)}, u32[]{:S(2)}) copy-start(f32[2,1024]{1,0:T(2,128)} %sky_ref.3) | copy-start | bytes 24580
  23.1 13.2 %collective-permute-start.5 = (f32[64,512]{1,0:T(8,128)S(1)}, f32[64,512]{1,0:T(8,128)S(1)}, u32[]{:S(2)}, u32[]{:S(2)}) collective-permute-start(f32[64,512]{1,0:T(8,128)S(1)} %constant_dynamic-update-slice_fusion.pass_ref), channel_id=1, source_target_pairs={{0,24},{1,25},{2,26},{3,27},{4,28},{5,29},{6,30},{7,31},{8,0},{9,1... | collective-permute-start | bytes 393224 | tf_op jit(solution)/shard_map/ppermute | solution.py:301
  25.9 10.4 %collective-permute-start.4 = (f32[64,512]{1,0:T(8,128)S(1)}, f32[64,512]{1,0:T(8,128)S(1)}, u32[]{:S(2)}, u32[]{:S(2)}) collective-permute-start(f32[64,512]{1,0:T(8,128)S(1)} %constant_dynamic-update-slice_fusion.pass_ref), channel_id=1, source_target_pairs={{0,16},{1,17},{2,18},{3,19},{4,20},{5,21},{6,22},{7,23},{8,24},{9,... | collective-permute-start | bytes 393224 | tf_op jit(solution)/shard_map/ppermute | solution.py:301
  26.2 10.0 %collective-permute-start.3 = (f32[64,512]{1,0:T(8,128)S(1)}, f32[64,512]{1,0:T(8,128)S(1)}, u32[]{:S(2)}, u32[]{:S(2)}) collective-permute-start(f32[64,512]{1,0:T(8,128)S(1)} %constant_dynamic-update-slice_fusion.pass_ref), channel_id=1, source_target_pairs={{0,8},{1,9},{2,10},{3,11},{4,12},{5,13},{6,14},{7,15},{8,16},{9,17... | collective-permute-start | bytes 393224 | tf_op jit(solution)/shard_map/ppermute | solution.py:301
  26.9 13.6 %copy-start.1 = (s32[2,2048]{1,0:T(2,128)S(1)}, s32[2,2048]{1,0:T(2,128)}, u32[]{:S(2)}) copy-start(s32[2,2048]{1,0:T(2,128)} %rest_2_.1) | copy-start | bytes 49156
  36.3 4.2 %collective-permute-start.6 = (f32[256,512]{1,0:T(8,128)S(1)}, f32[256,512]{1,0:T(8,128)S(1)}, u32[]{:S(2)}, u32[]{:S(2)}) collective-permute-start(f32[256,512]{1,0:T(8,128)S(1)} %constant_dynamic-update-slice_fusion.4.rest_0_), channel_id=1, source_target_pairs={{0,1},{1,0},{2,3},{3,2},{4,5},{5,4},{6,7},{7,6},{8,9},{9,8},{10,11... | collective-permute-start | bytes 1572872 | tf_op jit(solution)/shard_map/ppermute | solution.py:301
  40.5 18.5 %copy-start = (f32[2,4,2048]{2,1,0:T(4,128)S(1)}, f32[2,4,2048]{2,1,0:T(4,128)}, u32[]{:S(2)}) copy-start(f32[2,4,2048]{2,1,0:T(4,128)} %obs_ref.1) | copy-start | bytes 196612
  64.9 2.7 %collective-permute-start.7 = (f32[2,1024]{1,0:T(2,128)S(1)}, f32[2,1024]{1,0:T(2,128)S(1)}, u32[]{:S(2)}, u32[]{:S(2)}) collective-permute-start(f32[2,1024]{1,0:T(2,128)S(1)} %scores.1), channel_id=1, source_target_pairs={{0,1},{1,0},{2,3},{3,2},{4,5},{5,4},{6,7},{7,6},{8,9},{9,8},{10,11... | collective-permute-start | bytes 24584 | tf_op jit(solution)/shard_map/ppermute | solution.py:301

commit v5 on v4

--- a/solution.py
+++ b/solution.py
@@ -15,7 +15,8 @@
 WIDE = 2 * F * BLOCK
 CHUNK = 256
 TILE = 16
-GROUPS = (4, 4)
+GROUPS = (4, 3, 1)
+HALVES = ((0, 1, 2),)
 SCOPED = 10 << 20
 F32 = jnp.float32
 BF16 = jnp.bfloat16
@@ -76,8 +77,20 @@
 
 
 def table_kernel(first, count, me_ref, sky_ref, flux_ref, clus_ref, uvw_ref, pass_ref, *rest):
+    *rest, sky, flux, clus, uvw_all, arrived = rest
     *table_refs, pred_ref, passed, place_ref, hot = rest[-(sky_ref.shape[1] // CHUNK + 4) :]
-    passed[...] = pass_ref[...]
+    if first == 0:
+        sources, copies = (sky_ref, flux_ref, clus_ref, uvw_ref), (sky, flux, clus, uvw_all)
+        moves = [
+            pltpu.make_async_copy(source, copy, arrived.at[n])
+            for n, (source, copy) in enumerate(zip(sources, copies))
+        ]
+        for move in moves:
+            move.start()
+        for move in moves:
+            move.wait()
+        sky_ref, flux_ref, clus_ref, uvw_ref = copies
+    passed[...] = pass_ref[0 : passed.shape[0], :]
     comps = sky_ref.shape[1]
     chunks, tiles, pieces = comps // CHUNK, BLOCK // TILE, WIDE // BLOCK
 
@@ -125,22 +138,28 @@
     return pltpu.with_memory_space_constraint(x, pltpu.VMEM)
 
 
-def make_tables(first, count, me, sky, fluxes, clusters, uvw, after, held):
+def make_tables(first, count, me, sky, fluxes, clusters, uvw, after, passed, held):
     comps = sky.shape[1]
     vmem = pl.BlockSpec(memory_space=pltpu.VMEM)
     chunks = comps // CHUNK
+    inputs = (sky, fluxes, clusters, uvw)
+    if first == 0:
+        inputs = tuple(pltpu.with_memory_space_constraint(x, pltpu.HBM) for x in inputs)
+    place = pl.BlockSpec(memory_space=pltpu.HBM) if first == 0 else vmem
     return pl.pallas_call(
         functools.partial(table_kernel, first, count),
-        in_specs=[pl.BlockSpec(memory_space=pltpu.SMEM)] + [vmem] * (5 + len(held)),
+        in_specs=[pl.BlockSpec(memory_space=pltpu.SMEM)] + [place] * 4 + [vmem] * (1 + len(held)),
         out_specs=[vmem] * (chunks + 2),
         out_shape=[pltpu.VMEM((count, WIDE, CHUNK), BF16)] * chunks
         + [
             pltpu.VMEM((count, C, WIDE), F32),
-            jax.ShapeDtypeStruct(after.shape, F32),
+            jax.ShapeDtypeStruct((passed, after.shape[1]), F32),
         ],
         scratch_shapes=[
             pltpu.VMEM((32, comps), BF16),
             pltpu.VMEM((C, comps), BF16),
+            *(pltpu.VMEM(x.shape, x.dtype) for x in inputs),
+            pltpu.SemaphoreType.DMA((4,)),
         ],
         compiler_params=pltpu.CompilerParams(vmem_limit_bytes=SCOPED),
         cost_estimate=pl.CostEstimate(
@@ -149,19 +168,26 @@
             transcendentals=4 * comps * count * WIDE,
         ),
         name="tables",
-    )(me, sky, fluxes, clusters, uvw, after, *map(in_vmem, held))
-
-
-def model_kernel(me_ref, *rest):
-    pieces, pair_ref, preds = rest[:2], rest[2], rest[3 : 3 + len(GROUPS)]
-    gain_ref, model_ref, curv_ref, table, found = rest[-5:]
-    owned = pieces[0].shape[0] // 16
-    for n, piece in enumerate(pieces):
-        flat = jnp.transpose(piece[...])
-        high = flat.astype(BF16)
-        at = pl.ds(n * flat.shape[1], flat.shape[1])
-        table[pl.ds(0, flat.shape[0]), at] = high
-        table[pl.ds(flat.shape[0], flat.shape[0]), at] = (flat - high.astype(F32)).astype(BF16)
+    )(me, *inputs, after, *map(in_vmem, held))
+
+
+def model_kernel(first, counts, build, me_ref, *rest):
+    if build:
+        pieces, (pair_ref, *rest) = rest[:2], rest[2:]
+        gain_ref, model_ref, curv_ref, table, found = rest[-5:]
+        owned = pieces[0].shape[0] // 16
+        for n, piece in enumerate(pieces):
+            flat = jnp.transpose(piece[...])
+            high = flat.astype(BF16)
+            at = pl.ds(n * flat.shape[1], flat.shape[1])
+            table[pl.ds(0, flat.shape[0]), at] = high
+            low = (flat - high.astype(F32)).astype(BF16)
+            table[pl.ds(flat.shape[0], flat.shape[0]), at] = low
+    else:
+        table, pair_ref, *rest = rest
+        gain_ref, model_ref, curv_ref, found = rest[-4:]
+        owned = table.shape[1] // 32
+    preds = rest[: len(counts)]
 
     me = me_ref[0]
     my_y, my_z, my_core = me >> 3, (me >> 1) & 3, me & 1
@@ -175,7 +201,8 @@
 
     def gather(i):
         for side in range(2):
-            hot = ids == slot[side : side + 1, i * BLOCK : (i + 1) * BLOCK]
+            at = (first + i) * BLOCK
+            hot = ids == slot[side : side + 1, at : at + BLOCK]
             hot = jnp.where(hot, 1.0, 0.0).astype(BF16)
             both = jnp.dot(table[...], hot, preferred_element_type=F32)
             found[i % 2, side] = both[:columns] + both[columns:]
@@ -211,42 +238,57 @@
     curv_ref[...] = curv[:, :128] + curv[:, 128:]
 
 
-def make_model(me, pieces, stations, preds, held, peers):
-    rows, columns = pieces[0].shape
-    count = sum(pred.shape[0] for pred in preds)
+def make_model(first, me, pieces, stations, preds, held, peers):
+    build = len(pieces) == 2
+    columns = pieces[0].shape[1] if build else pieces[0].shape[0] // 2
+    known = 2 * pieces[0].shape[0] if build else pieces[0].shape[1]
+    counts = [pred.shape[0] for pred in preds]
+    count = sum(counts)
     vmem = pl.BlockSpec(memory_space=pltpu.VMEM)
+    table = [pltpu.VMEM((2 * columns, known), BF16)] if build else []
     return pl.pallas_call(
-        model_kernel,
-        in_specs=[pl.BlockSpec(memory_space=pltpu.SMEM)] + [vmem] * (3 + len(preds) + len(held)),
-        out_specs=[vmem] * 3,
+        functools.partial(model_kernel, first, counts, build),
+        in_specs=[pl.BlockSpec(memory_space=pltpu.SMEM)]
+        + [vmem] * (len(pieces) + 1 + len(preds) + len(held)),
+        out_specs=[vmem] * (3 + len(table)),
         out_shape=[
             pltpu.VMEM((count, C, WIDE), F32),
             jax.ShapeDtypeStruct((peers, 2 * F, count * BLOCK), F32),
             jax.ShapeDtypeStruct((C, 128), F32),
-        ],
-        scratch_shapes=[
-            pltpu.VMEM((2 * columns, 2 * rows), BF16),
-            pltpu.VMEM((2, 2, columns, BLOCK), F32),
-        ],
+        ]
+        + table,
+        scratch_shapes=[pltpu.VMEM((2, 2, columns, BLOCK), F32)],
         compiler_params=pltpu.CompilerParams(vmem_limit_bytes=SCOPED),
+        cost_estimate=pl.CostEstimate(
+            flops=16 * columns * known * count * BLOCK,
+            bytes_accessed=16 * C * count * WIDE,
+            transcendentals=0,
+        ),
         name="model",
-    )(me, *pieces, stations, *map(in_vmem, preds), *map(in_vmem, held))
-
-
-def score_kernel(parts_ref, obs_ref, gain_ref, clus_ref, curv_ref, *rest):
-    *tables, out_ref, weight = rest
-    chunks = len(tables) // len(GROUPS)
+    )(
+        me,
+        *(pieces if build else map(in_vmem, pieces)),
+        stations,
+        *map(in_vmem, preds),
+        *map(in_vmem, held),
+    )
+
+
+def score_kernel(first, counts, ends, more, parts_ref, obs_ref, gain_ref, clus_ref, *rest):
+    curvs, (*tables, out_ref, weight) = rest[:ends], rest[ends:]
+    earlier, tables = tables[:more], tables[more:]
+    chunks = len(tables) // len(counts)
     blocks = [
-        (tables[n * chunks : (n + 1) * chunks], i) for n in range(len(GROUPS)) for i in range(GROUPS[n])
+        (tables[n * chunks : (n + 1) * chunks], i) for n in range(len(counts)) for i in range(counts[n])
     ]
 
     def weigh(i):
-        at = pl.ds(i * BLOCK, BLOCK)
+        at, seen = pl.ds(i * BLOCK, BLOCK), pl.ds((first + i) * BLOCK, BLOCK)
         model = jnp.sum(parts_ref[:, :, at], axis=0)
         for f in range(F):
             re, im = pl.ds(f * BLOCK, BLOCK), pl.ds((F + f) * BLOCK, BLOCK)
-            r_re = SCALES[f] * (obs_ref[0, f : f + 1, at] - model[f : f + 1, :])
-            r_im = SCALES[f] * (obs_ref[1, f : f + 1, at] - model[F + f : F + f + 1, :])
+            r_re = SCALES[f] * (obs_ref[0, f : f + 1, seen] - model[f : f + 1, :])
+            r_im = SCALES[f] * (obs_ref[1, f : f + 1, seen] - model[F + f : F + f + 1, :])
             g_re, g_im = gain_ref[i, :, re], gain_ref[i, :, im]
             weight[i % 2, :, re] = (r_re * g_re + r_im * g_im).astype(BF16)
             weight[i % 2, :, im] = (r_re * g_im - r_im * g_re).astype(BF16)
@@ -261,24 +303,45 @@
         if i + 1 < len(blocks):
             weigh(i + 1)
     scores = jnp.concatenate(scores, axis=1)
+    if not ends:
+        out_ref[...] = scores
+        return
+    scores = sum([ref[...] for ref in earlier], scores)
     hot = lax.broadcasted_iota(jnp.int32, scores.shape, 0) == clus_ref[...]
-    curv = jnp.sum(curv_ref[...], axis=1, keepdims=True)
+    curv = jnp.sum(sum(curv[...] for curv in curvs), axis=1, keepdims=True)
     out_ref[0:1, :] = jnp.sum(jnp.where(hot, scores, 0.0), axis=0, keepdims=True)
     out_ref[1:2, :] = jnp.sum(jnp.where(hot, curv, 0.0), axis=0, keepdims=True)
 
 
-def make_scores(parts, observed, gain, clusters, curv, tables):
+def make_scores(first, parts, observed, gain, clusters, curvs, earlier, tables):
     comps = clusters.shape[1]
+    chunks = comps // CHUNK
+    counts = [tables[n].shape[0] for n in range(0, len(tables), chunks)]
     vmem = pl.BlockSpec(memory_space=pltpu.VMEM)
     return pl.pallas_call(
-        score_kernel,
-        in_specs=[vmem] * (5 + len(tables)),
+        functools.partial(score_kernel, first, counts, len(curvs), len(earlier)),
+        in_specs=[vmem] * (4 + len(curvs) + len(earlier) + len(tables)),
         out_specs=vmem,
-        out_shape=jax.ShapeDtypeStruct((2, comps), F32),
+        out_shape=jax.ShapeDtypeStruct((2, comps), F32)
+        if curvs
+        else pltpu.VMEM((C, comps), F32),
         scratch_shapes=[pltpu.VMEM((2, C, WIDE), BF16)],
         compiler_params=pltpu.CompilerParams(vmem_limit_bytes=SCOPED),
+        cost_estimate=pl.CostEstimate(
+            flops=2 * C * comps * sum(counts) * WIDE,
+            bytes_accessed=2 * comps * sum(counts) * WIDE,
+            transcendentals=0,
+        ),
         name="scores",
-    )(parts, observed, in_vmem(gain), clusters, curv, *map(in_vmem, tables))
+    )(
+        parts,
+        observed,
+        in_vmem(gain),
+        clusters,
+        *curvs,
+        *map(in_vmem, earlier),
+        *map(in_vmem, tables),
+    )
 
 
 def other_core():
@@ -311,10 +374,10 @@
 
     owned = station_gains + gain_step
     others = [permute(owned, turn_z(k)) for k in (1, 2, 3)]
-    tables, preds = [], []
+    groups, preds = [], []
     after = owned
     for n, count in enumerate(GROUPS):
-        *parts, pred, after = make_tables(
+        *group, pred, passed = make_tables(
             firsts[n],
             count,
             me,
@@ -323,18 +386,47 @@
             cluster_row,
             baseline_uvw,
             after,
-            tables + preds,
+            after.shape[0] if n < 2 else 8,
+            [x for held in groups for x in held] + preds,
         )
-        tables += parts
+        groups.append(group)
         preds.append(pred)
         if n == 0:
-            after = jnp.concatenate([after] + others, axis=0)
+            after = jnp.concatenate([passed] + others, axis=0)
             others = [permute(after, turn_y(k)) for k in (1, 2, 3)]
-    plane = jnp.concatenate([after] + others, axis=0)
-    pieces = [plane, permute(plane, other_core())]
-    gain, model, curv = make_model(me, pieces, stations, preds, tables, peers)
-    parts = lax.all_to_all(model, "comp", 0, 0, tiled=True)
-    sums = make_scores(parts, observed_vis, gain, cluster_row, curv, tables)
+        elif n == 1:
+            after = jnp.concatenate([passed] + others, axis=0)
+            pieces = [after, permute(after, other_core())]
+
+    tables = [x for held in groups for x in held]
+    gains, curvs, sent = [], [], []
+    for half in HALVES:
+        gain, model, curv, *table = make_model(
+            firsts[half[0]],
+            me,
+            pieces,
+            stations,
+            [preds[n] for n in half],
+            tables + gains,
+            peers,
+        )
+        gains.append(gain)
+        curvs.append(curv)
+        sent.append(lax.all_to_all(model, "comp", 0, 0, tiled=True))
+        pieces = table
+    earlier = []
+    for n, half in enumerate(HALVES):
+        sums = make_scores(
+            firsts[half[0]],
+            sent[n],
+            observed_vis,
+            gains[n],
+            cluster_row,
+            curvs if n == len(HALVES) - 1 else [],
+            earlier,
+            [x for group in half for x in groups[group]],
+        )
+        earlier = [sums]
     sums = sums + permute(sums, other_core())
     sums = lax.all_to_all(
         jnp.broadcast_to(sums[None], (16,) + sums.shape),

time: 84.5 us -> 82.4 us (0.975)
  local copies, waits for them, and re-layouts: 2.96 us -> 0.12 us
  Pallas kernels: 29.4 us -> 31.8 us
  starting transfers between devices: 18.5 us -> 17.4 us
  waiting for transfers between devices: 2.38 us -> 1.32 us
    unnamed x26 -> x18, local copies, waits for them, and re-layouts: 2.9 us -> 0.07 us
    pallas_call x2 -> x3, Pallas kernels: 18.5 us -> 20.9 us  [make_tables(): pl.pallas_call(functools.partial(table_kernel, first, count), in_specs=[p...]
    ppermute x8, starting transfers between devices: 18.5 us -> 17.4 us  [permute(): return lax.ppermute(x, 'row', pairs)]
    ppermute x8, waiting for transfers between devices: 2.38 us -> 1.32 us  [permute(): return lax.ppermute(x, 'row', pairs)]
  transfers between devices with their start and end apart: 8 -> 8, of which waited for: 2 -> 2; matrix products, arithmetic and copies ran while one was open for 0% -> 0% of each run, Pallas kernels for 22% -> 25%
where the time goes in v5:
time: 82.4 us; the launch traced here: 82.2 us
  Pallas kernels  31.8 us (39%)
  blocking collectives  29.8 us (36%)
  starting transfers between devices  17.4 us (21%)
  other arithmetic  1.45 us (2%)
  waiting for transfers between devices  1.32 us (2%)
    pallas_call x3, Pallas kernels, make_tables(): pl.pallas_call(functools.partial(table_kernel, first, count), in_specs=[p...  20.9 us
    ppermute x8, starting transfers between devices, permute(): return lax.ppermute(x, 'row', pairs)  17.4 us
    all_to_all x1, blocking collectives, per_device(): lax.all_to_all(jnp.broadcast_to(sums[None], (16,) + sums.shape), 'row', 0...  15.7 us
    all_to_all x1, blocking collectives, per_device(): sent.append(lax.all_to_all(model, 'comp', 0, 0, tiled=True))  14.2 us
    pallas_call x1, Pallas kernels, make_scores(): pl.pallas_call(functools.partial(score_kernel, first, counts, len(curvs),...  5.91 us
    pallas_call x1, Pallas kernels, make_model(): pl.pallas_call(functools.partial(model_kernel, first, counts, build), in_...  5.01 us
  transfers between devices with their start and end apart: 8, of which 2 were waited for; matrix products, arithmetic and copies ran while one was open for 0% of the time, Pallas kernels for 25%

profile of v5, /device:TPU:1, one launch (start us, length us, event | category | flops | bytes accessed | tf_op | source)
XLA Modules:
  0.0 82.2 jit_solution(16396523624744970868)
XLA Ops:
  0.0 0.8 add.9.pass_ref
  0.8 6.8 %collective-permute-start.2 = (f32[16,512]{1,0:T(8,128)S(1)}, f32[16,512]{1,0:T(8,128)S(1)}, u32[]{:S(2)}, u32[]{:S(2)}) collective-permute-start(f32[16,512]{1,0:T(8,128)S(1)} %add.9.pass_ref), channel_id=1, source_target_pairs={{0,6},{1,7},{2,0},{3,1},{4,2},{5,3},{6,4},{7,5},{8,14},{9,15},{10,... | collective-permute-start | bytes 98312 | tf_op jit(solution)/shard_map/ppermute | solution.py:364
  7.6 1.0 %collective-permute-start.1 = (f32[16,512]{1,0:T(8,128)S(1)}, f32[16,512]{1,0:T(8,128)S(1)}, u32[]{:S(2)}, u32[]{:S(2)}) collective-permute-start(f32[16,512]{1,0:T(8,128)S(1)} %add.9.pass_ref), channel_id=1, source_target_pairs={{0,4},{1,5},{2,6},{3,7},{4,0},{5,1},{6,2},{7,3},{8,12},{9,13},{10,... | collective-permute-start | bytes 98312 | tf_op jit(solution)/shard_map/ppermute | solution.py:364
  8.6 2.3 %collective-permute-start = (f32[16,512]{1,0:T(8,128)S(1)}, f32[16,512]{1,0:T(8,128)S(1)}, u32[]{:S(2)}, u32[]{:S(2)}) collective-permute-start(f32[16,512]{1,0:T(8,128)S(1)} %add.9.pass_ref), channel_id=1, source_target_pairs={{0,2},{1,3},{2,4},{3,5},{4,6},{5,7},{6,0},{7,1},{8,10},{9,11},{10,... | collective-permute-start | bytes 98312 | tf_op jit(solution)/shard_map/ppermute | solution.py:364
  10.9 10.2 %tables.3 = (bf16[4,2048,256]{2,1,0:T(8,128)(2,1)S(1)}, bf16[4,2048,256]{2,1,0:T(8,128)(2,1)S(1)}, bf16[4,2048,256]{2,1,0:T(8,128)(2,1)S(1)}, bf16[4,2048,256]{2...) custom-call(s32[1]{0:T(128)} %bitcast.me_ref, f32[2,1024]{1,0:T(2,128)} %sky_ref.5, ...), custom_call_target="tpu_custom_call" | custom-call | flops 1073741824 | bytes 16777216 | tf_op jit(solution)/shard_map/tables/pallas_call | solution.py:149
  21.1 0.0 collective-permute-done
  21.1 0.0 collective-permute-done.1
  21.1 0.0 collective-permute-done.2
  21.1 2.8 %collective-permute-start.5 = (f32[64,512]{1,0:T(8,128)S(1)}, f32[64,512]{1,0:T(8,128)S(1)}, u32[]{:S(2)}, u32[]{:S(2)}) collective-permute-start(f32[64,512]{1,0:T(8,128)S(1)} %constant_dynamic-update-slice_fusion.pass_ref), channel_id=1, source_target_pairs={{0,24},{1,25},{2,26},{3,27},{4,28},{5,29},{6,30},{7,31},{8,0},{9,1... | collective-permute-start | bytes 393224 | tf_op jit(solution)/shard_map/ppermute | solution.py:364
  24.0 0.3 collective-permute-start.4
  24.3 0.7 collective-permute-start.3
  25.0 0.0 copy-done.1
  25.0 0.0 copy-done.3
  25.0 0.0 copy-done.4
  25.0 0.0 copy-done.5
  25.0 7.2 %tables.4 = (bf16[3,2048,256]{2,1,0:T(8,128)(2,1)S(1)}, bf16[3,2048,256]{2,1,0:T(8,128)(2,1)S(1)}, bf16[3,2048,256]{2,1,0:T(8,128)(2,1)S(1)}, bf16[3,2048,256]{2...) custom-call(s32[1]{0:T(128)} %bitcast.me_ref, f32[2,1024]{1,0:T(2,128)S(1)} %copy-done.5, ...), custom_call_target="tpu_custom_call" | custom-call | flops 805306368 | bytes 12582912 | tf_op jit(solution)/shard_map/tables/pallas_call | solution.py:149
  32.2 0.5 collective-permute-done.3
  32.7 0.0 collective-permute-done.4
  32.7 0.0 collective-permute-done.5
  32.7 2.2 %collective-permute-start.6 = (f32[256,512]{1,0:T(8,128)S(1)}, f32[256,512]{1,0:T(8,128)S(1)}, u32[]{:S(2)}, u32[]{:S(2)}) collective-permute-start(f32[256,512]{1,0:T(8,128)S(1)} %constant_dynamic-update-slice_fusion.4.pass_ref.rest_0_), channel_id=1, source_target_pairs={{0,1},{1,0},{2,3},{3,2},{4,5},{5,4},{6,7},{7,6},{8,9},{9,8},{10,11... | collective-permute-start | bytes 1572872 | tf_op jit(solution)/shard_map/ppermute | solution.py:364
  35.0 3.6 %tables.5 = (bf16[1,2048,256]{2,1,0:T(8,128)(2,1)S(1)}, bf16[1,2048,256]{2,1,0:T(8,128)(2,1)S(1)}, bf16[1,2048,256]{2,1,0:T(8,128)(2,1)S(1)}, bf16[1,2048,256]{2...) custom-call(s32[1]{0:T(128)} %bitcast.me_ref, f32[2,1024]{1,0:T(2,128)S(1)} %copy-done.5, ...), custom_call_target="tpu_custom_call" | custom-call | flops 268435456 | bytes 4194304 | tf_op jit(solution)/shard_map/tables/pallas_call | solution.py:149
  38.5 0.0 collective-permute-done.6.rest_1_
  38.6 0.0 copy-done.2
  38.6 0.0 copy-start
  38.6 5.0 %model.1 = (f32[8,64,2048]{2,1,0:T(8,128)S(1)}, f32[8,8,2048]{2,1,0:T(8,128)S(1)}, f32[64,128]{1,0:T(8,128)S(1)}, bf16[1024,512]{1,0:T(8,128)(2,1)}) custom-call(s32[1]{0:T(128)} %bitcast.me_ref, f32[256,512]{1,0:T(8,128)S(1)} %constant_dynamic-update-slice_fusion.4.pass_ref.rest_0_, f32[256,512]{1,0:T(8,128)S(1)} %collective-permute-done.6.rest_1_, ...), custom_call_target="tpu_custom_call" | custom-call | flops 8589934592 | bytes 16777216 | tf_op jit(solution)/shard_map/model/pallas_call | solution.py:249
  43.6 14.2 %all_to_all.10.parts_ref = f32[8,8,2048]{2,1,0:T(8,128)S(1)} all-to-all(f32[8,8,2048]{2,1,0:T(8,128)S(1)} %get-tuple-element.42), channel_id=1, replica_groups=mesh['comp'=8,'row'=32] {'comp'}, dimensions={0} | all-to-all | bytes 1048576 | tf_op jit(solution)/shard_map/all_to_all | solution.py:415
  57.8 5.9 %scores.1 = f32[2,1024]{1,0:T(2,128)S(1)} custom-call(f32[8,8,2048]{2,1,0:T(8,128)S(1)} %all_to_all.10.parts_ref, f32[2,4,2048]{2,1,0:T(4,128)S(1)} %copy-done, f32[8,64,2048]{2,1,0:T(8,128)S(1)} %get-tuple-element.43.gain_ref, s32[1,1024]{1,0:T(1,128)S(1)} %bitcast.7, f32[64,128]{1,0:T(8,128)S(1)} %get-tuple-element.44.rest_0_, ...), custom_call_target="tpu_custom_call" | custom-call | flops 2147483648 | bytes 33554432 | tf_op jit(solution)/shard_map/scores/pallas_call | solution.py:321
  63.7 1.2 %collective-permute-start.7 = (f32[2,1024]{1,0:T(2,128)S(1)}, f32[2,1024]{1,0:T(2,128)S(1)}, u32[]{:S(2)}, u32[]{:S(2)}) collective-permute-start(f32[2,1024]{1,0:T(2,128)S(1)} %scores.1), channel_id=1, source_target_pairs={{0,1},{1,0},{2,3},{3,2},{4,5},{5,4},{6,7},{7,6},{8,9},{9,8},{10,11... | collective-permute-start | bytes 24584 | tf_op jit(solution)/shard_map/ppermute | solution.py:364
  64.9 0.8 %collective-permute-done.7 = f32[2,1024]{1,0:T(2,128)S(1)} collective-permute-done((f32[2,1024]{1,0:T(2,128)S(1)}, f32[2,1024]{1,0:T(2,128)S(1)}, u32[]{:S(2)}, u32[]{:S(2)}) %collective-permute-start.7) | collective-permute-done | bytes 8224 | tf_op jit(solution)/shard_map/ppermute | solution.py:364
  65.8 15.7 %all_to_all.11 = f32[16,2,1024]{2,1,0:T(2,128)S(1)} all-to-all(f32[16,2,1024]{2,1,0:T(2,128)S(1)} %broadcast_in_dim.18), channel_id=1, replica_groups={{0,2,4,6,8,10,12,14,16,18,20,22,24,26,28,30},{1,3,5,7,9,11,13,15,17,19,..., dimensions={0} | all-to-all | bytes 262144 | tf_op jit(solution)/shard_map/all_to_all | solution.py:431
  81.5 0.1 reduce_sum.9
  81.6 0.6 add.11
  (17 shorter events, 0.1 us)
Async XLA Ops:
  0.8 20.3 %collective-permute-start.2 = (f32[16,512]{1,0:T(8,128)S(1)}, f32[16,512]{1,0:T(8,128)S(1)}, u32[]{:S(2)}, u32[]{:S(2)}) collective-permute-start(f32[16,512]{1,0:T(8,128)S(1)} %add.9.pass_ref), channel_id=1, source_target_pairs={{0,6},{1,7},{2,0},{3,1},{4,2},{5,3},{6,4},{7,5},{8,14},{9,15},{10,... | collective-permute-start | bytes 98312 | tf_op jit(solution)/shard_map/ppermute | solution.py:364
  7.6 13.5 %collective-permute-start.1 = (f32[16,512]{1,0:T(8,128)S(1)}, f32[16,512]{1,0:T(8,128)S(1)}, u32[]{:S(2)}, u32[]{:S(2)}) collective-permute-start(f32[16,512]{1,0:T(8,128)S(1)} %add.9.pass_ref), channel_id=1, source_target_pairs={{0,4},{1,5},{2,6},{3,7},{4,0},{5,1},{6,2},{7,3},{8,12},{9,13},{10,... | collective-permute-start | bytes 98312 | tf_op jit(solution)/shard_map/ppermute | solution.py:364
  8.6 12.5 %collective-permute-start = (f32[16,512]{1,0:T(8,128)S(1)}, f32[16,512]{1,0:T(8,128)S(1)}, u32[]{:S(2)}, u32[]{:S(2)}) collective-permute-start(f32[16,512]{1,0:T(8,128)S(1)} %add.9.pass_ref), channel_id=1, source_target_pairs={{0,2},{1,3},{2,4},{3,5},{4,6},{5,7},{6,0},{7,1},{8,10},{9,11},{10,... | collective-permute-start | bytes 98312 | tf_op jit(solution)/shard_map/ppermute | solution.py:364
  10.9 14.1 %copy-start.1 = (f32[3,2048]{1,0:T(4,128)S(1)}, f32[3,2048]{1,0:T(4,128)}, u32[]{:S(2)}) copy-start(f32[3,2048]{1,0:T(4,128)} %uvw_ref.5) | copy-start | bytes 73732
  10.9 14.1 %copy-start.3 = (s32[1024]{0:T(1024)S(1)}, s32[1024]{0:T(1024)}, u32[]{:S(2)}) copy-start(s32[1024]{0:T(1024)} %param.11) | copy-start | bytes 12292
  10.9 14.1 %copy-start.4 = (f32[1024]{0:T(1024)S(1)}, f32[1024]{0:T(1024)}, u32[]{:S(2)}) copy-start(f32[1024]{0:T(1024)} %param.10) | copy-start | bytes 12292
  10.9 14.1 %copy-start.5 = (f32[2,1024]{1,0:T(2,128)S(1)}, f32[2,1024]{1,0:T(2,128)}, u32[]{:S(2)}) copy-start(f32[2,1024]{1,0:T(2,128)} %sky_ref.5) | copy-start | bytes 24580
  21.1 11.6 %collective-permute-start.5 = (f32[64,512]{1,0:T(8,128)S(1)}, f32[64,512]{1,0:T(8,128)S(1)}, u32[]{:S(2)}, u32[]{:S(2)}) collective-permute-start(f32[64,512]{1,0:T(8,128)S(1)} %constant_dynamic-update-slice_fusion.pass_ref), channel_id=1, source_target_pairs={{0,24},{1,25},{2,26},{3,27},{4,28},{5,29},{6,30},{7,31},{8,0},{9,1... | collective-permute-start | bytes 393224 | tf_op jit(solution)/shard_map/ppermute | solution.py:364
  24.0 8.7 %collective-permute-start.4 = (f32[64,512]{1,0:T(8,128)S(1)}, f32[64,512]{1,0:T(8,128)S(1)}, u32[]{:S(2)}, u32[]{:S(2)}) collective-permute-start(f32[64,512]{1,0:T(8,128)S(1)} %constant_dynamic-update-slice_fusion.pass_ref), channel_id=1, source_target_pairs={{0,16},{1,17},{2,18},{3,19},{4,20},{5,21},{6,22},{7,23},{8,24},{9,... | collective-permute-start | bytes 393224 | tf_op jit(solution)/shard_map/ppermute | solution.py:364
  24.3 8.4 %collective-permute-start.3 = (f32[64,512]{1,0:T(8,128)S(1)}, f32[64,512]{1,0:T(8,128)S(1)}, u32[]{:S(2)}, u32[]{:S(2)}) collective-permute-start(f32[64,512]{1,0:T(8,128)S(1)} %constant_dynamic-update-slice_fusion.pass_ref), channel_id=1, source_target_pairs={{0,8},{1,9},{2,10},{3,11},{4,12},{5,13},{6,14},{7,15},{8,16},{9,17... | collective-permute-start | bytes 393224 | tf_op jit(solution)/shard_map/ppermute | solution.py:364
  32.7 5.8 %collective-permute-start.6 = (f32[256,512]{1,0:T(8,128)S(1)}, f32[256,512]{1,0:T(8,128)S(1)}, u32[]{:S(2)}, u32[]{:S(2)}) collective-permute-start(f32[256,512]{1,0:T(8,128)S(1)} %constant_dynamic-update-slice_fusion.4.pass_ref.rest_0_), channel_id=1, source_target_pairs={{0,1},{1,0},{2,3},{3,2},{4,5},{5,4},{6,7},{7,6},{8,9},{9,8},{10,11... | collective-permute-start | bytes 1572872 | tf_op jit(solution)/shard_map/ppermute | solution.py:364
  35.0 3.6 %copy-start.2 = (s32[2,2048]{1,0:T(2,128)S(1)}, s32[2,2048]{1,0:T(2,128)}, u32[]{:S(2)}) copy-start(s32[2,2048]{1,0:T(2,128)} %rest_2_.1) | copy-start | bytes 49156
  38.6 19.2 %copy-start = (f32[2,4,2048]{2,1,0:T(4,128)S(1)}, f32[2,4,2048]{2,1,0:T(4,128)}, u32[]{:S(2)}) copy-start(f32[2,4,2048]{2,1,0:T(4,128)} %obs_ref.1) | copy-start | bytes 196612
  63.7 2.1 %collective-permute-start.7 = (f32[2,1024]{1,0:T(2,128)S(1)}, f32[2,1024]{1,0:T(2,128)S(1)}, u32[]{:S(2)}, u32[]{:S(2)}) collective-permute-start(f32[2,1024]{1,0:T(2,128)S(1)} %scores.1), channel_id=1, source_target_pairs={{0,1},{1,0},{2,3},{3,2},{4,5},{5,4},{6,7},{7,6},{8,9},{9,8},{10,11... | collective-permute-start | bytes 24584 | tf_op jit(solution)/shard_map/ppermute | solution.py:364

commit v6 on v5

--- a/solution.py
+++ b/solution.py
@@ -178,11 +178,7 @@
         owned = pieces[0].shape[0] // 16
         for n, piece in enumerate(pieces):
             flat = jnp.transpose(piece[...])
-            high = flat.astype(BF16)
-            at = pl.ds(n * flat.shape[1], flat.shape[1])
-            table[pl.ds(0, flat.shape[0]), at] = high
-            low = (flat - high.astype(F32)).astype(BF16)
-            table[pl.ds(flat.shape[0], flat.shape[0]), at] = low
+            table[:, pl.ds(n * flat.shape[1], flat.shape[1])] = flat.astype(BF16)
     else:
         table, pair_ref, *rest = rest
         gain_ref, model_ref, curv_ref, found = rest[-4:]
@@ -192,7 +188,6 @@
     me = me_ref[0]
     my_y, my_z, my_core = me >> 3, (me >> 1) & 3, me & 1
     stations = table.shape[1]
-    columns = table.shape[0] // 2
     ids = lax.broadcasted_iota(jnp.int32, (stations, BLOCK), 0)
     pair = pair_ref[...]
     owner, own = pair // owned, pair % owned
@@ -204,8 +199,7 @@
             at = (first + i) * BLOCK
             hot = ids == slot[side : side + 1, at : at + BLOCK]
             hot = jnp.where(hot, 1.0, 0.0).astype(BF16)
-            both = jnp.dot(table[...], hot, preferred_element_type=F32)
-            found[i % 2, side] = both[:columns] + both[columns:]
+            found[i % 2, side] = jnp.dot(table[...], hot, preferred_element_type=F32)
 
     curv = jnp.zeros((C, BLOCK), F32)
     count = gain_ref.shape[0]
@@ -240,12 +234,12 @@
 
 def make_model(first, me, pieces, stations, preds, held, peers):
     build = len(pieces) == 2
-    columns = pieces[0].shape[1] if build else pieces[0].shape[0] // 2
+    columns = pieces[0].shape[1] if build else pieces[0].shape[0]
     known = 2 * pieces[0].shape[0] if build else pieces[0].shape[1]
     counts = [pred.shape[0] for pred in preds]
     count = sum(counts)
     vmem = pl.BlockSpec(memory_space=pltpu.VMEM)
-    table = [pltpu.VMEM((2 * columns, known), BF16)] if build else []
+    table = [pltpu.VMEM((columns, known), BF16)] if build else []
     return pl.pallas_call(
         functools.partial(model_kernel, first, counts, build),
         in_specs=[pl.BlockSpec(memory_space=pltpu.SMEM)]
@@ -260,7 +254,7 @@
         scratch_shapes=[pltpu.VMEM((2, 2, columns, BLOCK), F32)],
         compiler_params=pltpu.CompilerParams(vmem_limit_bytes=SCOPED),
         cost_estimate=pl.CostEstimate(
-            flops=16 * columns * known * count * BLOCK,
+            flops=8 * columns * known * count * BLOCK,
             bytes_accessed=16 * C * count * WIDE,
             transcendentals=0,
         ),

time: 82.4 us -> 81.3 us (0.987)
  Pallas kernels: 31.8 us -> 30.7 us
    pallas_call x1, Pallas kernels: 5.01 us -> 3.9 us  [make_model(): pl.pallas_call(functools.partial(model_kernel, first, counts, build), in_...]
  transfers between devices with their start and end apart: 8 -> 8, of which waited for: 2 -> 2; matrix products, arithmetic and copies ran while one was open for 0% -> 0% of each run, Pallas kernels for 25% -> 26%
where the time goes in v6:
time: 81.3 us; the launch traced here: 81 us
  Pallas kernels  30.7 us (38%)
  blocking collectives  29.8 us (37%)
  starting transfers between devices  17.4 us (21%)
  other arithmetic  1.45 us (2%)
  waiting for transfers between devices  1.32 us (2%)
    pallas_call x3, Pallas kernels, make_tables(): pl.pallas_call(functools.partial(table_kernel, first, count), in_specs=[p...  20.9 us
    ppermute x8, starting transfers between devices, permute(): return lax.ppermute(x, 'row', pairs)  17.4 us
    all_to_all x1, blocking collectives, per_device(): lax.all_to_all(jnp.broadcast_to(sums[None], (16,) + sums.shape), 'row', 0...  15.7 us
    all_to_all x1, blocking collectives, per_device(): sent.append(lax.all_to_all(model, 'comp', 0, 0, tiled=True))  14.2 us
    pallas_call x1, Pallas kernels, make_scores(): pl.pallas_call(functools.partial(score_kernel, first, counts, len(curvs),...  5.91 us
    pallas_call x1, Pallas kernels, make_model(): pl.pallas_call(functools.partial(model_kernel, first, counts, build), in_...  3.9 us
  transfers between devices with their start and end apart: 8, of which 2 were waited for; matrix products, arithmetic and copies ran while one was open for 0% of the time, Pallas kernels for 26%

profile of v6, /device:TPU:1, one launch (start us, length us, event | category | flops | bytes accessed | tf_op | source)
XLA Modules:
  0.0 81.0 jit_solution(15668926988097290807)
XLA Ops:
  0.0 0.8 add.9.pass_ref
  0.8 6.8 %collective-permute-start.2 = (f32[16,512]{1,0:T(8,128)S(1)}, f32[16,512]{1,0:T(8,128)S(1)}, u32[]{:S(2)}, u32[]{:S(2)}) collective-permute-start(f32[16,512]{1,0:T(8,128)S(1)} %add.9.pass_ref), channel_id=1, source_target_pairs={{0,6},{1,7},{2,0},{3,1},{4,2},{5,3},{6,4},{7,5},{8,14},{9,15},{10,... | collective-permute-start | bytes 98312 | tf_op jit(solution)/shard_map/ppermute | solution.py:358
  7.6 1.0 %collective-permute-start.1 = (f32[16,512]{1,0:T(8,128)S(1)}, f32[16,512]{1,0:T(8,128)S(1)}, u32[]{:S(2)}, u32[]{:S(2)}) collective-permute-start(f32[16,512]{1,0:T(8,128)S(1)} %add.9.pass_ref), channel_id=1, source_target_pairs={{0,4},{1,5},{2,6},{3,7},{4,0},{5,1},{6,2},{7,3},{8,12},{9,13},{10,... | collective-permute-start | bytes 98312 | tf_op jit(solution)/shard_map/ppermute | solution.py:358
  8.6 2.3 %collective-permute-start = (f32[16,512]{1,0:T(8,128)S(1)}, f32[16,512]{1,0:T(8,128)S(1)}, u32[]{:S(2)}, u32[]{:S(2)}) collective-permute-start(f32[16,512]{1,0:T(8,128)S(1)} %add.9.pass_ref), channel_id=1, source_target_pairs={{0,2},{1,3},{2,4},{3,5},{4,6},{5,7},{6,0},{7,1},{8,10},{9,11},{10,... | collective-permute-start | bytes 98312 | tf_op jit(solution)/shard_map/ppermute | solution.py:358
  10.9 10.2 %tables.3 = (bf16[4,2048,256]{2,1,0:T(8,128)(2,1)S(1)}, bf16[4,2048,256]{2,1,0:T(8,128)(2,1)S(1)}, bf16[4,2048,256]{2,1,0:T(8,128)(2,1)S(1)}, bf16[4,2048,256]{2...) custom-call(s32[1]{0:T(128)} %bitcast.me_ref, f32[2,1024]{1,0:T(2,128)} %sky_ref.5, ...), custom_call_target="tpu_custom_call" | custom-call | flops 1073741824 | bytes 16777216 | tf_op jit(solution)/shard_map/tables/pallas_call | solution.py:149
  21.1 0.0 collective-permute-done
  21.1 0.0 collective-permute-done.1
  21.1 0.0 collective-permute-done.2
  21.1 2.8 %collective-permute-start.5 = (f32[64,512]{1,0:T(8,128)S(1)}, f32[64,512]{1,0:T(8,128)S(1)}, u32[]{:S(2)}, u32[]{:S(2)}) collective-permute-start(f32[64,512]{1,0:T(8,128)S(1)} %constant_dynamic-update-slice_fusion.pass_ref), channel_id=1, source_target_pairs={{0,24},{1,25},{2,26},{3,27},{4,28},{5,29},{6,30},{7,31},{8,0},{9,1... | collective-permute-start | bytes 393224 | tf_op jit(solution)/shard_map/ppermute | solution.py:358
  24.0 0.3 collective-permute-start.4
  24.3 0.7 collective-permute-start.3
  25.0 0.0 copy-done.1
  25.0 0.0 copy-done.3
  25.0 0.0 copy-done.4
  25.0 0.0 copy-done.5
  25.0 7.2 %tables.4 = (bf16[3,2048,256]{2,1,0:T(8,128)(2,1)S(1)}, bf16[3,2048,256]{2,1,0:T(8,128)(2,1)S(1)}, bf16[3,2048,256]{2,1,0:T(8,128)(2,1)S(1)}, bf16[3,2048,256]{2...) custom-call(s32[1]{0:T(128)} %bitcast.me_ref, f32[2,1024]{1,0:T(2,128)S(1)} %copy-done.5, ...), custom_call_target="tpu_custom_call" | custom-call | flops 805306368 | bytes 12582912 | tf_op jit(solution)/shard_map/tables/pallas_call | solution.py:149
  32.2 0.5 collective-permute-done.3
  32.7 0.0 collective-permute-done.4
  32.7 0.0 collective-permute-done.5
  32.7 2.2 %collective-permute-start.6 = (f32[256,512]{1,0:T(8,128)S(1)}, f32[256,512]{1,0:T(8,128)S(1)}, u32[]{:S(2)}, u32[]{:S(2)}) collective-permute-start(f32[256,512]{1,0:T(8,128)S(1)} %constant_dynamic-update-slice_fusion.4.pass_ref.rest_0_), channel_id=1, source_target_pairs={{0,1},{1,0},{2,3},{3,2},{4,5},{5,4},{6,7},{7,6},{8,9},{9,8},{10,11... | collective-permute-start | bytes 1572872 | tf_op jit(solution)/shard_map/ppermute | solution.py:358
  35.0 3.6 %tables.5 = (bf16[1,2048,256]{2,1,0:T(8,128)(2,1)S(1)}, bf16[1,2048,256]{2,1,0:T(8,128)(2,1)S(1)}, bf16[1,2048,256]{2,1,0:T(8,128)(2,1)S(1)}, bf16[1,2048,256]{2...) custom-call(s32[1]{0:T(128)} %bitcast.me_ref, f32[2,1024]{1,0:T(2,128)S(1)} %copy-done.5, ...), custom_call_target="tpu_custom_call" | custom-call | flops 268435456 | bytes 4194304 | tf_op jit(solution)/shard_map/tables/pallas_call | solution.py:149
  38.5 0.0 collective-permute-done.6.rest_1_
  38.6 0.0 copy-done.2
  38.6 0.0 copy-start
  38.6 3.9 %model.1 = (f32[8,64,2048]{2,1,0:T(8,128)S(1)}, f32[8,8,2048]{2,1,0:T(8,128)S(1)}, f32[64,128]{1,0:T(8,128)S(1)}, bf16[512,512]{1,0:T(8,128)(2,1)}) custom-call(s32[1]{0:T(128)} %bitcast.me_ref, f32[256,512]{1,0:T(8,128)S(1)} %constant_dynamic-update-slice_fusion.4.pass_ref.rest_0_, f32[256,512]{1,0:T(8,128)S(1)} %collective-permute-done.6.rest_1_, ...), custom_call_target="tpu_custom_call" | custom-call | flops 4294967296 | bytes 16777216 | tf_op jit(solution)/shard_map/model/pallas_call | solution.py:243
  42.5 14.2 %all_to_all.10.parts_ref = f32[8,8,2048]{2,1,0:T(8,128)S(1)} all-to-all(f32[8,8,2048]{2,1,0:T(8,128)S(1)} %get-tuple-element.42), channel_id=1, replica_groups=mesh['comp'=8,'row'=32] {'comp'}, dimensions={0} | all-to-all | bytes 1048576 | tf_op jit(solution)/shard_map/all_to_all | solution.py:409
  56.6 5.9 %scores.1 = f32[2,1024]{1,0:T(2,128)S(1)} custom-call(f32[8,8,2048]{2,1,0:T(8,128)S(1)} %all_to_all.10.parts_ref, f32[2,4,2048]{2,1,0:T(4,128)S(1)} %copy-done, f32[8,64,2048]{2,1,0:T(8,128)S(1)} %get-tuple-element.43.gain_ref, s32[1,1024]{1,0:T(1,128)S(1)} %bitcast.7, f32[64,128]{1,0:T(8,128)S(1)} %get-tuple-element.44.rest_0_, ...), custom_call_target="tpu_custom_call" | custom-call | flops 2147483648 | bytes 33554432 | tf_op jit(solution)/shard_map/scores/pallas_call | solution.py:315
  62.6 1.2 %collective-permute-start.7 = (f32[2,1024]{1,0:T(2,128)S(1)}, f32[2,1024]{1,0:T(2,128)S(1)}, u32[]{:S(2)}, u32[]{:S(2)}) collective-permute-start(f32[2,1024]{1,0:T(2,128)S(1)} %scores.1), channel_id=1, source_target_pairs={{0,1},{1,0},{2,3},{3,2},{4,5},{5,4},{6,7},{7,6},{8,9},{9,8},{10,11... | collective-permute-start | bytes 24584 | tf_op jit(solution)/shard_map/ppermute | solution.py:358
  63.8 0.8 %collective-permute-done.7 = f32[2,1024]{1,0:T(2,128)S(1)} collective-permute-done((f32[2,1024]{1,0:T(2,128)S(1)}, f32[2,1024]{1,0:T(2,128)S(1)}, u32[]{:S(2)}, u32[]{:S(2)}) %collective-permute-start.7) | collective-permute-done | bytes 8224 | tf_op jit(solution)/shard_map/ppermute | solution.py:358
  64.7 15.7 %all_to_all.11 = f32[16,2,1024]{2,1,0:T(2,128)S(1)} all-to-all(f32[16,2,1024]{2,1,0:T(2,128)S(1)} %broadcast_in_dim.18), channel_id=1, replica_groups={{0,2,4,6,8,10,12,14,16,18,20,22,24,26,28,30},{1,3,5,7,9,11,13,15,17,19,..., dimensions={0} | all-to-all | bytes 262144 | tf_op jit(solution)/shard_map/all_to_all | solution.py:425
  80.3 0.1 reduce_sum.9
  80.4 0.6 add.11
  (17 shorter events, 0.1 us)
Async XLA Ops:
  0.8 20.3 %collective-permute-start.2 = (f32[16,512]{1,0:T(8,128)S(1)}, f32[16,512]{1,0:T(8,128)S(1)}, u32[]{:S(2)}, u32[]{:S(2)}) collective-permute-start(f32[16,512]{1,0:T(8,128)S(1)} %add.9.pass_ref), channel_id=1, source_target_pairs={{0,6},{1,7},{2,0},{3,1},{4,2},{5,3},{6,4},{7,5},{8,14},{9,15},{10,... | collective-permute-start | bytes 98312 | tf_op jit(solution)/shard_map/ppermute | solution.py:358
  7.6 13.5 %collective-permute-start.1 = (f32[16,512]{1,0:T(8,128)S(1)}, f32[16,512]{1,0:T(8,128)S(1)}, u32[]{:S(2)}, u32[]{:S(2)}) collective-permute-start(f32[16,512]{1,0:T(8,128)S(1)} %add.9.pass_ref), channel_id=1, source_target_pairs={{0,4},{1,5},{2,6},{3,7},{4,0},{5,1},{6,2},{7,3},{8,12},{9,13},{10,... | collective-permute-start | bytes 98312 | tf_op jit(solution)/shard_map/ppermute | solution.py:358
  8.6 12.5 %collective-permute-start = (f32[16,512]{1,0:T(8,128)S(1)}, f32[16,512]{1,0:T(8,128)S(1)}, u32[]{:S(2)}, u32[]{:S(2)}) collective-permute-start(f32[16,512]{1,0:T(8,128)S(1)} %add.9.pass_ref), channel_id=1, source_target_pairs={{0,2},{1,3},{2,4},{3,5},{4,6},{5,7},{6,0},{7,1},{8,10},{9,11},{10,... | collective-permute-start | bytes 98312 | tf_op jit(solution)/shard_map/ppermute | solution.py:358
  10.9 14.1 %copy-start.1 = (f32[3,2048]{1,0:T(4,128)S(1)}, f32[3,2048]{1,0:T(4,128)}, u32[]{:S(2)}) copy-start(f32[3,2048]{1,0:T(4,128)} %uvw_ref.5) | copy-start | bytes 73732
  10.9 14.1 %copy-start.3 = (s32[1024]{0:T(1024)S(1)}, s32[1024]{0:T(1024)}, u32[]{:S(2)}) copy-start(s32[1024]{0:T(1024)} %param.11) | copy-start | bytes 12292
  10.9 14.1 %copy-start.4 = (f32[1024]{0:T(1024)S(1)}, f32[1024]{0:T(1024)}, u32[]{:S(2)}) copy-start(f32[1024]{0:T(1024)} %param.10) | copy-start | bytes 12292
  10.9 14.1 %copy-start.5 = (f32[2,1024]{1,0:T(2,128)S(1)}, f32[2,1024]{1,0:T(2,128)}, u32[]{:S(2)}) copy-start(f32[2,1024]{1,0:T(2,128)} %sky_ref.5) | copy-start | bytes 24580
  21.1 11.6 %collective-permute-start.5 = (f32[64,512]{1,0:T(8,128)S(1)}, f32[64,512]{1,0:T(8,128)S(1)}, u32[]{:S(2)}, u32[]{:S(2)}) collective-permute-start(f32[64,512]{1,0:T(8,128)S(1)} %constant_dynamic-update-slice_fusion.pass_ref), channel_id=1, source_target_pairs={{0,24},{1,25},{2,26},{3,27},{4,28},{5,29},{6,30},{7,31},{8,0},{9,1... | collective-permute-start | bytes 393224 | tf_op jit(solution)/shard_map/ppermute | solution.py:358
  24.0 8.7 %collective-permute-start.4 = (f32[64,512]{1,0:T(8,128)S(1)}, f32[64,512]{1,0:T(8,128)S(1)}, u32[]{:S(2)}, u32[]{:S(2)}) collective-permute-start(f32[64,512]{1,0:T(8,128)S(1)} %constant_dynamic-update-slice_fusion.pass_ref), channel_id=1, source_target_pairs={{0,16},{1,17},{2,18},{3,19},{4,20},{5,21},{6,22},{7,23},{8,24},{9,... | collective-permute-start | bytes 393224 | tf_op jit(solution)/shard_map/ppermute | solution.py:358
  24.3 8.4 %collective-permute-start.3 = (f32[64,512]{1,0:T(8,128)S(1)}, f32[64,512]{1,0:T(8,128)S(1)}, u32[]{:S(2)}, u32[]{:S(2)}) collective-permute-start(f32[64,512]{1,0:T(8,128)S(1)} %constant_dynamic-update-slice_fusion.pass_ref), channel_id=1, source_target_pairs={{0,8},{1,9},{2,10},{3,11},{4,12},{5,13},{6,14},{7,15},{8,16},{9,17... | collective-permute-start | bytes 393224 | tf_op jit(solution)/shard_map/ppermute | solution.py:358
  32.7 5.8 %collective-permute-start.6 = (f32[256,512]{1,0:T(8,128)S(1)}, f32[256,512]{1,0:T(8,128)S(1)}, u32[]{:S(2)}, u32[]{:S(2)}) collective-permute-start(f32[256,512]{1,0:T(8,128)S(1)} %constant_dynamic-update-slice_fusion.4.pass_ref.rest_0_), channel_id=1, source_target_pairs={{0,1},{1,0},{2,3},{3,2},{4,5},{5,4},{6,7},{7,6},{8,9},{9,8},{10,11... | collective-permute-start | bytes 1572872 | tf_op jit(solution)/shard_map/ppermute | solution.py:358
  35.0 3.6 %copy-start.2 = (s32[2,2048]{1,0:T(2,128)S(1)}, s32[2,2048]{1,0:T(2,128)}, u32[]{:S(2)}) copy-start(s32[2,2048]{1,0:T(2,128)} %rest_2_.1) | copy-start | bytes 49156
  38.6 18.1 %copy-start = (f32[2,4,2048]{2,1,0:T(4,128)S(1)}, f32[2,4,2048]{2,1,0:T(4,128)}, u32[]{:S(2)}) copy-start(f32[2,4,2048]{2,1,0:T(4,128)} %obs_ref.1) | copy-start | bytes 196612
  62.6 2.1 %collective-permute-start.7 = (f32[2,1024]{1,0:T(2,128)S(1)}, f32[2,1024]{1,0:T(2,128)S(1)}, u32[]{:S(2)}, u32[]{:S(2)}) collective-permute-start(f32[2,1024]{1,0:T(2,128)S(1)} %scores.1), channel_id=1, source_target_pairs={{0,1},{1,0},{2,3},{3,2},{4,5},{5,4},{6,7},{7,6},{8,9},{9,8},{10,11... | collective-permute-start | bytes 24584 | tf_op jit(solution)/shard_map/ppermute | solution.py:358

commit v7 on v6

--- a/solution.py
+++ b/solution.py
@@ -302,9 +302,20 @@
         return
     scores = sum([ref[...] for ref in earlier], scores)
     hot = lax.broadcasted_iota(jnp.int32, scores.shape, 0) == clus_ref[...]
-    curv = jnp.sum(sum(curv[...] for curv in curvs), axis=1, keepdims=True)
-    out_ref[0:1, :] = jnp.sum(jnp.where(hot, scores, 0.0), axis=0, keepdims=True)
-    out_ref[1:2, :] = jnp.sum(jnp.where(hot, curv, 0.0), axis=0, keepdims=True)
+    comps = scores.shape[1]
+    curv = sum(curv[...] for curv in curvs)
+    curv = jnp.concatenate([curv, jnp.zeros_like(curv)], axis=0)
+    out_ref[:, 0:comps] = jnp.sum(jnp.where(hot, scores, 0.0), axis=0, keepdims=True)
+    out_ref[:, comps : comps + 128] = jnp.sum(jnp.transpose(curv), axis=0, keepdims=True)
+
+
+def flux_kernel(parts_ref, flux_ref, clus_ref, out_ref):
+    total = jnp.sum(parts_ref[...], axis=0)
+    comps = flux_ref.shape[1]
+    curv = jnp.transpose(jnp.broadcast_to(total[:, comps:], (128, 128)))[0:C, 0:1]
+    hot = lax.broadcasted_iota(jnp.int32, (C, comps), 0) == clus_ref[...]
+    curv = jnp.sum(jnp.where(hot, curv, 0.0), axis=0, keepdims=True)
+    out_ref[...] = flux_ref[...] + total[:, 0:comps] / curv
 
 
 def make_scores(first, parts, observed, gain, clusters, curvs, earlier, tables):
@@ -316,7 +327,7 @@
         functools.partial(score_kernel, first, counts, len(curvs), len(earlier)),
         in_specs=[vmem] * (4 + len(curvs) + len(earlier) + len(tables)),
         out_specs=vmem,
-        out_shape=jax.ShapeDtypeStruct((2, comps), F32)
+        out_shape=jax.ShapeDtypeStruct((1, comps + 128), F32)
         if curvs
         else pltpu.VMEM((C, comps), F32),
         scratch_shapes=[pltpu.VMEM((2, C, WIDE), BF16)],
@@ -429,8 +440,10 @@
         0,
         axis_index_groups=plane_groups(),
         tiled=True,
-    ).sum(0)
-    return fluxes + sums[0] / sums[1]
+    )
+    return pl.pallas_call(
+        flux_kernel, out_shape=jax.ShapeDtypeStruct(flux_row.shape, F32), name="flux"
+    )(sums, flux_row, cluster_row)[0]
 
 
 def solution(mesh):

time: 81.3 us -> 81.4 us (level)
  Pallas kernels: 30.7 us -> 32.4 us
  blocking collectives: 29.8 us -> 28.8 us
    pallas_call x0 -> x1, Pallas kernels: none -> 1.7 us  [per_device(): pl.pallas_call(flux_kernel, out_shape=jax.ShapeDtypeStruct(flux_row.shape...]
    all_to_all x1, blocking collectives: 15.7 us -> 14.7 us  [per_device(): lax.all_to_all(jnp.broadcast_to(sums[None], (16,) + sums.shape), 'row', 0...]
where the time goes in v7:
time: 81.4 us; the launch traced here: 81.1 us
  Pallas kernels  32.4 us (40%)
  blocking collectives  28.8 us (35%)
  starting transfers between devices  17.4 us (21%)
  waiting for transfers between devices  1.31 us (2%)
    pallas_call x3, Pallas kernels, make_tables(): pl.pallas_call(functools.partial(table_kernel, first, count), in_specs=[p...  20.9 us
    ppermute x8, starting transfers between devices, permute(): return lax.ppermute(x, 'row', pairs)  17.4 us
    all_to_all x1, blocking collectives, per_device(): lax.all_to_all(jnp.broadcast_to(sums[None], (16,) + sums.shape), 'row', 0...  14.7 us
    all_to_all x1, blocking collectives, per_device(): sent.append(lax.all_to_all(model, 'comp', 0, 0, tiled=True))  14.2 us
    pallas_call x1, Pallas kernels, make_scores(): pl.pallas_call(functools.partial(score_kernel, first, counts, len(curvs),...  5.91 us
    pallas_call x1, Pallas kernels, make_model(): pl.pallas_call(functools.partial(model_kernel, first, counts, build), in_...  3.9 us
    pallas_call x1, Pallas kernels, per_device(): pl.pallas_call(flux_kernel, out_shape=jax.ShapeDtypeStruct(flux_row.shape...  1.7 us
  transfers between devices with their start and end apart: 8, of which 2 were waited for; matrix products, arithmetic and copies ran while one was open for 0% of the time, Pallas kernels for 26%

profile of v7, /device:TPU:1, one launch (start us, length us, event | category | flops | bytes accessed | tf_op | source)
XLA Modules:
  0.0 81.1 jit_solution(13032545118156133350)
XLA Ops:
  0.0 0.8 add.6.pass_ref
  0.8 6.8 %collective-permute-start.2 = (f32[16,512]{1,0:T(8,128)S(1)}, f32[16,512]{1,0:T(8,128)S(1)}, u32[]{:S(2)}, u32[]{:S(2)}) collective-permute-start(f32[16,512]{1,0:T(8,128)S(1)} %add.6.pass_ref), channel_id=1, source_target_pairs={{0,6},{1,7},{2,0},{3,1},{4,2},{5,3},{6,4},{7,5},{8,14},{9,15},{10,... | collective-permute-start | bytes 98312 | tf_op jit(solution)/shard_map/ppermute | solution.py:369
  7.6 1.0 %collective-permute-start.1 = (f32[16,512]{1,0:T(8,128)S(1)}, f32[16,512]{1,0:T(8,128)S(1)}, u32[]{:S(2)}, u32[]{:S(2)}) collective-permute-start(f32[16,512]{1,0:T(8,128)S(1)} %add.6.pass_ref), channel_id=1, source_target_pairs={{0,4},{1,5},{2,6},{3,7},{4,0},{5,1},{6,2},{7,3},{8,12},{9,13},{10,... | collective-permute-start | bytes 98312 | tf_op jit(solution)/shard_map/ppermute | solution.py:369
  8.6 2.3 %collective-permute-start = (f32[16,512]{1,0:T(8,128)S(1)}, f32[16,512]{1,0:T(8,128)S(1)}, u32[]{:S(2)}, u32[]{:S(2)}) collective-permute-start(f32[16,512]{1,0:T(8,128)S(1)} %add.6.pass_ref), channel_id=1, source_target_pairs={{0,2},{1,3},{2,4},{3,5},{4,6},{5,7},{6,0},{7,1},{8,10},{9,11},{10,... | collective-permute-start | bytes 98312 | tf_op jit(solution)/shard_map/ppermute | solution.py:369
  10.9 10.2 %tables.3 = (bf16[4,2048,256]{2,1,0:T(8,128)(2,1)S(1)}, bf16[4,2048,256]{2,1,0:T(8,128)(2,1)S(1)}, bf16[4,2048,256]{2,1,0:T(8,128)(2,1)S(1)}, bf16[4,2048,256]{2...) custom-call(s32[1]{0:T(128)} %bitcast.me_ref, f32[2,1024]{1,0:T(2,128)} %sky_ref.5, ...), custom_call_target="tpu_custom_call" | custom-call | flops 1073741824 | bytes 16777216 | tf_op jit(solution)/shard_map/tables/pallas_call | solution.py:149
  21.1 0.0 collective-permute-done
  21.1 0.0 collective-permute-done.1
  21.1 0.0 collective-permute-done.2
  21.1 2.8 %collective-permute-start.5 = (f32[64,512]{1,0:T(8,128)S(1)}, f32[64,512]{1,0:T(8,128)S(1)}, u32[]{:S(2)}, u32[]{:S(2)}) collective-permute-start(f32[64,512]{1,0:T(8,128)S(1)} %constant_dynamic-update-slice_fusion.pass_ref), channel_id=1, source_target_pairs={{0,24},{1,25},{2,26},{3,27},{4,28},{5,29},{6,30},{7,31},{8,0},{9,1... | collective-permute-start | bytes 393224 | tf_op jit(solution)/shard_map/ppermute | solution.py:369
  24.0 0.3 collective-permute-start.4
  24.3 0.7 collective-permute-start.3
  25.0 0.0 copy-done.1
  25.0 0.0 copy-done.2
  25.0 0.0 copy-done.4
  25.0 0.0 copy-done.5
  25.0 7.2 %tables.4 = (bf16[3,2048,256]{2,1,0:T(8,128)(2,1)S(1)}, bf16[3,2048,256]{2,1,0:T(8,128)(2,1)S(1)}, bf16[3,2048,256]{2,1,0:T(8,128)(2,1)S(1)}, bf16[3,2048,256]{2...) custom-call(s32[1]{0:T(128)} %bitcast.me_ref, f32[2,1024]{1,0:T(2,128)S(1)} %copy-done.5, ...), custom_call_target="tpu_custom_call" | custom-call | flops 805306368 | bytes 12582912 | tf_op jit(solution)/shard_map/tables/pallas_call | solution.py:149
  32.2 0.5 collective-permute-done.3
  32.7 0.0 collective-permute-done.4
  32.7 0.0 collective-permute-done.5
  32.7 2.2 %collective-permute-start.6 = (f32[256,512]{1,0:T(8,128)S(1)}, f32[256,512]{1,0:T(8,128)S(1)}, u32[]{:S(2)}, u32[]{:S(2)}) collective-permute-start(f32[256,512]{1,0:T(8,128)S(1)} %constant_dynamic-update-slice_fusion.4.pass_ref.rest_0_), channel_id=1, source_target_pairs={{0,1},{1,0},{2,3},{3,2},{4,5},{5,4},{6,7},{7,6},{8,9},{9,8},{10,11... | collective-permute-start | bytes 1572872 | tf_op jit(solution)/shard_map/ppermute | solution.py:369
  35.0 3.6 %tables.5 = (bf16[1,2048,256]{2,1,0:T(8,128)(2,1)S(1)}, bf16[1,2048,256]{2,1,0:T(8,128)(2,1)S(1)}, bf16[1,2048,256]{2,1,0:T(8,128)(2,1)S(1)}, bf16[1,2048,256]{2...) custom-call(s32[1]{0:T(128)} %bitcast.me_ref, f32[2,1024]{1,0:T(2,128)S(1)} %copy-done.5, ...), custom_call_target="tpu_custom_call" | custom-call | flops 268435456 | bytes 4194304 | tf_op jit(solution)/shard_map/tables/pallas_call | solution.py:149
  38.5 0.0 collective-permute-done.6.rest_1_
  38.6 0.0 copy-done.3
  38.6 0.0 copy-start
  38.6 3.9 %model.1 = (f32[8,64,2048]{2,1,0:T(8,128)S(1)}, f32[8,8,2048]{2,1,0:T(8,128)S(1)}, f32[64,128]{1,0:T(8,128)S(1)}, bf16[512,512]{1,0:T(8,128)(2,1)}) custom-call(s32[1]{0:T(128)} %bitcast.me_ref, f32[256,512]{1,0:T(8,128)S(1)} %constant_dynamic-update-slice_fusion.4.pass_ref.rest_0_, f32[256,512]{1,0:T(8,128)S(1)} %collective-permute-done.6.rest_1_, ...), custom_call_target="tpu_custom_call" | custom-call | flops 4294967296 | bytes 16777216 | tf_op jit(solution)/shard_map/model/pallas_call | solution.py:243
  42.5 14.2 %all_to_all.10.parts_ref = f32[8,8,2048]{2,1,0:T(8,128)S(1)} all-to-all(f32[8,8,2048]{2,1,0:T(8,128)S(1)} %get-tuple-element.42), channel_id=1, replica_groups=mesh['comp'=8,'row'=32] {'comp'}, dimensions={0} | all-to-all | bytes 1048576 | tf_op jit(solution)/shard_map/all_to_all | solution.py:420
  56.6 0.0 copy-done
  56.6 5.9 %scores.1 = f32[1,1152]{1,0:T(1,128)S(1)} custom-call(f32[8,8,2048]{2,1,0:T(8,128)S(1)} %all_to_all.10.parts_ref, f32[2,4,2048]{2,1,0:T(4,128)S(1)} %copy-done, f32[8,64,2048]{2,1,0:T(8,128)S(1)} %get-tuple-element.43.gain_ref, s32[1,1024]{1,0:T(1,128)S(1)} %bitcast.8, f32[64,128]{1,0:T(8,128)S(1)} %get-tuple-element.44.rest_0_, ...), custom_call_target="tpu_custom_call" | custom-call | flops 2147483648 | bytes 33554432 | tf_op jit(solution)/shard_map/scores/pallas_call | solution.py:326
  62.6 1.2 %collective-permute-start.7 = (f32[1,1152]{1,0:T(1,128)S(1)}, f32[1,1152]{1,0:T(1,128)S(1)}, u32[]{:S(2)}, u32[]{:S(2)}) collective-permute-start(f32[1,1152]{1,0:T(1,128)S(1)} %scores.1), channel_id=1, source_target_pairs={{0,1},{1,0},{2,3},{3,2},{4,5},{5,4},{6,7},{7,6},{8,9},{9,8},{10,11... | collective-permute-start | bytes 13832 | tf_op jit(solution)/shard_map/ppermute | solution.py:369
  63.8 0.8 %collective-permute-done.7 = f32[1,1152]{1,0:T(1,128)S(1)} collective-permute-done((f32[1,1152]{1,0:T(1,128)S(1)}, f32[1,1152]{1,0:T(1,128)S(1)}, u32[]{:S(2)}, u32[]{:S(2)}) %collective-permute-start.7) | collective-permute-done | bytes 4640 | tf_op jit(solution)/shard_map/ppermute | solution.py:369
  64.7 14.7 %all_to_all.11.parts_ref = f32[16,1,1152]{2,1,0:T(1,128)} all-to-all(f32[16,1,1152]{2,1,0:T(1,128)S(1)} %broadcast_in_dim.21), channel_id=1, replica_groups={{0,2,4,6,8,10,12,14,16,18,20,22,24,26,28,30},{1,3,5,7,9,11,13,15,17,19,..., dimensions={0} | all-to-all | bytes 147456 | tf_op jit(solution)/shard_map/all_to_all | solution.py:436
  79.4 1.7 %flux.1 = f32[1,1024]{1,0:T(1,128)} custom-call(f32[16,1,1152]{2,1,0:T(1,128)} %all_to_all.11.parts_ref, f32[1,1024]{1,0:T(1,128)} %bitcast.10, s32[1,1024]{1,0:T(1,128)} %bitcast.5), custom_call_target="tpu_custom_call" | custom-call | tf_op jit(solution)/shard_map/flux/pallas_call | solution.py:444
  (15 shorter events, 0.1 us)
Async XLA Ops:
  0.8 20.3 %collective-permute-start.2 = (f32[16,512]{1,0:T(8,128)S(1)}, f32[16,512]{1,0:T(8,128)S(1)}, u32[]{:S(2)}, u32[]{:S(2)}) collective-permute-start(f32[16,512]{1,0:T(8,128)S(1)} %add.6.pass_ref), channel_id=1, source_target_pairs={{0,6},{1,7},{2,0},{3,1},{4,2},{5,3},{6,4},{7,5},{8,14},{9,15},{10,... | collective-permute-start | bytes 98312 | tf_op jit(solution)/shard_map/ppermute | solution.py:369
  7.6 13.5 %collective-permute-start.1 = (f32[16,512]{1,0:T(8,128)S(1)}, f32[16,512]{1,0:T(8,128)S(1)}, u32[]{:S(2)}, u32[]{:S(2)}) collective-permute-start(f32[16,512]{1,0:T(8,128)S(1)} %add.6.pass_ref), channel_id=1, source_target_pairs={{0,4},{1,5},{2,6},{3,7},{4,0},{5,1},{6,2},{7,3},{8,12},{9,13},{10,... | collective-permute-start | bytes 98312 | tf_op jit(solution)/shard_map/ppermute | solution.py:369
  8.6 12.5 %collective-permute-start = (f32[16,512]{1,0:T(8,128)S(1)}, f32[16,512]{1,0:T(8,128)S(1)}, u32[]{:S(2)}, u32[]{:S(2)}) collective-permute-start(f32[16,512]{1,0:T(8,128)S(1)} %add.6.pass_ref), channel_id=1, source_target_pairs={{0,2},{1,3},{2,4},{3,5},{4,6},{5,7},{6,0},{7,1},{8,10},{9,11},{10,... | collective-permute-start | bytes 98312 | tf_op jit(solution)/shard_map/ppermute | solution.py:369
  10.9 14.1 %copy-start.1 = (s32[1024]{0:T(1024)S(1)}, s32[1024]{0:T(1024)}, u32[]{:S(2)}) copy-start(s32[1024]{0:T(1024)} %param.11) | copy-start | bytes 12292
  10.9 14.1 %copy-start.2 = (f32[3,2048]{1,0:T(4,128)S(1)}, f32[3,2048]{1,0:T(4,128)}, u32[]{:S(2)}) copy-start(f32[3,2048]{1,0:T(4,128)} %uvw_ref.5) | copy-start | bytes 73732
  10.9 14.1 %copy-start.4 = (f32[1024]{0:T(1024)S(1)}, f32[1024]{0:T(1024)}, u32[]{:S(2)}) copy-start(f32[1024]{0:T(1024)} %param.10) | copy-start | bytes 12292
  10.9 14.1 %copy-start.5 = (f32[2,1024]{1,0:T(2,128)S(1)}, f32[2,1024]{1,0:T(2,128)}, u32[]{:S(2)}) copy-start(f32[2,1024]{1,0:T(2,128)} %sky_ref.5) | copy-start | bytes 24580
  21.1 11.6 %collective-permute-start.5 = (f32[64,512]{1,0:T(8,128)S(1)}, f32[64,512]{1,0:T(8,128)S(1)}, u32[]{:S(2)}, u32[]{:S(2)}) collective-permute-start(f32[64,512]{1,0:T(8,128)S(1)} %constant_dynamic-update-slice_fusion.pass_ref), channel_id=1, source_target_pairs={{0,24},{1,25},{2,26},{3,27},{4,28},{5,29},{6,30},{7,31},{8,0},{9,1... | collective-permute-start | bytes 393224 | tf_op jit(solution)/shard_map/ppermute | solution.py:369
  24.0 8.7 %collective-permute-start.4 = (f32[64,512]{1,0:T(8,128)S(1)}, f32[64,512]{1,0:T(8,128)S(1)}, u32[]{:S(2)}, u32[]{:S(2)}) collective-permute-start(f32[64,512]{1,0:T(8,128)S(1)} %constant_dynamic-update-slice_fusion.pass_ref), channel_id=1, source_target_pairs={{0,16},{1,17},{2,18},{3,19},{4,20},{5,21},{6,22},{7,23},{8,24},{9,... | collective-permute-start | bytes 393224 | tf_op jit(solution)/shard_map/ppermute | solution.py:369
  24.3 8.4 %collective-permute-start.3 = (f32[64,512]{1,0:T(8,128)S(1)}, f32[64,512]{1,0:T(8,128)S(1)}, u32[]{:S(2)}, u32[]{:S(2)}) collective-permute-start(f32[64,512]{1,0:T(8,128)S(1)} %constant_dynamic-update-slice_fusion.pass_ref), channel_id=1, source_target_pairs={{0,8},{1,9},{2,10},{3,11},{4,12},{5,13},{6,14},{7,15},{8,16},{9,17... | collective-permute-start | bytes 393224 | tf_op jit(solution)/shard_map/ppermute | solution.py:369
  32.7 5.8 %collective-permute-start.6 = (f32[256,512]{1,0:T(8,128)S(1)}, f32[256,512]{1,0:T(8,128)S(1)}, u32[]{:S(2)}, u32[]{:S(2)}) collective-permute-start(f32[256,512]{1,0:T(8,128)S(1)} %constant_dynamic-update-slice_fusion.4.pass_ref.rest_0_), channel_id=1, source_target_pairs={{0,1},{1,0},{2,3},{3,2},{4,5},{5,4},{6,7},{7,6},{8,9},{9,8},{10,11... | collective-permute-start | bytes 1572872 | tf_op jit(solution)/shard_map/ppermute | solution.py:369
  35.0 3.6 %copy-start.3 = (s32[2,2048]{1,0:T(2,128)S(1)}, s32[2,2048]{1,0:T(2,128)}, u32[]{:S(2)}) copy-start(s32[2,2048]{1,0:T(2,128)} %rest_2_.1) | copy-start | bytes 49156
  38.6 18.1 %copy-start = (f32[2,4,2048]{2,1,0:T(4,128)S(1)}, f32[2,4,2048]{2,1,0:T(4,128)}, u32[]{:S(2)}) copy-start(f32[2,4,2048]{2,1,0:T(4,128)} %obs_ref.1) | copy-start | bytes 196612
  62.6 2.1 %collective-permute-start.7 = (f32[1,1152]{1,0:T(1,128)S(1)}, f32[1,1152]{1,0:T(1,128)S(1)}, u32[]{:S(2)}, u32[]{:S(2)}) collective-permute-start(f32[1,1152]{1,0:T(1,128)S(1)} %scores.1), channel_id=1, source_target_pairs={{0,1},{1,0},{2,3},{3,2},{4,5},{5,4},{6,7},{7,6},{8,9},{9,8},{10,11... | collective-permute-start | bytes 13832 | tf_op jit(solution)/shard_map/ppermute | solution.py:369

commit v8 on v7

--- a/solution.py
+++ b/solution.py
@@ -15,8 +15,8 @@
 WIDE = 2 * F * BLOCK
 CHUNK = 256
 TILE = 16
-GROUPS = (4, 3, 1)
-HALVES = ((0, 1, 2),)
+GROUPS = (4, 4)
+HALVES = ((0, 1),)
 SCOPED = 10 << 20
 F32 = jnp.float32
 BF16 = jnp.bfloat16

time: 81.4 us -> 81.1 us (level)
  Pallas kernels: 32.4 us -> 30.6 us
  starting transfers between devices: 17.4 us -> 18.5 us
  waiting for transfers between devices: 1.31 us -> 2.38 us
    pallas_call x3 -> x2, Pallas kernels: 20.9 us -> 19.5 us  [make_tables(): pl.pallas_call(functools.partial(table_kernel, first, count), in_specs=[p...]
    ppermute x8, starting transfers between devices: 17.4 us -> 18.5 us  [permute(): return lax.ppermute(x, 'row', pairs)]
    ppermute x8, waiting for transfers between devices: 1.31 us -> 2.38 us  [permute(): return lax.ppermute(x, 'row', pairs)]
  transfers between devices with their start and end apart: 8 -> 8, of which waited for: 2 -> 2; matrix products, arithmetic and copies ran while one was open for 0% -> 0% of each run, Pallas kernels for 26% -> 24%
where the time goes in v8:
time: 81.1 us; the launch traced here: 80.7 us
  Pallas kernels  30.6 us (38%)
  blocking collectives  28.2 us (35%)
  starting transfers between devices  18.5 us (23%)
  waiting for transfers between devices  2.38 us (3%)
    pallas_call x2, Pallas kernels, make_tables(): pl.pallas_call(functools.partial(table_kernel, first, count), in_specs=[p...  19.5 us
    ppermute x8, starting transfers between devices, permute(): return lax.ppermute(x, 'row', pairs)  18.5 us
    all_to_all x1, blocking collectives, per_device(): lax.all_to_all(jnp.broadcast_to(sums[None], (16,) + sums.shape), 'row', 0...  14.7 us
    all_to_all x1, blocking collectives, per_device(): sent.append(lax.all_to_all(model, 'comp', 0, 0, tiled=True))  13.5 us
    pallas_call x1, Pallas kernels, make_scores(): pl.pallas_call(functools.partial(score_kernel, first, counts, len(curvs),...  5.9 us
    pallas_call x1, Pallas kernels, make_model(): pl.pallas_call(functools.partial(model_kernel, first, counts, build), in_...  3.5 us
    ppermute x8, waiting for transfers between devices, permute(): return lax.ppermute(x, 'row', pairs)  2.38 us
    pallas_call x1, Pallas kernels, per_device(): pl.pallas_call(flux_kernel, out_shape=jax.ShapeDtypeStruct(flux_row.shape...  1.7 us
  transfers between devices with their start and end apart: 8, of which 2 were waited for; matrix products, arithmetic and copies ran while one was open for 0% of the time, Pallas kernels for 24%

profile of v8, /device:TPU:1, one launch (start us, length us, event | category | flops | bytes accessed | tf_op | source)
XLA Modules:
  0.0 80.7 jit_solution(5106210713863855880)
XLA Ops:
  0.0 0.8 add.6.pass_ref
  0.8 6.8 %collective-permute-start.2 = (f32[16,512]{1,0:T(8,128)S(1)}, f32[16,512]{1,0:T(8,128)S(1)}, u32[]{:S(2)}, u32[]{:S(2)}) collective-permute-start(f32[16,512]{1,0:T(8,128)S(1)} %add.6.pass_ref), channel_id=1, source_target_pairs={{0,6},{1,7},{2,0},{3,1},{4,2},{5,3},{6,4},{7,5},{8,14},{9,15},{10,... | collective-permute-start | bytes 98312 | tf_op jit(solution)/shard_map/ppermute | solution.py:369
  7.6 1.0 %collective-permute-start.1 = (f32[16,512]{1,0:T(8,128)S(1)}, f32[16,512]{1,0:T(8,128)S(1)}, u32[]{:S(2)}, u32[]{:S(2)}) collective-permute-start(f32[16,512]{1,0:T(8,128)S(1)} %add.6.pass_ref), channel_id=1, source_target_pairs={{0,4},{1,5},{2,6},{3,7},{4,0},{5,1},{6,2},{7,3},{8,12},{9,13},{10,... | collective-permute-start | bytes 98312 | tf_op jit(solution)/shard_map/ppermute | solution.py:369
  8.6 2.3 %collective-permute-start = (f32[16,512]{1,0:T(8,128)S(1)}, f32[16,512]{1,0:T(8,128)S(1)}, u32[]{:S(2)}, u32[]{:S(2)}) collective-permute-start(f32[16,512]{1,0:T(8,128)S(1)} %add.6.pass_ref), channel_id=1, source_target_pairs={{0,2},{1,3},{2,4},{3,5},{4,6},{5,7},{6,0},{7,1},{8,10},{9,11},{10,... | collective-permute-start | bytes 98312 | tf_op jit(solution)/shard_map/ppermute | solution.py:369
  10.9 0.0 copy-start.2
  10.9 10.2 %tables.2 = (bf16[4,2048,256]{2,1,0:T(8,128)(2,1)S(1)}, bf16[4,2048,256]{2,1,0:T(8,128)(2,1)S(1)}, bf16[4,2048,256]{2,1,0:T(8,128)(2,1)S(1)}, bf16[4,2048,256]{2...) custom-call(s32[1]{0:T(128)} %bitcast.me_ref, f32[2,1024]{1,0:T(2,128)} %sky_ref.3, ...), custom_call_target="tpu_custom_call" | custom-call | flops 1073741824 | bytes 16777216 | tf_op jit(solution)/shard_map/tables/pallas_call | solution.py:149
  21.1 0.0 collective-permute-done
  21.1 0.0 collective-permute-done.1
  21.1 0.0 collective-permute-done.2
  21.1 2.8 %collective-permute-start.5 = (f32[64,512]{1,0:T(8,128)S(1)}, f32[64,512]{1,0:T(8,128)S(1)}, u32[]{:S(2)}, u32[]{:S(2)}) collective-permute-start(f32[64,512]{1,0:T(8,128)S(1)} %constant_dynamic-update-slice_fusion.pass_ref), channel_id=1, source_target_pairs={{0,24},{1,25},{2,26},{3,27},{4,28},{5,29},{6,30},{7,31},{8,0},{9,1... | collective-permute-start | bytes 393224 | tf_op jit(solution)/shard_map/ppermute | solution.py:369
  24.0 0.3 collective-permute-start.4
  24.3 0.7 collective-permute-start.3
  25.0 0.0 copy-done.2
  25.0 0.0 copy-done.3
  25.0 0.0 copy-done.4
  25.0 0.0 copy-done.5
  25.0 0.0 copy-start.1
  25.0 9.3 %tables.3 = (bf16[4,2048,256]{2,1,0:T(8,128)(2,1)S(1)}, bf16[4,2048,256]{2,1,0:T(8,128)(2,1)S(1)}, bf16[4,2048,256]{2,1,0:T(8,128)(2,1)S(1)}, bf16[4,2048,256]{2...) custom-call(s32[1]{0:T(128)} %bitcast.me_ref, f32[2,1024]{1,0:T(2,128)S(1)} %copy-done.5, ...), custom_call_target="tpu_custom_call" | custom-call | flops 1073741824 | bytes 16777216 | tf_op jit(solution)/shard_map/tables/pallas_call | solution.py:149
  34.4 0.0 collective-permute-done.3
  34.4 0.0 collective-permute-done.4
  34.4 0.0 collective-permute-done.5
  34.5 2.7 %collective-permute-start.6 = (f32[256,512]{1,0:T(8,128)S(1)}, f32[256,512]{1,0:T(8,128)S(1)}, u32[]{:S(2)}, u32[]{:S(2)}) collective-permute-start(f32[256,512]{1,0:T(8,128)S(1)} %constant_dynamic-update-slice_fusion.4.rest_0_), channel_id=1, source_target_pairs={{0,1},{1,0},{2,3},{3,2},{4,5},{5,4},{6,7},{7,6},{8,9},{9,8},{10,11... | collective-permute-start | bytes 1572872 | tf_op jit(solution)/shard_map/ppermute | solution.py:369
  37.1 1.5 %collective-permute-done.6.rest_1_ = f32[256,512]{1,0:T(8,128)S(1)} collective-permute-done((f32[256,512]{1,0:T(8,128)S(1)}, f32[256,512]{1,0:T(8,128)S(1)}, u32[]{:S(2)}, u32[]{:S(2)}) %collective-permute-start.6) | collective-permute-done | bytes 524320 | tf_op jit(solution)/shard_map/ppermute | solution.py:369
  38.7 0.0 copy-done.1
  38.7 3.5 %model.1 = (f32[8,64,2048]{2,1,0:T(8,128)S(1)}, f32[8,8,2048]{2,1,0:T(8,128)S(1)}, f32[64,128]{1,0:T(8,128)S(1)}, bf16[512,512]{1,0:T(8,128)(2,1)}) custom-call(s32[1]{0:T(128)} %bitcast.me_ref, f32[256,512]{1,0:T(8,128)S(1)} %constant_dynamic-update-slice_fusion.4.rest_0_, f32[256,512]{1,0:T(8,128)S(1)} %collective-permute-done.6.rest_1_, ...), custom_call_target="tpu_custom_call" | custom-call | flops 4294967296 | bytes 16777216 | tf_op jit(solution)/shard_map/model/pallas_call | solution.py:243
  42.2 13.5 %all_to_all.10.parts_ref = f32[8,8,2048]{2,1,0:T(8,128)S(1)} all-to-all(f32[8,8,2048]{2,1,0:T(8,128)S(1)} %get-tuple-element.32), channel_id=1, replica_groups=mesh['comp'=8,'row'=32] {'comp'}, dimensions={0} | all-to-all | bytes 1048576 | tf_op jit(solution)/shard_map/all_to_all | solution.py:420
  55.6 0.0 copy-done
  55.6 5.9 %scores.1 = f32[1,1152]{1,0:T(1,128)S(1)} custom-call(f32[8,8,2048]{2,1,0:T(8,128)S(1)} %all_to_all.10.parts_ref, f32[2,4,2048]{2,1,0:T(4,128)S(1)} %copy-done, f32[8,64,2048]{2,1,0:T(8,128)S(1)} %get-tuple-element.33.gain_ref, s32[1,1024]{1,0:T(1,128)S(1)} %bitcast.7, f32[64,128]{1,0:T(8,128)S(1)} %get-tuple-element.34.rest_0_, ...), custom_call_target="tpu_custom_call" | custom-call | flops 2147483648 | bytes 33554432 | tf_op jit(solution)/shard_map/scores/pallas_call | solution.py:326
  61.6 1.9 %collective-permute-start.7 = (f32[1,1152]{1,0:T(1,128)S(1)}, f32[1,1152]{1,0:T(1,128)S(1)}, u32[]{:S(2)}, u32[]{:S(2)}) collective-permute-start(f32[1,1152]{1,0:T(1,128)S(1)} %scores.1), channel_id=1, source_target_pairs={{0,1},{1,0},{2,3},{3,2},{4,5},{5,4},{6,7},{7,6},{8,9},{9,8},{10,11... | collective-permute-start | bytes 13832 | tf_op jit(solution)/shard_map/ppermute | solution.py:369
  63.5 0.8 %collective-permute-done.7 = f32[1,1152]{1,0:T(1,128)S(1)} collective-permute-done((f32[1,1152]{1,0:T(1,128)S(1)}, f32[1,1152]{1,0:T(1,128)S(1)}, u32[]{:S(2)}, u32[]{:S(2)}) %collective-permute-start.7) | collective-permute-done | bytes 4640 | tf_op jit(solution)/shard_map/ppermute | solution.py:369
  64.4 14.7 %all_to_all.11.parts_ref = f32[16,1,1152]{2,1,0:T(1,128)} all-to-all(f32[16,1,1152]{2,1,0:T(1,128)S(1)} %broadcast_in_dim.21), channel_id=1, replica_groups={{0,2,4,6,8,10,12,14,16,18,20,22,24,26,28,30},{1,3,5,7,9,11,13,15,17,19,..., dimensions={0} | all-to-all | bytes 147456 | tf_op jit(solution)/shard_map/all_to_all | solution.py:436
  79.0 1.7 %flux.1 = f32[1,1024]{1,0:T(1,128)} custom-call(f32[16,1,1152]{2,1,0:T(1,128)} %all_to_all.11.parts_ref, f32[1,1024]{1,0:T(1,128)} %bitcast.9, s32[1,1024]{1,0:T(1,128)} %bitcast.5), custom_call_target="tpu_custom_call" | custom-call | tf_op jit(solution)/shard_map/flux/pallas_call | solution.py:444
  (14 shorter events, 0.1 us)
Async XLA Ops:
  0.8 20.3 %collective-permute-start.2 = (f32[16,512]{1,0:T(8,128)S(1)}, f32[16,512]{1,0:T(8,128)S(1)}, u32[]{:S(2)}, u32[]{:S(2)}) collective-permute-start(f32[16,512]{1,0:T(8,128)S(1)} %add.6.pass_ref), channel_id=1, source_target_pairs={{0,6},{1,7},{2,0},{3,1},{4,2},{5,3},{6,4},{7,5},{8,14},{9,15},{10,... | collective-permute-start | bytes 98312 | tf_op jit(solution)/shard_map/ppermute | solution.py:369
  7.6 13.5 %collective-permute-start.1 = (f32[16,512]{1,0:T(8,128)S(1)}, f32[16,512]{1,0:T(8,128)S(1)}, u32[]{:S(2)}, u32[]{:S(2)}) collective-permute-start(f32[16,512]{1,0:T(8,128)S(1)} %add.6.pass_ref), channel_id=1, source_target_pairs={{0,4},{1,5},{2,6},{3,7},{4,0},{5,1},{6,2},{7,3},{8,12},{9,13},{10,... | collective-permute-start | bytes 98312 | tf_op jit(solution)/shard_map/ppermute | solution.py:369
  8.6 12.5 %collective-permute-start = (f32[16,512]{1,0:T(8,128)S(1)}, f32[16,512]{1,0:T(8,128)S(1)}, u32[]{:S(2)}, u32[]{:S(2)}) collective-permute-start(f32[16,512]{1,0:T(8,128)S(1)} %add.6.pass_ref), channel_id=1, source_target_pairs={{0,2},{1,3},{2,4},{3,5},{4,6},{5,7},{6,0},{7,1},{8,10},{9,11},{10,... | collective-permute-start | bytes 98312 | tf_op jit(solution)/shard_map/ppermute | solution.py:369
  10.9 14.1 %copy-start.2 = (s32[1024]{0:T(1024)S(1)}, s32[1024]{0:T(1024)}, u32[]{:S(2)}) copy-start(s32[1024]{0:T(1024)} %param.11) | copy-start | bytes 12292
  10.9 14.1 %copy-start.3 = (f32[1024]{0:T(1024)S(1)}, f32[1024]{0:T(1024)}, u32[]{:S(2)}) copy-start(f32[1024]{0:T(1024)} %param.10) | copy-start | bytes 12292
  10.9 14.1 %copy-start.4 = (f32[3,2048]{1,0:T(4,128)S(1)}, f32[3,2048]{1,0:T(4,128)}, u32[]{:S(2)}) copy-start(f32[3,2048]{1,0:T(4,128)} %uvw_ref.3) | copy-start | bytes 73732
  10.9 14.1 %copy-start.5 = (f32[2,1024]{1,0:T(2,128)S(1)}, f32[2,1024]{1,0:T(2,128)}, u32[]{:S(2)}) copy-start(f32[2,1024]{1,0:T(2,128)} %sky_ref.3) | copy-start | bytes 24580
  21.1 13.3 %collective-permute-start.5 = (f32[64,512]{1,0:T(8,128)S(1)}, f32[64,512]{1,0:T(8,128)S(1)}, u32[]{:S(2)}, u32[]{:S(2)}) collective-permute-start(f32[64,512]{1,0:T(8,128)S(1)} %constant_dynamic-update-slice_fusion.pass_ref), channel_id=1, source_target_pairs={{0,24},{1,25},{2,26},{3,27},{4,28},{5,29},{6,30},{7,31},{8,0},{9,1... | collective-permute-start | bytes 393224 | tf_op jit(solution)/shard_map/ppermute | solution.py:369
  24.0 10.4 %collective-permute-start.4 = (f32[64,512]{1,0:T(8,128)S(1)}, f32[64,512]{1,0:T(8,128)S(1)}, u32[]{:S(2)}, u32[]{:S(2)}) collective-permute-start(f32[64,512]{1,0:T(8,128)S(1)} %constant_dynamic-update-slice_fusion.pass_ref), channel_id=1, source_target_pairs={{0,16},{1,17},{2,18},{3,19},{4,20},{5,21},{6,22},{7,23},{8,24},{9,... | collective-permute-start | bytes 393224 | tf_op jit(solution)/shard_map/ppermute | solution.py:369
  24.3 10.1 %collective-permute-start.3 = (f32[64,512]{1,0:T(8,128)S(1)}, f32[64,512]{1,0:T(8,128)S(1)}, u32[]{:S(2)}, u32[]{:S(2)}) collective-permute-start(f32[64,512]{1,0:T(8,128)S(1)} %constant_dynamic-update-slice_fusion.pass_ref), channel_id=1, source_target_pairs={{0,8},{1,9},{2,10},{3,11},{4,12},{5,13},{6,14},{7,15},{8,16},{9,17... | collective-permute-start | bytes 393224 | tf_op jit(solution)/shard_map/ppermute | solution.py:369
  25.0 13.6 %copy-start.1 = (s32[2,2048]{1,0:T(2,128)S(1)}, s32[2,2048]{1,0:T(2,128)}, u32[]{:S(2)}) copy-start(s32[2,2048]{1,0:T(2,128)} %rest_2_.1) | copy-start | bytes 49156
  34.5 4.2 %collective-permute-start.6 = (f32[256,512]{1,0:T(8,128)S(1)}, f32[256,512]{1,0:T(8,128)S(1)}, u32[]{:S(2)}, u32[]{:S(2)}) collective-permute-start(f32[256,512]{1,0:T(8,128)S(1)} %constant_dynamic-update-slice_fusion.4.rest_0_), channel_id=1, source_target_pairs={{0,1},{1,0},{2,3},{3,2},{4,5},{5,4},{6,7},{7,6},{8,9},{9,8},{10,11... | collective-permute-start | bytes 1572872 | tf_op jit(solution)/shard_map/ppermute | solution.py:369
  38.7 17.0 %copy-start = (f32[2,4,2048]{2,1,0:T(4,128)S(1)}, f32[2,4,2048]{2,1,0:T(4,128)}, u32[]{:S(2)}) copy-start(f32[2,4,2048]{2,1,0:T(4,128)} %obs_ref.1) | copy-start | bytes 196612
  61.6 2.7 %collective-permute-start.7 = (f32[1,1152]{1,0:T(1,128)S(1)}, f32[1,1152]{1,0:T(1,128)S(1)}, u32[]{:S(2)}, u32[]{:S(2)}) collective-permute-start(f32[1,1152]{1,0:T(1,128)S(1)} %scores.1), channel_id=1, source_target_pairs={{0,1},{1,0},{2,3},{3,2},{4,5},{5,4},{6,7},{7,6},{8,9},{9,8},{10,11... | collective-permute-start | bytes 13832 | tf_op jit(solution)/shard_map/ppermute | solution.py:369
